TPU v7x, 512 devices: a whole 4x8x8 slice. The times are simulated.
512 devices in a mesh: inter: 16 (over x, y_lo, core), intra: 32 (over y_hi, z).
Axes of the slice: x: 4, y: 8 (y_hi: 4, y_lo: 2; y = y_hi * 2 + y_lo), z: 8, core: 2. Of those that a mesh axis runs over, the one named last changes fastest.
Arguments:
- acts: bfloat16 [65536, 256], P(('inter', 'intra')), may hold values from -4 to 4, as said below
- cotangent: bfloat16 [65536, 14336], P(('inter', 'intra')), may hold values from -2 to 2, as said below
- first_exp: int32 [256, 112], replicated, may hold values from 0 to 3
- second_exp: int32 [256, 112], P('intra'), may hold values from 4 to 6
Outputs:
- grad_shard: float32 [256, 14336], P('intra', 'inter')
Inputs may be any that keep to these rules, and one draw needn't show every extreme that they name: `acts`: entries are multiples of 1/32. `cotangent`: entries are multiples of 1/64.
All inputs are finite; a program needn't handle non-finite values.
Results may differ from a plain program's by a relative error of at most 0.0003.
Values may be sent and summed in bfloat16 or wider, within the bound.
No kernel may reach another device: no remote copies, remote signals or barrier semaphores. Data moves between devices by JAX's collectives and lax.ppermute only.
A program may use at most 64 MiB of HBM per device.

v0:
```python
import jax
import jax.numpy as jnp
from jax import lax
from jax.sharding import PartitionSpec as P

BLK = 128
SLABS = 8


def power_two(expo):
    total = jnp.zeros(expo.shape, jnp.float32)
    for power in range(-8, 9):
        total = total + jnp.where(expo == power, jnp.float32(2.0**power), jnp.float32(0.0))
    return total


def round_even(values):
    lower = jnp.floor(values)
    part = values - lower
    parity = lower - 2.0 * jnp.floor(lower * 0.5)
    return jnp.where(part > 0.5, lower + 1.0, jnp.where(part < 0.5, lower, lower + parity))


def apply_scale(values, scale):
    row_count, col_count = values.shape
    shaped = values.reshape(row_count, col_count // BLK, BLK) * scale[:, :, None]
    return shaped.reshape(row_count, col_count)


def quantize(values, inverse):
    return round_even(jnp.clip(apply_scale(values, inverse), -127.0, 127.0))


def body(acts, cotangent, first_exp, second_exp):
    members = lax.axis_size("intra")
    groups = lax.axis_size("inter")
    member_index = lax.axis_index("intra")
    group_index = lax.axis_index("inter")
    row_count = acts.shape[1]
    col_count = cotangent.shape[1]
    part_rows = row_count // members
    slab_cols = col_count // SLABS
    slab_blocks = slab_cols // BLK
    inverse_one = power_two(-first_exp)
    my_scale_one = lax.dynamic_slice_in_dim(
        power_two(first_exp), member_index * part_rows, part_rows, 0
    )
    inverse_two = power_two(-second_exp)
    scale_two = power_two(second_exp)

    def make_codes(slab_index):
        columns = cotangent[:, slab_index * slab_cols : (slab_index + 1) * slab_cols]
        local = lax.dot_general(
            acts, columns, (((0,), (0,)), ((), ())), preferred_element_type=jnp.float32
        )
        block_inverse = inverse_one[:, slab_index * slab_blocks : (slab_index + 1) * slab_blocks]
        return quantize(local, block_inverse).astype(jnp.bfloat16)

    codes = jnp.concatenate([make_codes(slab_index) for slab_index in range(SLABS)], axis=1)
    arrived = lax.all_to_all(codes, "intra", split_axis=0, concat_axis=0, tiled=True)
    width_here = arrived.shape[1]
    code_sum = jnp.sum(arrived.reshape(members, part_rows, width_here), axis=0, dtype=jnp.float32)
    summed = apply_scale(code_sum, my_scale_one)
    second = quantize(summed, inverse_two).astype(jnp.bfloat16)
    owned = col_count // groups
    owned_blocks = owned // BLK
    received = lax.all_to_all(second, "inter", split_axis=1, concat_axis=0, tiled=True)
    total = jnp.sum(received.reshape(groups, part_rows, owned), axis=0, dtype=jnp.float32)
    my_scale_two = lax.dynamic_slice_in_dim(scale_two, group_index * owned_blocks, owned_blocks, 1)
    return apply_scale(total, my_scale_two) * (1.0 / (members * groups))


def solution(mesh):
    return jax.shard_map(
        body,
        mesh=mesh,
        in_specs=(P(("inter", "intra"), None), P(("inter", "intra"), None), P(), P("intra", None)),
        out_specs=P("intra", "inter"),
        check_vma=False,
    )
```

profile of v0, /device:TPU:6, one launch (start us, length us, event | category | flops | bytes accessed | tf_op | source)
XLA Modules:
  0.0 289.8 jit_solution(1336563593832813474)
XLA Ops:
  0.0 0.0 copy-start
  0.0 1.2 select_add_fusion.1
  1.3 0.1 mul.194
  1.4 1.7 copy.35
  3.1 0.1 mul.199
  3.3 1.7 copy.36
  5.0 0.1 mul.204
  5.2 1.7 copy.37
  6.9 0.1 mul.209
  7.0 1.7 copy.38
  8.7 0.1 mul.214
  8.9 1.7 copy.39
  10.6 0.1 mul.219
  10.7 1.7 copy.40
  12.4 0.1 mul.224
  12.6 1.7 copy.41
  14.3 0.1 mul.229
  14.4 1.8 copy.42
  16.2 0.0 copy-done
  16.2 3.8 %fusion.55 = bf16[32,8,14336]{2,1,0:T(8,128)(2,1)} fusion(f32[256,1792]{1,0:T(8,128)} %copy.35, bf16[128,256]{1,0:T(8,128)(2,1)S(1)} %copy-done, bf16[128,14336]{1,0:T(8,128)(2,1)} %param.5), kind=kOutput, calls=%fused_computation.96 | convolution fusion | flops 124321792 | bytes 3276800 | tf_op jit(solution)/shard_map/dot_general | solution.py:53
  20.0 0.0 copy-done.1
  20.0 0.0 copy-done.10
  20.0 2.1 fusion.53
  22.1 0.0 copy-done.2
  22.1 2.0 fusion.51
  24.1 2.1 fusion.49
  26.2 2.1 fusion.47
  28.2 2.1 fusion.45
  30.3 2.0 fusion.43
  32.4 2.1 fusion.41
  34.5 16.2 %all-to-all-start = ((bf16[32,8,14336]{2,1,0:T(8,128)(2,1)}), bf16[32,8,14336]{2,1,0:T(8,128)(2,1)}, u32[]{:S(2)}, u32[]{:S(2)}) async-start(bf16[32,8,14336]{2,1,0:T(8,128)(2,1)} %fusion.41), calls=%async_computation | async-start | bytes 14680064 | tf_op jit(solution)/shard_map/all_to_all | solution.py:60
  50.7 0.0 copy-start.9
  50.7 0.1 fusion.74
  50.9 0.1 copy.43
  50.9 0.2 mul.235
  51.1 0.1 mul.236
  51.2 0.1 copy-done.9
  51.4 0.2 mul.238
  51.6 0.1 mul.239
  51.7 218.9 %all-to-all-done = bf16[32,8,14336]{2,1,0:T(8,128)(2,1)} async-done(((bf16[32,8,14336]{2,1,0:T(8,128)(2,1)}), bf16[32,8,14336]{2,1,0:T(8,128)(2,1)}, u32[]{:S(2)}, u32[]{:S(2)}) %all-to-all-start) | async-done | bytes 7340064 | tf_op jit(solution)/shard_map/all_to_all | solution.py:60
  270.6 4.2 %convert_reduce_fusion = f32[8,14336]{1,0:T(8,128)S(1)} fusion(bf16[32,8,14336]{2,1,0:T(8,128)(2,1)} %all-to-all-done), kind=kLoop, calls=%fused_computation | loop fusion | flops 7225344 | bytes 7798784 | tf_op jit(solution)/shard_map/reduce_sum | solution.py:62
  274.8 0.3 fusion.57
  275.0 0.7 copy.44
  275.8 7.8 %all-to-all-start.1 = ((bf16[8,16,896]{2,0,1:T(8,128)(2,1)}), bf16[8,16,896]{2,0,1:T(8,128)(2,1)S(1)}, u32[]{:S(2)}, u32[]{:S(2)}) async-start(bf16[8,16,896]{2,0,1:T(8,128)(2,1)} %copy.44), calls=%async_computation.1 | async-start | bytes 458752 | tf_op jit(solution)/shard_map/all_to_all | solution.py:67
  283.6 0.1 constant_dynamic-slice_fusion
  283.7 0.1 copy.45
  283.8 5.3 %all-to-all-done.1 = bf16[8,16,896]{2,0,1:T(8,128)(2,1)S(1)} async-done(((bf16[8,16,896]{2,0,1:T(8,128)(2,1)}), bf16[8,16,896]{2,0,1:T(8,128)(2,1)S(1)}, u32[]{:S(2)}, u32[]{:S(2)}) %all-to-all-start.1) | async-done | bytes 229408 | tf_op jit(solution)/shard_map/all_to_all | solution.py:67
  289.1 0.7 fusion.75
  (19 shorter events, 0.1 us)
Async XLA Ops:
  0.0 16.2 %copy-start = (bf16[128,256]{1,0:T(8,128)(2,1)S(1)}, bf16[128,256]{1,0:T(8,128)(2,1)}, u32[]{:S(2)}) copy-start(bf16[128,256]{1,0:T(8,128)(2,1)} %param.4) | copy-start | bytes 196612
  16.2 3.8 %copy-start.1 = (f32[256,1792]{1,0:T(8,128)S(1)}, f32[256,1792]{1,0:T(8,128)}, u32[]{:S(2)}) copy-start(f32[256,1792]{1,0:T(8,128)} %copy.36) | copy-start | bytes 5505028
  16.2 3.8 %copy-start.10 = (bf16[128,14336]{1,0:T(8,128)(2,1)S(1)}, bf16[128,14336]{1,0:T(8,128)(2,1)}, u32[]{:S(2)}) copy-start(bf16[128,14336]{1,0:T(8,128)(2,1)} %param.5) | copy-start | bytes 11010052
  20.0 2.1 copy-start.2
  22.1 2.0 copy-start.3
  24.1 2.1 copy-start.4
  26.2 2.1 copy-start.5
  28.2 2.1 copy-start.6
  30.3 2.0 copy-start.7
  34.5 16.2 %copy-start.8 = (s32[256,112]{0,1:T(8,128)S(1)}, s32[256,112]{0,1:T(8,128)}, u32[]{:S(2)}) copy-start(s32[256,112]{0,1:T(8,128)} %param.6) | copy-start | bytes 344068
  34.5 236.2 %all-to-all-start = ((bf16[32,8,14336]{2,1,0:T(8,128)(2,1)}), bf16[32,8,14336]{2,1,0:T(8,128)(2,1)}, u32[]{:S(2)}, u32[]{:S(2)}) async-start(bf16[32,8,14336]{2,1,0:T(8,128)(2,1)} %fusion.41), calls=%async_computation | async-start | bytes 14680064 | tf_op jit(solution)/shard_map/all_to_all | solution.py:60
  50.7 0.7 copy-start.9
  275.8 13.3 %all-to-all-start.1 = ((bf16[8,16,896]{2,0,1:T(8,128)(2,1)}), bf16[8,16,896]{2,0,1:T(8,128)(2,1)S(1)}, u32[]{:S(2)}, u32[]{:S(2)}) async-start(bf16[8,16,896]{2,0,1:T(8,128)(2,1)} %copy.44), calls=%async_computation.1 | async-start | bytes 458752 | tf_op jit(solution)/shard_map/all_to_all | solution.py:67
where the time goes:
time: 296 us; the launch traced here: 290 us
  waiting for transfers between devices  224 us (76%)
  starting transfers between devices  24.1 us (8%)
  matrix products  18.2 us (6%)
  local copies, waits for them, and re-layouts  16.5 us (6%)
  other arithmetic  6.56 us (2%)
    all_to_all x1, waiting for transfers between devices, body(): lax.all_to_all(codes, 'intra', split_axis=0, concat_axis=0, tiled=True)  219 us
    dot_general x8, matrix products, make_codes(): lax.dot_general(acts, columns, (((0,), (0,)), ((), ())), preferred_elemen...  18.2 us
    all_to_all x1, starting transfers between devices, body(): lax.all_to_all(codes, 'intra', split_axis=0, concat_axis=0, tiled=True)  16.2 us
    mul x20, local copies, waits for them, and re-layouts, apply_scale(): values.reshape(row_count, col_count // BLK, BLK) * scale[:, :, None]  15.4 us
    all_to_all x1, starting transfers between devices, body(): lax.all_to_all(second, 'inter', split_axis=1, concat_axis=0, tiled=True)  7.85 us
  transfers between devices with their start and end apart: 2, of which 2 were waited for; matrix products, arithmetic and copies ran while one was open for 0% of the time, Pallas kernels for 0%

commit v1 on v0

v1 whole, which is shorter than its diff:
```python
import jax
import jax.numpy as jnp
from jax import lax
from jax.experimental import pallas as pl
from jax.experimental.pallas import tpu as pltpu
from jax.sharding import PartitionSpec as P

BLK = 128
NY = 4
NZ = 8
NG = 16
NM = NY * NZ
HALF = 7168
CZ = HALF // NZ
CY = HALF // NY
OFFS = (2, 1, -1)
MAGIC = 12582912.0
Z_GROUPS = [[y * NZ + z for z in range(NZ)] for y in range(NY)]
Y_GROUPS = [[y * NZ + z for y in range(NY)] for z in range(NZ)]


def y_shift(step):
    return [(y * NZ + z, ((y + step) % NY) * NZ + z) for y in range(NY) for z in range(NZ)]


def last_moves(flip):
    moves = []
    for group in range(NG):
        k, h = group // 2, group % 2
        for y in range(NY):
            for z in range(NZ):
                if h == flip:
                    target = z * NM + y * NZ + k
                else:
                    target = (8 + 2 * y + k % 2) * NM + (k // 2) * NZ + z
                moves.append((group * NM + y * NZ + z, target))
    return moves


def power_two(expo):
    total = jnp.zeros(expo.shape, jnp.float32)
    for power in range(-8, 9):
        total = total + jnp.where(expo == power, jnp.float32(2.0**power), jnp.float32(0.0))
    return total


def round_clip(values):
    return (jnp.clip(values, -127.0, 127.0) + MAGIC) - MAGIC


def pack_kernel(pos, acts, cot, hz, p2, p1, p3, sems):
    y = pos[0]
    copies = []
    for j in range(NZ):
        copies.append((cot.at[:, j * CZ : (j + 1) * CZ], hz.at[j]))
    for step, out in zip(OFFS, (p2, p1, p3)):
        start = HALF + CY * lax.rem(y + step + NY, NY)
        copies.append((cot.at[:, pl.ds(pl.multiple_of(start, CY), CY)], out.at[:, 0:CY]))
        copies.append((acts, out.at[:, CY : CY + 256]))
    started = [pltpu.make_async_copy(src, dst, sems.at[i]) for i, (src, dst) in enumerate(copies)]
    for copy in started:
        copy.start()
    for copy in started:
        copy.wait()


def pack(pos, acts, cot):
    any_spec = pl.BlockSpec(memory_space=pl.ANY)
    wide = jax.ShapeDtypeStruct((128, CY + 256), jnp.bfloat16)
    return pl.pallas_call(
        pack_kernel,
        out_shape=[jax.ShapeDtypeStruct((NZ, 128, CZ), jnp.bfloat16), wide, wide, wide],
        in_specs=[pl.BlockSpec(memory_space=pltpu.SMEM), any_spec, any_spec],
        out_specs=[any_spec] * 4,
        scratch_shapes=[pltpu.SemaphoreType.DMA((NZ + 6,))],
        cost_estimate=pl.CostEstimate(flops=0, bytes_accessed=7000000, transcendentals=0),
    )(pos, acts, cot)


def spread(inverse, first_block, width):
    block = lax.broadcasted_iota(jnp.int32, (BLK, width), 0)
    column = lax.broadcasted_iota(jnp.int32, (BLK, width), 1)
    pick = jnp.where(block == first_block + column // BLK, 1.0, 0.0).astype(jnp.bfloat16)
    return jnp.dot(inverse, pick, preferred_element_type=jnp.float32)


def sum_y_kernel(pos, lhs, inverse, own, q2, q1, q3, out):
    i = pl.program_id(0)
    scale = spread(inverse[...], HALF // BLK + pos[0] * (CY // BLK) + 2 * i, 256)
    total = jnp.zeros((256, 256), jnp.float32)
    for r, part in enumerate((own, q2, q1, q3)):
        local = jnp.dot(lhs[r], part[...], preferred_element_type=jnp.float32)
        total = total + round_clip(local * scale)
    for z in range(NZ):
        rows = [total[64 * y + 8 * z : 64 * y + 8 * z + 8] for y in range(NY)]
        out[z] = jnp.concatenate(rows, axis=0).astype(jnp.int16)


def sum_y(pos, lhs, inverse, cot, q2, q1, q3):
    def piece(i, pos):
        return (0, i)

    return pl.pallas_call(
        sum_y_kernel,
        out_shape=jax.ShapeDtypeStruct((NZ, 32, CY), jnp.int16),
        grid_spec=pltpu.PrefetchScalarGridSpec(
            num_scalar_prefetch=1,
            grid=(CY // 256,),
            in_specs=[
                pl.BlockSpec((4, 256, 128), lambda i, pos: (0, 0, 0)),
                pl.BlockSpec((256, BLK), lambda i, pos: (0, 0)),
                pl.BlockSpec((128, 256), lambda i, pos: (0, HALF // 256 + pos[0] * (CY // 256) + i)),
                pl.BlockSpec((128, 256), piece),
                pl.BlockSpec((128, 256), piece),
                pl.BlockSpec((128, 256), piece),
            ],
            out_specs=pl.BlockSpec((NZ, 32, 256), lambda i, pos: (0, 0, i)),
        ),
        cost_estimate=pl.CostEstimate(flops=2 * 4 * 256 * 128 * CY, bytes_accessed=3000000, transcendentals=0),
    )(pos, lhs, inverse, cot, q2, q1, q3)


def sum_z_kernel(pos, lhs, inverse, parts, own, s2, s1, s3, total_ref):
    i = pl.program_id(0)
    y = pos[0]
    scale = spread(inverse[...], pos[1] * (CZ // BLK) + i, BLK)
    total = jnp.zeros((256, BLK), jnp.float32)
    for r in range(NZ):
        local = jnp.dot(lhs[r], parts[r], preferred_element_type=jnp.float32)
        total = total + round_clip(local * scale)
    total_ref[...] = total
    for step, out in zip((0,) + OFFS, (own, s2, s1, s3)):
        start = 64 * lax.rem(y + step + NY, NY)
        out[...] = total_ref[pl.ds(pl.multiple_of(start, 64), 64), :].astype(jnp.int16)


def sum_z(pos, lhs, inverse, parts):
    return pl.pallas_call(
        sum_z_kernel,
        out_shape=[jax.ShapeDtypeStruct((64, CZ), jnp.int16)] * 4,
        grid_spec=pltpu.PrefetchScalarGridSpec(
            num_scalar_prefetch=1,
            grid=(CZ // BLK,),
            in_specs=[
                pl.BlockSpec((NZ, 256, 128), lambda i, pos: (0, 0, 0)),
                pl.BlockSpec((256, BLK), lambda i, pos: (0, 0)),
                pl.BlockSpec((NZ, 128, BLK), lambda i, pos: (0, 0, i)),
            ],
            out_specs=[pl.BlockSpec((64, BLK), lambda i, pos: (0, i))] * 4,
            scratch_shapes=[pltpu.VMEM((256, BLK), jnp.float32)],
        ),
        cost_estimate=pl.CostEstimate(flops=2 * 8 * 256 * 128 * CZ, bytes_accessed=3000000, transcendentals=0),
    )(pos, lhs, inverse, parts)


def second_kernel(own, s2, s1, s3, sy, scale_z, scale_y, out):
    total = own[...].astype(jnp.float32)
    for part in (s2, s1, s3):
        total = total + part[...].astype(jnp.float32)
    qz = round_clip(total * scale_z[...])
    total = sy[0].astype(jnp.float32)
    for r in range(1, NZ):
        total = total + sy[r].astype(jnp.float32)
    qy = round_clip(total * scale_y[...])
    for k in range(8):
        zk = qz[8 * k : 8 * k + 8]
        yk = qy[8 * (k // 2) : 8 * (k // 2) + 8, CZ * (k % 2) : CZ * (k % 2) + CZ]
        out[2 * k] = jnp.concatenate([zk[0:4], yk[0:4]], axis=0).astype(jnp.bfloat16)
        out[2 * k + 1] = jnp.concatenate([zk[4:8], yk[4:8]], axis=0).astype(jnp.bfloat16)


def second_codes(own, s2, s1, s3, sy, scale_z, scale_y):
    return pl.pallas_call(
        second_kernel,
        out_shape=jax.ShapeDtypeStruct((NG, 8, CZ), jnp.bfloat16),
        cost_estimate=pl.CostEstimate(flops=4000000, bytes_accessed=2500000, transcendentals=0),
    )(own, s2, s1, s3, sy, scale_z, scale_y)


def body(acts, cotangent, first_exp, second_exp):
    member = lax.axis_index("intra")
    group = lax.axis_index("inter")
    y, z = member // NZ, member % NZ
    pos = jnp.stack([y, z]).astype(jnp.int32)

    hz, p2, p1, p3 = pack(pos, acts, cotangent)
    rz = lax.all_to_all(hz, "intra", 0, 0, axis_index_groups=Z_GROUPS, tiled=True)
    q2, q1, q3 = [lax.ppermute(p, "intra", y_shift(step)) for step, p in zip(OFFS, (p2, p1, p3))]

    inverse = jnp.pad(power_two(-first_exp), ((0, 0), (0, BLK - first_exp.shape[1]))).astype(jnp.bfloat16)
    extra = jnp.pad(second_exp, ((0, 0), (0, 256 - second_exp.shape[1]))).astype(jnp.bfloat16)
    along_z = lax.all_gather(jnp.concatenate([acts, extra], 0), "intra", axis_index_groups=Z_GROUPS)
    exp_y = lax.all_gather(second_exp, "intra", axis_index_groups=Y_GROUPS)
    lhs_z = jnp.swapaxes(along_z[:, :128], 1, 2)
    lhs_y = jnp.swapaxes(jnp.stack([acts] + [q[:, CY:] for q in (q2, q1, q3)]), 1, 2)

    blocks_z, blocks_y = CZ // BLK, CY // BLK
    second_z = along_z[:, 128:, : first_exp.shape[1]].reshape(64, -1).astype(jnp.int32)
    first_z = lax.dynamic_slice_in_dim(first_exp, 64 * y, 64, 0)
    diff_z = lax.dynamic_slice_in_dim(first_z - second_z, blocks_z * z, blocks_z, 1)
    scale_z = jnp.repeat(power_two(diff_z), BLK, axis=1)
    first_y = lax.dynamic_slice_in_dim(first_exp.reshape(NY, NZ, 8, -1), z, 1, 1).reshape(32, -1)
    diff_y = first_y - exp_y.reshape(32, -1)
    diff_y = lax.dynamic_slice_in_dim(diff_y, HALF // BLK + blocks_y * y, blocks_y, 1)
    scale_y = jnp.repeat(power_two(diff_y), BLK, axis=1)

    sy = sum_y(pos, lhs_y, inverse, cotangent, q2, q1, q3)
    ry = lax.all_to_all(sy, "intra", 0, 0, axis_index_groups=Z_GROUPS, tiled=True)
    own, s2, s1, s3 = sum_z(pos, lhs_z, inverse, rz)
    t2, t1, t3 = [lax.ppermute(s, "intra", y_shift(step)) for step, s in zip(OFFS, (s2, s1, s3))]
    second = second_codes(own, t2, t1, t3, ry, scale_z, scale_y)

    received = lax.all_to_all(second, "inter", 0, 0, tiled=True)
    total = jnp.sum(received, axis=0, dtype=jnp.float32)
    part_z, part_y = total[:4], total[4:]
    low = group % 2 == 0
    one = lax.ppermute(jnp.where(low, part_z, part_y), ("inter", "intra"), last_moves(0))
    two = lax.ppermute(jnp.where(low, part_y, part_z), ("inter", "intra"), last_moves(1))
    rows = jnp.where(group < 8, jnp.concatenate([one, two], 0), jnp.concatenate([two, one], 0))
    my_exp = lax.dynamic_slice_in_dim(second_exp, group * blocks_z, blocks_z, 1)
    return rows * (jnp.repeat(power_two(my_exp), BLK, axis=1) * (1.0 / (NG * NM)))


def solution(mesh):
    return jax.shard_map(
        body,
        mesh=mesh,
        in_specs=(P(("inter", "intra"), None), P(("inter", "intra"), None), P(), P("intra", None)),
        out_specs=P("intra", "inter"),
        check_vma=False,
    )
```

time: 296 us -> 304 us (1.027); the launches traced: 290 us -> 303 us
  waiting for transfers between devices: 224 us -> 46.8 us
  Pallas kernels: 0 us -> 122 us
  blocking collectives: 0 us -> 56.5 us
  starting transfers between devices: 24.1 us -> 66.9 us
  matrix products: 18.2 us -> 0 us
  local copies, waits for them, and re-layouts: 16.5 us -> 8.3 us
  other arithmetic: 6.56 us -> 1.99 us
    all_to_all x2 -> x3, waiting for transfers between devices: 224 us -> 5.42 us  [the longest x1 5.41 us: body(): received = lax.all_to_all(second, 'inter', 0, 0, tiled=True)]
    pallas_call x0 -> x4, Pallas kernels: none -> 122 us  [the longest x1 105 us: pack(): pl.pallas_call(pack_kernel, out_shape=[jax.ShapeDtypeStruct((NZ, 128, CZ)...]
    all_gather x0 -> x2, blocking collectives: none -> 56.5 us  [the longest x1 42.7 us: body(): lax.all_gather(jnp.concatenate([acts, extra], 0), 'intra', axis_index_gro...]
    ppermute x0 -> x8, starting transfers between devices: none -> 42.1 us  [the longest x3 16.4 us: body(): lax.ppermute(s, 'intra', y_shift(step))]
    ppermute x0 -> x8, waiting for transfers between devices: none -> 41.4 us  [the longest x3 35.6 us: body(): lax.ppermute(p, 'intra', y_shift(step))]
    dot_general x8 -> x0, matrix products: 18.2 us -> none  [make_codes(): lax.dot_general(acts, columns, (((0,), (0,)), ((), ())), preferred_elemen...]
    mul x20 -> x1, local copies, waits for them, and re-layouts: 15.4 us -> 0.08 us  [body(): jnp.repeat(power_two(my_exp), BLK, axis=1) * (1.0 / (NG * NM))]
    unnamed x22 -> x25, local copies, waits for them, and re-layouts: 0.17 us -> 4.68 us
  transfers between devices with their start and end apart: 2 -> 11, of which waited for: 2 -> 3; matrix products, arithmetic and copies ran while one was open for 0% -> 3% of each run, Pallas kernels for 0% -> 5%
where the time goes in v1:
time: 304 us; the launch traced here: 303 us
  Pallas kernels  122 us (40%)
  starting transfers between devices  66.9 us (22%)
  blocking collectives  56.5 us (19%)
  waiting for transfers between devices  46.8 us (15%)
  local copies, waits for them, and re-layouts  8.3 us (3%)
    pallas_call x1, Pallas kernels, pack(): pl.pallas_call(pack_kernel, out_shape=[jax.ShapeDtypeStruct((NZ, 128, CZ)...  105 us
    all_gather x1, blocking collectives, body(): lax.all_gather(jnp.concatenate([acts, extra], 0), 'intra', axis_index_gro...  42.7 us
    ppermute x3, waiting for transfers between devices, body(): lax.ppermute(p, 'intra', y_shift(step))  35.6 us
    ppermute x3, starting transfers between devices, body(): lax.ppermute(s, 'intra', y_shift(step))  16.4 us
    ppermute x3, starting transfers between devices, body(): lax.ppermute(p, 'intra', y_shift(step))  14.5 us
    all_gather x1, blocking collectives, body(): exp_y = lax.all_gather(second_exp, 'intra', axis_index_groups=Y_GROUPS)  13.7 us
    all_to_all x1, starting transfers between devices, body(): lax.all_to_all(hz, 'intra', 0, 0, axis_index_groups=Z_GROUPS, tiled=True)  10.5 us
    all_to_all x1, starting transfers between devices, body(): received = lax.all_to_all(second, 'inter', 0, 0, tiled=True)  7.4 us
  transfers between devices with their start and end apart: 11, of which 3 were waited for; matrix products, arithmetic and copies ran while one was open for 3% of the time, Pallas kernels for 5%

profile of v1, /device:TPU:6, one launch (start us, length us, event | category | flops | bytes accessed | tf_op | source)
XLA Modules:
  0.0 302.5 jit_solution(7188935780126812839)
XLA Ops:
  0.0 0.6 pad_add_fusion.pos
  0.6 105.1 %shard_map.46 = (bf16[8,128,896]{2,1,0:T(8,128)(2,1)}, bf16[128,2048]{1,0:T(8,128)(2,1)}, bf16[128,2048]{1,0:T(8,128)(2,1)}, bf16[128,2048]{1,0:T(8,128)(2,1)}) custom-call(s32[2]{0:T(128)} %pad_add_fusion.pos, bf16[128,256]{1,0:T(8,128)(2,1)} %acts.1, bf16[128,14336]{1,0:T(8,128)(2,1)} %own.1), custom_call_target="tpu_custom_call" | custom-call | bytes 7000000 | tf_op jit(solution)/shard_map/pallas_call | solution.py:70
  105.8 0.0 copy-start.5
  105.8 0.0 copy-start.4
  105.8 10.5 %all-to-all-start = ((bf16[8,128,896]{2,1,0:T(8,128)(2,1)}), bf16[8,128,896]{2,1,0:T(8,128)(2,1)S(1)}, u32[]{:S(2)}, u32[]{:S(2)}) async-start(bf16[8,128,896]{2,1,0:T(8,128)(2,1)} %get-tuple-element.13), calls=%async_computation | async-start | bytes 3670016 | tf_op jit(solution)/shard_map/all_to_all | solution.py:187
  116.2 6.2 %collective-permute-start.5 = (bf16[128,2048]{1,0:T(8,128)(2,1)}, bf16[128,2048]{1,0:T(8,128)(2,1)S(1)}, u32[]{:S(2)}, u32[]{:S(2)}) collective-permute-start(bf16[128,2048]{1,0:T(8,128)(2,1)} %get-tuple-element.20), channel_id=1, source_target_pairs={{0,24},{1,25},{2,26},{3,27},{4,28},{5,29},{6,30},{7,31},{8,0},{9,1... | collective-permute-start | bytes 1572872 | tf_op jit(solution)/shard_map/ppermute | solution.py:188
  122.4 1.9 collective-permute-start.4
  124.3 6.4 %collective-permute-start.3 = (bf16[128,2048]{1,0:T(8,128)(2,1)}, bf16[128,2048]{1,0:T(8,128)(2,1)}, u32[]{:S(2)}, u32[]{:S(2)}) collective-permute-start(bf16[128,2048]{1,0:T(8,128)(2,1)} %get-tuple-element.18), channel_id=1, source_target_pairs={{0,16},{1,17},{2,18},{3,19},{4,20},{5,21},{6,22},{7,23},{8,24},{9,... | collective-permute-start | bytes 1572872 | tf_op jit(solution)/shard_map/ppermute | solution.py:188
  130.7 0.1 copy.11
  130.8 0.2 add_convert_fusion
  131.1 0.6 pad.11.inverse
  131.7 35.6 %collective-permute-done.5.q3 = bf16[128,2048]{1,0:T(8,128)(2,1)S(1)} collective-permute-done((bf16[128,2048]{1,0:T(8,128)(2,1)}, bf16[128,2048]{1,0:T(8,128)(2,1)S(1)}, u32[]{:S(2)}, u32[]{:S(2)}) %collective-permute-start.5) | collective-permute-done | bytes 524320 | tf_op jit(solution)/shard_map/ppermute | solution.py:188
  167.4 0.0 collective-permute-done.3.q2
  167.4 0.9 slice_bitcast_fusion.2
  168.4 0.8 copy.12.lhs
  169.2 7.1 %shard_map.48 = s16[8,32,1792]{2,1,0:T(8,128)(2,1)} custom-call(s32[2]{0:T(128)} %pad_add_fusion.pos, bf16[4,256,128]{2,1,0:T(8,128)(2,1)} %copy.12.lhs, bf16[256,128]{1,0:T(8,128)(2,1)} %pad.11.inverse, bf16[128,14336]{1,0:T(8,128)(2,1)} %own.1, bf16[128,2048]{1,0:T(8,128)(2,1)} %collective-permute-done.3.q2, bf16[128,2048]{1,0:T(8,128)(2,1)} %copy-done.3, ...), custom_call_target="tpu_custom_call" | custom-call | flops 469762048 | bytes 3000000 | tf_op jit(solution)/shard_map/pallas_call | solution.py:103
  176.4 6.9 %all-to-all-start.1 = ((s16[8,32,1792]{2,1,0:T(8,128)(2,1)}), s16[8,32,1792]{2,1,0:T(8,128)(2,1)S(1)}, u32[]{:S(2)}, u32[]{:S(2)}) async-start(s16[8,32,1792]{2,1,0:T(8,128)(2,1)} %shard_map.48), calls=%async_computation.1 | async-start | bytes 1835008 | tf_op jit(solution)/shard_map/all_to_all | solution.py:208
  183.4 42.7 %all-gather = bf16[1088,256]{1,0:T(8,128)(2,1)S(1)} all-gather(bf16[136,256]{1,0:T(8,128)(2,1)S(1)} %fusion.1), channel_id=2, replica_groups={{0,1,2,3,4,5,6,7},{8,9,10,11,12,13,14,15},{16,17,18,19,20,21,22,23},{24..., dimensions={0}, use_global_device_ids=true | all-gather | bytes 626688 | tf_op jit(solution)/shard_map/all_gather | solution.py:192
  226.1 0.8 slice.28
  226.9 2.0 copy.16
  229.0 0.1 select_add_fusion
  229.1 7.0 %shard_map.47 = (s16[64,896]{1,0:T(8,128)(2,1)}, s16[64,896]{1,0:T(8,128)(2,1)}, s16[64,896]{1,0:T(8,128)(2,1)}, s16[64,896]{1,0:T(8,128)(2,1)}) custom-call(s32[2]{0:T(128)} %pad_add_fusion.pos, bf16[8,256,128]{2,1,0:T(8,128)(2,1)} %bitcast.31, bf16[256,128]{1,0:T(8,128)(2,1)} %pad.11.inverse, bf16[8,128,896]{2,1,0:T(8,128)(2,1)} %copy-done), custom_call_target="tpu_custom_call" | custom-call | flops 469762048 | bytes 3000000 | tf_op jit(solution)/shard_map/pallas_call | solution.py:138
  236.1 1.9 collective-permute-start
  238.1 10.2 %collective-permute-start.1 = (s16[64,896]{1,0:T(8,128)(2,1)}, s16[64,896]{1,0:T(8,128)(2,1)S(1)}, u32[]{:S(2)}, u32[]{:S(2)}) collective-permute-start(s16[64,896]{1,0:T(8,128)(2,1)} %get-tuple-element.16), channel_id=1, source_target_pairs={{0,8},{1,9},{2,10},{3,11},{4,12},{5,13},{6,14},{7,15},{8,16},{9,17... | collective-permute-start | bytes 344072 | tf_op jit(solution)/shard_map/ppermute | solution.py:210
  248.3 4.2 %collective-permute-start.2 = (s16[64,896]{1,0:T(8,128)(2,1)}, s16[64,896]{1,0:T(8,128)(2,1)S(1)}, u32[]{:S(2)}, u32[]{:S(2)}) collective-permute-start(s16[64,896]{1,0:T(8,128)(2,1)} %get-tuple-element.17), channel_id=1, source_target_pairs={{0,24},{1,25},{2,26},{3,27},{4,28},{5,29},{6,30},{7,31},{8,0},{9,1... | collective-permute-start | bytes 344072 | tf_op jit(solution)/shard_map/ppermute | solution.py:210
  252.5 13.7 %all-gather.1 = s32[32,112]{1,0:T(8,128)S(1)} all-gather(s32[8,112]{1,0:T(8,128)S(1)} %copy-done.9), channel_id=3, replica_groups={{0,8,16,24},{1,9,17,25},{2,10,18,26},{3,11,19,27},{4,12,20,28},{5,13,21..., dimensions={0}, use_global_device_ids=true | all-gather | bytes 17920 | tf_op jit(solution)/shard_map/all_gather | solution.py:193
  266.3 0.1 broadcast_in_dim.333
  266.4 0.8 copy.22
  267.1 0.1 select_add_fusion.1
  267.2 0.1 broadcast_in_dim.352
  267.4 0.8 copy.21
  268.2 0.0 all-to-all-done.1.sy
  268.2 0.0 collective-permute-done.1.s1
  268.2 0.0 collective-permute-done.2.s3
  268.2 0.9 copy-done.1
  269.1 0.0 copy-done.6
  269.1 0.1 copy-done.7
  269.2 0.0 copy-done.8
  269.2 2.6 shard_map.49
  271.8 7.4 %all-to-all-start.2 = ((bf16[16,8,896]{2,1,0:T(8,128)(2,1)}), bf16[16,8,896]{2,1,0:T(8,128)(2,1)S(1)}, u32[]{:S(2)}, u32[]{:S(2)}) async-start(bf16[16,8,896]{2,1,0:T(8,128)(2,1)} %shard_map.49), calls=%async_computation.2 | async-start | bytes 458752 | tf_op jit(solution)/shard_map/all_to_all | solution.py:213
  279.2 5.4 %all-to-all-done.2 = bf16[16,8,896]{2,1,0:T(8,128)(2,1)S(1)} async-done(((bf16[16,8,896]{2,1,0:T(8,128)(2,1)}), bf16[16,8,896]{2,1,0:T(8,128)(2,1)S(1)}, u32[]{:S(2)}, u32[]{:S(2)}) %all-to-all-start.2) | async-done | bytes 229408 | tf_op jit(solution)/shard_map/all_to_all | solution.py:213
  284.7 5.6 %collective-permute-start.6 = (f32[4,896]{1,0:T(4,128)S(1)}, f32[4,896]{1,0:T(4,128)S(1)}, u32[]{:S(2)}, u32[]{:S(2)}) collective-permute-start(f32[4,896]{1,0:T(4,128)S(1)} %get-tuple-element.21), channel_id=1, source_target_pairs={{0,0},{1,32},{2,64},{3,96},{4,128},{5,160},{6,192},{7,224},{8,8},{... | collective-permute-start | bytes 43016 | tf_op jit(solution)/shard_map/ppermute | solution.py:217
  290.2 5.7 %collective-permute-start.7 = (f32[4,896]{1,0:T(4,128)S(1)}, f32[4,896]{1,0:T(4,128)S(1)}, u32[]{:S(2)}, u32[]{:S(2)}) collective-permute-start(f32[4,896]{1,0:T(4,128)S(1)} %get-tuple-element.22), channel_id=1, source_target_pairs={{0,256},{1,257},{2,258},{3,259},{4,260},{5,261},{6,262},{7,263},{8... | collective-permute-start | bytes 43016 | tf_op jit(solution)/shard_map/ppermute | solution.py:218
  295.9 0.1 add_multiply_fusion
  296.0 0.1 copy.15
  296.1 0.0 collective-permute-done.6
  296.1 5.8 %collective-permute-done.7 = f32[4,896]{1,0:T(4,128)S(1)} collective-permute-done((f32[4,896]{1,0:T(4,128)S(1)}, f32[4,896]{1,0:T(4,128)S(1)}, u32[]{:S(2)}, u32[]{:S(2)}) %collective-permute-start.7) | collective-permute-done | bytes 14368 | tf_op jit(solution)/shard_map/ppermute | solution.py:218
  301.8 0.7 fusion.2
  (26 shorter events, 0.2 us)
Async XLA Ops:
  105.8 25.0 %copy-start.5 = (s32[256,112]{0,1:T(8,128)S(1)}, s32[256,112]{0,1:T(8,128)}, u32[]{:S(2)}) copy-start(s32[256,112]{0,1:T(8,128)} %param.6) | copy-start | bytes 344068
  105.8 62.6 %copy-start.4 = (bf16[128,256]{1,0:T(8,128)(2,1)S(1)}, bf16[128,256]{1,0:T(8,128)(2,1)}, u32[]{:S(2)}) copy-start(bf16[128,256]{1,0:T(8,128)(2,1)} %acts.1) | copy-start | bytes 196612
  105.8 70.6 %all-to-all-start = ((bf16[8,128,896]{2,1,0:T(8,128)(2,1)}), bf16[8,128,896]{2,1,0:T(8,128)(2,1)S(1)}, u32[]{:S(2)}, u32[]{:S(2)}) async-start(bf16[8,128,896]{2,1,0:T(8,128)(2,1)} %get-tuple-element.13), calls=%async_computation | async-start | bytes 3670016 | tf_op jit(solution)/shard_map/all_to_all | solution.py:187
  116.2 51.1 %collective-permute-start.5 = (bf16[128,2048]{1,0:T(8,128)(2,1)}, bf16[128,2048]{1,0:T(8,128)(2,1)S(1)}, u32[]{:S(2)}, u32[]{:S(2)}) collective-permute-start(bf16[128,2048]{1,0:T(8,128)(2,1)} %get-tuple-element.20), channel_id=1, source_target_pairs={{0,24},{1,25},{2,26},{3,27},{4,28},{5,29},{6,30},{7,31},{8,0},{9,1... | collective-permute-start | bytes 1572872 | tf_op jit(solution)/shard_map/ppermute | solution.py:188
  122.4 45.0 %collective-permute-start.4 = (bf16[128,2048]{1,0:T(8,128)(2,1)}, bf16[128,2048]{1,0:T(8,128)(2,1)S(1)}, u32[]{:S(2)}, u32[]{:S(2)}) collective-permute-start(bf16[128,2048]{1,0:T(8,128)(2,1)} %get-tuple-element.19), channel_id=1, source_target_pairs={{0,8},{1,9},{2,10},{3,11},{4,12},{5,13},{6,14},{7,15},{8,16},{9,17... | collective-permute-start | bytes 1572872 | tf_op jit(solution)/shard_map/ppermute | solution.py:188
  124.3 43.1 %collective-permute-start.3 = (bf16[128,2048]{1,0:T(8,128)(2,1)}, bf16[128,2048]{1,0:T(8,128)(2,1)}, u32[]{:S(2)}, u32[]{:S(2)}) collective-permute-start(bf16[128,2048]{1,0:T(8,128)(2,1)} %get-tuple-element.18), channel_id=1, source_target_pairs={{0,16},{1,17},{2,18},{3,19},{4,20},{5,21},{6,22},{7,23},{8,24},{9,... | collective-permute-start | bytes 1572872 | tf_op jit(solution)/shard_map/ppermute | solution.py:188
  167.3 1.9 copy-start.2
  167.4 1.9 copy-start.3
  176.4 7.0 %copy-start.9 = (s32[8,112]{1,0:T(8,128)S(1)}, s32[8,112]{1,0:T(8,128)}, u32[]{:S(2)}) copy-start(s32[8,112]{1,0:T(8,128)} %param.7) | copy-start | bytes 10756
  176.4 52.6 %copy-start = (bf16[8,128,896]{2,1,0:T(8,128)(2,1)}, bf16[8,128,896]{2,1,0:T(8,128)(2,1)S(1)}, u32[]{:S(2)}) copy-start(bf16[8,128,896]{2,1,0:T(8,128)(2,1)S(1)} %all-to-all-done.parts) | copy-start | bytes 5505028
  176.4 91.8 %all-to-all-start.1 = ((s16[8,32,1792]{2,1,0:T(8,128)(2,1)}), s16[8,32,1792]{2,1,0:T(8,128)(2,1)S(1)}, u32[]{:S(2)}, u32[]{:S(2)}) async-start(s16[8,32,1792]{2,1,0:T(8,128)(2,1)} %shard_map.48), calls=%async_computation.1 | async-start | bytes 1835008 | tf_op jit(solution)/shard_map/all_to_all | solution.py:208
  236.1 32.0 %collective-permute-start = (s16[64,896]{1,0:T(8,128)(2,1)}, s16[64,896]{1,0:T(8,128)(2,1)S(1)}, u32[]{:S(2)}, u32[]{:S(2)}) collective-permute-start(s16[64,896]{1,0:T(8,128)(2,1)} %get-tuple-element.15), channel_id=1, source_target_pairs={{0,16},{1,17},{2,18},{3,19},{4,20},{5,21},{6,22},{7,23},{8,24},{9,... | collective-permute-start | bytes 344072 | tf_op jit(solution)/shard_map/ppermute | solution.py:210
  238.1 30.1 %collective-permute-start.1 = (s16[64,896]{1,0:T(8,128)(2,1)}, s16[64,896]{1,0:T(8,128)(2,1)S(1)}, u32[]{:S(2)}, u32[]{:S(2)}) collective-permute-start(s16[64,896]{1,0:T(8,128)(2,1)} %get-tuple-element.16), channel_id=1, source_target_pairs={{0,8},{1,9},{2,10},{3,11},{4,12},{5,13},{6,14},{7,15},{8,16},{9,17... | collective-permute-start | bytes 344072 | tf_op jit(solution)/shard_map/ppermute | solution.py:210
  248.3 19.9 %collective-permute-start.2 = (s16[64,896]{1,0:T(8,128)(2,1)}, s16[64,896]{1,0:T(8,128)(2,1)S(1)}, u32[]{:S(2)}, u32[]{:S(2)}) collective-permute-start(s16[64,896]{1,0:T(8,128)(2,1)} %get-tuple-element.17), channel_id=1, source_target_pairs={{0,24},{1,25},{2,26},{3,27},{4,28},{5,29},{6,30},{7,31},{8,0},{9,1... | collective-permute-start | bytes 344072 | tf_op jit(solution)/shard_map/ppermute | solution.py:210
  268.2 0.9 copy-start.1
  268.2 1.0 copy-start.6
  268.2 1.0 copy-start.7
  268.2 1.0 copy-start.8
  271.8 12.8 %all-to-all-start.2 = ((bf16[16,8,896]{2,1,0:T(8,128)(2,1)}), bf16[16,8,896]{2,1,0:T(8,128)(2,1)S(1)}, u32[]{:S(2)}, u32[]{:S(2)}) async-start(bf16[16,8,896]{2,1,0:T(8,128)(2,1)} %shard_map.49), calls=%async_computation.2 | async-start | bytes 458752 | tf_op jit(solution)/shard_map/all_to_all | solution.py:213
  284.7 11.4 %collective-permute-start.6 = (f32[4,896]{1,0:T(4,128)S(1)}, f32[4,896]{1,0:T(4,128)S(1)}, u32[]{:S(2)}, u32[]{:S(2)}) collective-permute-start(f32[4,896]{1,0:T(4,128)S(1)} %get-tuple-element.21), channel_id=1, source_target_pairs={{0,0},{1,32},{2,64},{3,96},{4,128},{5,160},{6,192},{7,224},{8,8},{... | collective-permute-start | bytes 43016 | tf_op jit(solution)/shard_map/ppermute | solution.py:217
  290.2 11.6 %collective-permute-start.7 = (f32[4,896]{1,0:T(4,128)S(1)}, f32[4,896]{1,0:T(4,128)S(1)}, u32[]{:S(2)}, u32[]{:S(2)}) collective-permute-start(f32[4,896]{1,0:T(4,128)S(1)} %get-tuple-element.22), channel_id=1, source_target_pairs={{0,256},{1,257},{2,258},{3,259},{4,260},{5,261},{6,262},{7,263},{8... | collective-permute-start | bytes 43016 | tf_op jit(solution)/shard_map/ppermute | solution.py:218

commit v2 on v1

v2 whole, which is shorter than its diff:
```python
import jax
import jax.numpy as jnp
from jax import lax
from jax.experimental import pallas as pl
from jax.experimental.pallas import tpu as pltpu
from jax.sharding import PartitionSpec as P

BLK = 128
NY = 4
NZ = 8
NG = 16
NM = NY * NZ
HALF = 7168
CZ = HALF // NZ
CY = HALF // NY
OFFS = (2, 1, -1)
MAGIC = 12582912.0
Z_GROUPS = [[y * NZ + z for z in range(NZ)] for y in range(NY)]


def y_shift(step):
    return [(y * NZ + z, ((y + step) % NY) * NZ + z) for y in range(NY) for z in range(NZ)]


def last_moves():
    moves = []
    for group in range(NG):
        for y in range(NY):
            for z in range(NZ):
                if group < 8:
                    target = z * NM + y * NZ + group
                else:
                    target = (8 + 2 * y + group % 2) * NM + ((group - 8) // 2) * NZ + z
                moves.append((group * NM + y * NZ + z, target))
    return moves


def power_two(expo):
    total = jnp.zeros(expo.shape, jnp.float32)
    for power in range(-8, 9):
        total = total + jnp.where(expo == power, jnp.float32(2.0**power), jnp.float32(0.0))
    return total


def round_clip(values):
    return (jnp.clip(values, -127.0, 127.0) + MAGIC) - MAGIC


def pack_z_kernel(acts, exps, cot, out, held, padded, into, outof):
    loads = []
    for j in range(NZ):
        for b in range(CZ // BLK):
            column = j * CZ + b * BLK
            rows = pl.ds(256 + b * BLK, BLK)
            loads.append(
                pltpu.make_async_copy(cot.at[:, column : column + BLK], held.at[j, rows, :], into.at[len(loads)])
            )
    for load in loads:
        load.start()
    turned = acts[...].T
    padded[...] = jnp.zeros((16, BLK), jnp.float32)
    padded[0:8, 0 : exps.shape[1]] = exps[...].astype(jnp.float32)
    tail = padded[...].astype(jnp.bfloat16)
    for j in range(NZ):
        held[j, 0:256, :] = turned
        held[j, 256 + CZ : 256 + CZ + 16, :] = tail
    stores = [pltpu.make_async_copy(held.at[j], out.at[j], outof.at[j]) for j in range(NZ)]
    for j in range(NZ):
        for b in range(CZ // BLK):
            loads[j * (CZ // BLK) + b].wait()
        stores[j].start()
    for store in stores:
        store.wait()


def pack_z(acts, exps, cot):
    shape = (NZ, 256 + CZ + 16, BLK)
    any_spec = pl.BlockSpec(memory_space=pl.ANY)
    vmem_spec = pl.BlockSpec(memory_space=pltpu.VMEM)
    return pl.pallas_call(
        pack_z_kernel,
        out_shape=jax.ShapeDtypeStruct(shape, jnp.bfloat16),
        in_specs=[vmem_spec, vmem_spec, any_spec],
        out_specs=any_spec,
        scratch_shapes=[
            pltpu.VMEM(shape, jnp.bfloat16),
            pltpu.VMEM((16, BLK), jnp.float32),
            pltpu.SemaphoreType.DMA((HALF // BLK,)),
            pltpu.SemaphoreType.DMA((NZ,)),
        ],
        cost_estimate=pl.CostEstimate(flops=0, bytes_accessed=4000000, transcendentals=0),
    )(acts, exps, cot)


def pack_y_kernel(pos, hz, cot, p2, p1, p3, held, into, outof):
    loads, stores = [], []
    per = CY // BLK + 2
    for i, (step, out) in enumerate(zip(OFFS, (p2, p1, p3))):
        start = HALF + CY * lax.rem(pos[0] + step + NY, NY)
        moves = [(hz.at[0, 0:256], held.at[i, 0:256]), (hz.at[0, pl.ds(256 + CZ, 16)], held.at[i, pl.ds(256 + CY, 16)])]
        for b in range(CY // BLK):
            column = pl.multiple_of(start + b * BLK, BLK)
            moves.append((cot.at[:, pl.ds(column, BLK)], held.at[i, pl.ds(256 + b * BLK, BLK), :]))
        loads += [pltpu.make_async_copy(src, dst, into.at[i * per + k]) for k, (src, dst) in enumerate(moves)]
        stores.append(pltpu.make_async_copy(held.at[i], out, outof.at[i]))
    for load in loads:
        load.start()
    for i in range(3):
        for k in range(per):
            loads[i * per + k].wait()
        stores[i].start()
    for store in stores:
        store.wait()


def pack_y(pos, hz, cot):
    any_spec = pl.BlockSpec(memory_space=pl.ANY)
    piece = jax.ShapeDtypeStruct((256 + CY + 16, BLK), jnp.bfloat16)
    return pl.pallas_call(
        pack_y_kernel,
        out_shape=[piece, piece, piece],
        in_specs=[pl.BlockSpec(memory_space=pltpu.SMEM), any_spec, any_spec],
        out_specs=[any_spec] * 3,
        scratch_shapes=[
            pltpu.VMEM((3, 256 + CY + 16, BLK), jnp.bfloat16),
            pltpu.SemaphoreType.DMA((3 * (CY // BLK + 2),)),
            pltpu.SemaphoreType.DMA((3,)),
        ],
        cost_estimate=pl.CostEstimate(flops=0, bytes_accessed=3000000, transcendentals=0),
    )(pos, hz, cot)


def spread(inverse, first_block, width):
    block = lax.broadcasted_iota(jnp.int32, (BLK, width), 0)
    column = lax.broadcasted_iota(jnp.int32, (BLK, width), 1)
    pick = jnp.where(block == first_block + column // BLK, 1.0, 0.0).astype(jnp.bfloat16)
    return jnp.dot(inverse, pick, preferred_element_type=jnp.float32)


def sum_y_kernel(pos, inverse, own_lhs, lhs2, lhs1, lhs3, own, q2, q1, q3, out):
    i = pl.program_id(0)
    scale = spread(inverse[...], HALF // BLK + pos[0] * (CY // BLK) + 2 * i, 256)
    local = jnp.dot(own_lhs[0], own[...], preferred_element_type=jnp.float32)
    total = round_clip(local * scale)
    for lhs, part in ((lhs2, q2), (lhs1, q1), (lhs3, q3)):
        both = jnp.concatenate([part[0:BLK], part[BLK : 2 * BLK]], axis=1)
        local = jnp.dot(lhs[...], both, preferred_element_type=jnp.float32)
        total = total + round_clip(local * scale)
    for z in range(NZ):
        rows = [total[64 * y + 8 * z : 64 * y + 8 * z + 8] for y in range(NY)]
        out[z] = jnp.concatenate(rows, axis=0).astype(jnp.int16)


def sum_y(pos, inverse, hz, cot, q2, q1, q3):
    lhs = pl.BlockSpec((256, BLK), lambda i, pos: (0, 0))
    piece = pl.BlockSpec((256, BLK), lambda i, pos: (1 + i, 0))
    return pl.pallas_call(
        sum_y_kernel,
        out_shape=jax.ShapeDtypeStruct((NZ, 32, CY), jnp.int16),
        grid_spec=pltpu.PrefetchScalarGridSpec(
            num_scalar_prefetch=1,
            grid=(CY // 256,),
            in_specs=[
                pl.BlockSpec((256, BLK), lambda i, pos: (0, 0)),
                pl.BlockSpec((1, 256, BLK), lambda i, pos: (0, 0, 0)),
                lhs,
                lhs,
                lhs,
                pl.BlockSpec((128, 256), lambda i, pos: (0, HALF // 256 + pos[0] * (CY // 256) + i)),
                piece,
                piece,
                piece,
            ],
            out_specs=pl.BlockSpec((NZ, 32, 256), lambda i, pos: (0, 0, i)),
        ),
        cost_estimate=pl.CostEstimate(flops=2 * 4 * 256 * 128 * CY, bytes_accessed=3000000, transcendentals=0),
    )(pos, inverse, hz, q2, q1, q3, cot, q2, q1, q3)


def sum_z_kernel(pos, inverse, lhs, parts, own, s2, s1, s3, total_ref):
    i = pl.program_id(0)
    y = pos[0]
    scale = spread(inverse[...], pos[1] * (CZ // BLK) + i, BLK)
    total = jnp.zeros((256, BLK), jnp.float32)
    for r in range(NZ):
        local = jnp.dot(lhs[r], parts[r], preferred_element_type=jnp.float32)
        total = total + round_clip(local * scale)
    total_ref[...] = total
    for step, out in zip((0,) + OFFS, (own, s2, s1, s3)):
        start = 64 * lax.rem(y + step + NY, NY)
        out[...] = total_ref[pl.ds(pl.multiple_of(start, 64), 64), :].astype(jnp.int16)


def sum_z(pos, inverse, parts):
    return pl.pallas_call(
        sum_z_kernel,
        out_shape=[jax.ShapeDtypeStruct((64, CZ), jnp.int16)] * 4,
        grid_spec=pltpu.PrefetchScalarGridSpec(
            num_scalar_prefetch=1,
            grid=(CZ // BLK,),
            in_specs=[
                pl.BlockSpec((256, BLK), lambda i, pos: (0, 0)),
                pl.BlockSpec((NZ, 256, BLK), lambda i, pos: (0, 0, 0)),
                pl.BlockSpec((NZ, BLK, BLK), lambda i, pos: (0, 2 + i, 0)),
            ],
            out_specs=[pl.BlockSpec((64, BLK), lambda i, pos: (0, i))] * 4,
            scratch_shapes=[pltpu.VMEM((256, BLK), jnp.float32)],
        ),
        cost_estimate=pl.CostEstimate(flops=2 * 8 * 256 * 128 * CZ, bytes_accessed=3000000, transcendentals=0),
    )(pos, inverse, parts, parts)


def second_kernel(own, s2, s1, s3, sy, scale_z, scale_y, out):
    total = own[...].astype(jnp.float32)
    for part in (s2, s1, s3):
        total = total + part[...].astype(jnp.float32)
    qz = round_clip(total * scale_z[...])
    total = sy[0].astype(jnp.float32)
    for r in range(1, NZ):
        total = total + sy[r].astype(jnp.float32)
    qy = round_clip(total * scale_y[...])
    for k in range(8):
        out[k] = qz[8 * k : 8 * k + 8].astype(jnp.bfloat16)
        yk = qy[8 * (k // 2) : 8 * (k // 2) + 8, CZ * (k % 2) : CZ * (k % 2) + CZ]
        out[8 + k] = yk.astype(jnp.bfloat16)


def second_codes(own, s2, s1, s3, sy, scale_z, scale_y):
    return pl.pallas_call(
        second_kernel,
        out_shape=jax.ShapeDtypeStruct((NG, 8, CZ), jnp.bfloat16),
        cost_estimate=pl.CostEstimate(flops=4000000, bytes_accessed=2500000, transcendentals=0),
    )(own, s2, s1, s3, sy, scale_z, scale_y)


def body(acts, cotangent, first_exp, second_exp):
    member = lax.axis_index("intra")
    group = lax.axis_index("inter")
    y, z = member // NZ, member % NZ
    pos = jnp.stack([y, z]).astype(jnp.int32)

    hz = pack_z(acts, second_exp, cotangent)
    rz = lax.all_to_all(hz, "intra", 0, 0, axis_index_groups=Z_GROUPS, tiled=True)
    q2, q1, q3 = [lax.ppermute(p, "intra", y_shift(step)) for step, p in zip(OFFS, pack_y(pos, hz, cotangent))]
    inverse = jnp.pad(power_two(-first_exp), ((0, 0), (0, BLK - first_exp.shape[1]))).astype(jnp.bfloat16)

    blocks_z, blocks_y = CZ // BLK, CY // BLK
    count = first_exp.shape[1]
    by_y_z = first_exp.reshape(NY, NZ, 8, count)
    first_z = lax.dynamic_index_in_dim(by_y_z, y, 0, False)
    diff_z = (first_z - rz[:, 256 + CZ : 264 + CZ, :count].astype(jnp.int32)).reshape(64, count)
    diff_z = lax.dynamic_slice_in_dim(diff_z, blocks_z * z, blocks_z, 1)
    scale_z = jnp.repeat(power_two(diff_z), BLK, axis=1)
    by_step = jnp.stack([second_exp] + [q[256 + CY : 264 + CY, :count].astype(jnp.int32) for q in (q3, q2, q1)])
    second_y = by_step[(jnp.arange(NY) - y) % NY]
    diff_y = (lax.dynamic_index_in_dim(by_y_z, z, 1, False) - second_y).reshape(32, count)
    diff_y = lax.dynamic_slice_in_dim(diff_y, HALF // BLK + blocks_y * y, blocks_y, 1)
    scale_y = jnp.repeat(power_two(diff_y), BLK, axis=1)

    sy = sum_y(pos, inverse, hz, cotangent, q2, q1, q3)
    ry = lax.all_to_all(sy, "intra", 0, 0, axis_index_groups=Z_GROUPS, tiled=True)
    own, s2, s1, s3 = sum_z(pos, inverse, rz)
    t2, t1, t3 = [lax.ppermute(s, "intra", y_shift(step)) for step, s in zip(OFFS, (s2, s1, s3))]
    second = second_codes(own, t2, t1, t3, ry, scale_z, scale_y)

    received = lax.all_to_all(second, "inter", 0, 0, tiled=True)
    total = jnp.sum(received, axis=0, dtype=jnp.float32)
    rows = lax.ppermute(total, ("inter", "intra"), last_moves())
    my_exp = lax.dynamic_slice_in_dim(second_exp, group * blocks_z, blocks_z, 1)
    return rows * (jnp.repeat(power_two(my_exp), BLK, axis=1) * (1.0 / (NG * NM)))


def solution(mesh):
    return jax.shard_map(
        body,
        mesh=mesh,
        in_specs=(P(("inter", "intra"), None), P(("inter", "intra"), None), P(), P("intra", None)),
        out_specs=P("intra", "inter"),
        check_vma=False,
    )
```

time: 304 us -> 145 us (0.48)
  Pallas kernels: 122 us -> 24 us
  blocking collectives: 56.5 us -> 0 us
  starting transfers between devices: 66.9 us -> 55.7 us
  waiting for transfers between devices: 46.8 us -> 50.6 us
  other arithmetic: 1.99 us -> 5.6 us
    pallas_call x1 -> x2, Pallas kernels: 105 us -> 7.28 us  [the longest x1 3.76 us: pack_z(): pl.pallas_call(pack_z_kernel, out_shape=jax.ShapeDtypeStruct(shape, jnp.b...]
    all_gather x2 -> x0, blocking collectives: 56.5 us -> none  [the longest x1 42.7 us: body(): lax.all_gather(jnp.concatenate([acts, extra], 0), 'intra', axis_index_gro...]
    ppermute x2 -> x1, starting transfers between devices: 11.2 us -> 5.41 us  [body(): rows = lax.ppermute(total, ('inter', 'intra'), last_moves())]
    ppermute x3, waiting for transfers between devices: 0.01 us -> 4.55 us  [body(): lax.ppermute(s, 'intra', y_shift(step))]
    ppermute x3, starting transfers between devices: 16.4 us -> 12.6 us  [body(): lax.ppermute(s, 'intra', y_shift(step))]
  transfers between devices with their start and end apart: 11 -> 10, of which waited for: 3 -> 8; matrix products, arithmetic and copies ran while one was open for 3% -> 7% of each run, Pallas kernels for 5% -> 12%
where the time goes in v2:
time: 145 us; the launch traced here: 142 us
  starting transfers between devices  55.7 us (38%)
  waiting for transfers between devices  50.6 us (35%)
  Pallas kernels  24 us (17%)
  local copies, waits for them, and re-layouts  6.06 us (4%)
  other arithmetic  5.6 us (4%)
    ppermute x3, waiting for transfers between devices, body(): lax.ppermute(p, 'intra', y_shift(step))  35.4 us
    ppermute x3, starting transfers between devices, body(): lax.ppermute(p, 'intra', y_shift(step))  15.7 us
    ppermute x3, starting transfers between devices, body(): lax.ppermute(s, 'intra', y_shift(step))  12.6 us
    all_to_all x1, starting transfers between devices, body(): lax.all_to_all(hz, 'intra', 0, 0, axis_index_groups=Z_GROUPS, tiled=True)  10.3 us
    pallas_call x1, Pallas kernels, sum_y(): pl.pallas_call(sum_y_kernel, out_shape=jax.ShapeDtypeStruct((NZ, 32, CY),...  7.13 us
    pallas_call x1, Pallas kernels, sum_z(): pl.pallas_call(sum_z_kernel, out_shape=[jax.ShapeDtypeStruct((64, CZ), jn...  7.09 us
    all_to_all x1, starting transfers between devices, body(): lax.all_to_all(sy, 'intra', 0, 0, axis_index_groups=Z_GROUPS, tiled=True)  6.98 us
    all_to_all x1, waiting for transfers between devices, body(): received = lax.all_to_all(second, 'inter', 0, 0, tiled=True)  5.41 us
  transfers between devices with their start and end apart: 10, of which 8 were waited for; matrix products, arithmetic and copies ran while one was open for 7% of the time, Pallas kernels for 12%

profile of v2, /device:TPU:6, one launch (start us, length us, event | category | flops | bytes accessed | tf_op | source)
XLA Modules:
  0.0 142.2 jit_solution(10763902925622713176)
XLA Ops:
  0.0 3.8 %shard_map.46.hz.own_lhs = bf16[8,1168,128]{2,1,0:T(8,128)(2,1)} custom-call(bf16[128,256]{1,0:T(8,128)(2,1)} %acts.1, s32[8,112]{1,0:T(8,128)} %exps.1, bf16[128,14336]{1,0:T(8,128)(2,1)} %own.1), custom_call_target="tpu_custom_call" | custom-call | bytes 4000000 | tf_op jit(solution)/shard_map/pallas_call | solution.py:80
  3.8 10.3 %all-to-all-start = ((bf16[8,1168,128]{2,1,0:T(8,128)(2,1)}), bf16[8,1168,128]{2,1,0:T(8,128)(2,1)S(1)}, u32[]{:S(2)}, u32[]{:S(2)}) async-start(bf16[8,1168,128]{2,1,0:T(8,128)(2,1)} %shard_map.46.hz.own_lhs), calls=%async_computation | async-start | bytes 4784128 | tf_op jit(solution)/shard_map/all_to_all | solution.py:243
  14.1 0.6 pad_add_fusion.1.pos
  14.7 3.5 %shard_map.48 = (bf16[2064,128]{1,0:T(8,128)(2,1)}, bf16[2064,128]{1,0:T(8,128)(2,1)}, bf16[2064,128]{1,0:T(8,128)(2,1)}) custom-call(s32[2]{0:T(128)} %pad_add_fusion.1.pos, bf16[8,1168,128]{2,1,0:T(8,128)(2,1)} %shard_map.46.hz.own_lhs, bf16[128,14336]{1,0:T(8,128)(2,1)} %own.1), custom_call_target="tpu_custom_call" | custom-call | bytes 3000000 | tf_op jit(solution)/shard_map/pallas_call | solution.py:119
  18.2 7.7 %collective-permute-start.3 = (bf16[2064,128]{1,0:T(8,128)(2,1)}, bf16[2064,128]{1,0:T(8,128)(2,1)S(1)}, u32[]{:S(2)}, u32[]{:S(2)}) collective-permute-start(bf16[2064,128]{1,0:T(8,128)(2,1)} %get-tuple-element.16), channel_id=1, source_target_pairs={{0,16},{1,17},{2,18},{3,19},{4,20},{5,21},{6,22},{7,23},{8,24},{9,... | collective-permute-start | bytes 1585160 | tf_op jit(solution)/shard_map/ppermute | solution.py:244
  25.9 2.7 %collective-permute-start.4 = (bf16[2064,128]{1,0:T(8,128)(2,1)}, bf16[2064,128]{1,0:T(8,128)(2,1)S(1)}, u32[]{:S(2)}, u32[]{:S(2)}) collective-permute-start(bf16[2064,128]{1,0:T(8,128)(2,1)} %get-tuple-element.17), channel_id=1, source_target_pairs={{0,8},{1,9},{2,10},{3,11},{4,12},{5,13},{6,14},{7,15},{8,16},{9,17... | collective-permute-start | bytes 1585160 | tf_op jit(solution)/shard_map/ppermute | solution.py:244
  28.7 5.2 %collective-permute-start.5 = (bf16[2064,128]{1,0:T(8,128)(2,1)}, bf16[2064,128]{1,0:T(8,128)(2,1)}, u32[]{:S(2)}, u32[]{:S(2)}) collective-permute-start(bf16[2064,128]{1,0:T(8,128)(2,1)} %get-tuple-element.18), channel_id=1, source_target_pairs={{0,24},{1,25},{2,26},{3,27},{4,28},{5,29},{6,30},{7,31},{8,0},{9,1... | collective-permute-start | bytes 1585160 | tf_op jit(solution)/shard_map/ppermute | solution.py:244
  33.9 1.6 %copy.9 = s32[256,112]{1,0:T(8,128)} copy(s32[256,112]{0,1:T(8,128)} %param.6) | data formatting | bytes 229376 | tf_op args[2]
  35.6 1.1 add_convert_fusion
  36.7 0.6 pad.5.inverse
  37.3 12.8 %collective-permute-done.3.lhs2.q2 = bf16[2064,128]{1,0:T(8,128)(2,1)S(1)} collective-permute-done((bf16[2064,128]{1,0:T(8,128)(2,1)}, bf16[2064,128]{1,0:T(8,128)(2,1)S(1)}, u32[]{:S(2)}, u32[]{:S(2)}) %collective-permute-start.3) | collective-permute-done | bytes 528416 | tf_op jit(solution)/shard_map/ppermute | solution.py:244
  50.1 21.2 %collective-permute-done.4.lhs1.q1 = bf16[2064,128]{1,0:T(8,128)(2,1)S(1)} collective-permute-done((bf16[2064,128]{1,0:T(8,128)(2,1)}, bf16[2064,128]{1,0:T(8,128)(2,1)S(1)}, u32[]{:S(2)}, u32[]{:S(2)}) %collective-permute-start.4) | collective-permute-done | bytes 528416 | tf_op jit(solution)/shard_map/ppermute | solution.py:244
  71.3 1.4 %collective-permute-done.5.lhs3.q3 = bf16[2064,128]{1,0:T(8,128)(2,1)} collective-permute-done((bf16[2064,128]{1,0:T(8,128)(2,1)}, bf16[2064,128]{1,0:T(8,128)(2,1)}, u32[]{:S(2)}, u32[]{:S(2)}) %collective-permute-start.5) | collective-permute-done | bytes 528416 | tf_op jit(solution)/shard_map/ppermute | solution.py:244
  72.7 0.0 copy-done.3
  72.7 7.1 %shard_map.49 = s16[8,32,1792]{2,1,0:T(8,128)(2,1)} custom-call(s32[2]{0:T(128)} %pad_add_fusion.1.pos, bf16[256,128]{1,0:T(8,128)(2,1)} %pad.5.inverse, bf16[8,1168,128]{2,1,0:T(8,128)(2,1)} %shard_map.46.hz.own_lhs, bf16[2064,128]{1,0:T(8,128)(2,1)} %copy-done.2, bf16[2064,128]{1,0:T(8,128)(2,1)} %copy-done.3, ...), custom_call_target="tpu_custom_call" | custom-call | flops 469762048 | bytes 3000000 | tf_op jit(solution)/shard_map/pallas_call | solution.py:157
  79.9 0.0 all-to-all-done.lhs.parts
  79.9 0.0 copy-start
  79.9 7.0 %all-to-all-start.1 = ((s16[8,32,1792]{2,1,0:T(8,128)(2,1)}), s16[8,32,1792]{2,1,0:T(8,128)(2,1)S(1)}, u32[]{:S(2)}, u32[]{:S(2)}) async-start(s16[8,32,1792]{2,1,0:T(8,128)(2,1)} %shard_map.49), calls=%async_computation.1 | async-start | bytes 1835008 | tf_op jit(solution)/shard_map/all_to_all | solution.py:261
  86.9 0.7 dynamic-slice_bitcast_fusion
  87.6 0.7 fusion.2
  88.3 0.7 fusion.1
  88.9 0.7 fusion.3
  89.6 0.6 gather_fusion
  90.2 0.1 select_add_fusion.1
  90.3 0.1 broadcast_in_dim.353
  90.4 0.8 copy.16
  91.2 0.0 copy-done
  91.2 7.1 %shard_map.47 = (s16[64,896]{1,0:T(8,128)(2,1)}, s16[64,896]{1,0:T(8,128)(2,1)}, s16[64,896]{1,0:T(8,128)(2,1)}, s16[64,896]{1,0:T(8,128)(2,1)}) custom-call(s32[2]{0:T(128)} %pad_add_fusion.1.pos, bf16[256,128]{1,0:T(8,128)(2,1)} %pad.5.inverse, bf16[8,1168,128]{2,1,0:T(8,128)(2,1)} %copy-done, bf16[8,1168,128]{2,1,0:T(8,128)(2,1)} %copy-done), custom_call_target="tpu_custom_call" | custom-call | flops 469762048 | bytes 3000000 | tf_op jit(solution)/shard_map/pallas_call | solution.py:195
  98.3 4.6 %collective-permute-start = (s16[64,896]{1,0:T(8,128)(2,1)}, s16[64,896]{1,0:T(8,128)(2,1)S(1)}, u32[]{:S(2)}, u32[]{:S(2)}) collective-permute-start(s16[64,896]{1,0:T(8,128)(2,1)} %get-tuple-element.13), channel_id=1, source_target_pairs={{0,16},{1,17},{2,18},{3,19},{4,20},{5,21},{6,22},{7,23},{8,24},{9,... | collective-permute-start | bytes 344072 | tf_op jit(solution)/shard_map/ppermute | solution.py:263
  102.9 4.8 %collective-permute-start.1 = (s16[64,896]{1,0:T(8,128)(2,1)}, s16[64,896]{1,0:T(8,128)(2,1)S(1)}, u32[]{:S(2)}, u32[]{:S(2)}) collective-permute-start(s16[64,896]{1,0:T(8,128)(2,1)} %get-tuple-element.14), channel_id=1, source_target_pairs={{0,8},{1,9},{2,10},{3,11},{4,12},{5,13},{6,14},{7,15},{8,16},{9,17... | collective-permute-start | bytes 344072 | tf_op jit(solution)/shard_map/ppermute | solution.py:263
  107.7 3.1 %collective-permute-start.2 = (s16[64,896]{1,0:T(8,128)(2,1)}, s16[64,896]{1,0:T(8,128)(2,1)S(1)}, u32[]{:S(2)}, u32[]{:S(2)}) collective-permute-start(s16[64,896]{1,0:T(8,128)(2,1)} %get-tuple-element.15), channel_id=1, source_target_pairs={{0,24},{1,25},{2,26},{3,27},{4,28},{5,29},{6,30},{7,31},{8,0},{9,1... | collective-permute-start | bytes 344072 | tf_op jit(solution)/shard_map/ppermute | solution.py:263
  110.9 0.8 fusion
  111.7 0.1 select_add_fusion
  111.8 0.1 broadcast_in_dim.334
  111.9 0.7 copy.17
  112.7 0.3 all-to-all-done.1.sy
  113.0 0.0 collective-permute-done.s2
  113.0 1.3 collective-permute-done.1.s1
  114.3 3.2 %collective-permute-done.2.s3 = s16[64,896]{1,0:T(8,128)(2,1)S(1)} collective-permute-done((s16[64,896]{1,0:T(8,128)(2,1)}, s16[64,896]{1,0:T(8,128)(2,1)S(1)}, u32[]{:S(2)}, u32[]{:S(2)}) %collective-permute-start.2) | collective-permute-done | bytes 114720 | tf_op jit(solution)/shard_map/ppermute | solution.py:263
  117.5 0.6 copy-done.6
  118.2 2.5 %shard_map.50 = bf16[16,8,896]{2,1,0:T(8,128)(2,1)} custom-call(s16[64,896]{1,0:T(8,128)(2,1)} %get-tuple-element.12.own, s16[64,896]{1,0:T(8,128)(2,1)} %copy-done.4, s16[64,896]{1,0:T(8,128)(2,1)} %copy-done.5, s16[64,896]{1,0:T(8,128)(2,1)} %copy-done.6, s16[8,32,1792]{2,1,0:T(8,128)(2,1)} %copy-done.1, f32[64,896]{1,0:T(8,128)} %bitcast.43, ...), custom_call_target="tpu_custom_call" | custom-call | flops 4000000 | bytes 2500000 | tf_op jit(solution)/shard_map/pallas_call | solution.py:229
  120.7 4.8 %all-to-all-start.2 = ((bf16[16,8,896]{2,1,0:T(8,128)(2,1)}), bf16[16,8,896]{2,1,0:T(8,128)(2,1)S(1)}, u32[]{:S(2)}, u32[]{:S(2)}) async-start(bf16[16,8,896]{2,1,0:T(8,128)(2,1)} %shard_map.50), calls=%async_computation.2 | async-start | bytes 458752 | tf_op jit(solution)/shard_map/all_to_all | solution.py:266
  125.5 5.4 %all-to-all-done.2 = bf16[16,8,896]{2,1,0:T(8,128)(2,1)S(1)} async-done(((bf16[16,8,896]{2,1,0:T(8,128)(2,1)}), bf16[16,8,896]{2,1,0:T(8,128)(2,1)S(1)}, u32[]{:S(2)}, u32[]{:S(2)}) %all-to-all-start.2) | async-done | bytes 229408 | tf_op jit(solution)/shard_map/all_to_all | solution.py:266
  131.0 5.4 %collective-permute-start.6 = (f32[8,896]{1,0:T(8,128)S(1)}, f32[8,896]{1,0:T(8,128)S(1)}, u32[]{:S(2)}, u32[]{:S(2)}) collective-permute-start(f32[8,896]{1,0:T(8,128)S(1)} %convert_reduce_fusion), channel_id=1, source_target_pairs={{0,0},{1,32},{2,64},{3,96},{4,128},{5,160},{6,192},{7,224},{8,8},{... | collective-permute-start | bytes 86024 | tf_op jit(solution)/shard_map/ppermute | solution.py:268
  136.4 0.1 add_multiply_fusion
  136.5 0.1 copy.11
  136.6 5.0 %collective-permute-done.6 = f32[8,896]{1,0:T(8,128)S(1)} collective-permute-done((f32[8,896]{1,0:T(8,128)S(1)}, f32[8,896]{1,0:T(8,128)S(1)}, u32[]{:S(2)}, u32[]{:S(2)}) %collective-permute-start.6) | collective-permute-done | bytes 28704 | tf_op jit(solution)/shard_map/ppermute | solution.py:268
  141.5 0.7 bitcast_multiply_fusion
  (16 shorter events, 0.1 us)
Async XLA Ops:
  3.8 76.1 %all-to-all-start = ((bf16[8,1168,128]{2,1,0:T(8,128)(2,1)}), bf16[8,1168,128]{2,1,0:T(8,128)(2,1)S(1)}, u32[]{:S(2)}, u32[]{:S(2)}) async-start(bf16[8,1168,128]{2,1,0:T(8,128)(2,1)} %shard_map.46.hz.own_lhs), calls=%async_computation | async-start | bytes 4784128 | tf_op jit(solution)/shard_map/all_to_all | solution.py:243
  18.2 31.9 %collective-permute-start.3 = (bf16[2064,128]{1,0:T(8,128)(2,1)}, bf16[2064,128]{1,0:T(8,128)(2,1)S(1)}, u32[]{:S(2)}, u32[]{:S(2)}) collective-permute-start(bf16[2064,128]{1,0:T(8,128)(2,1)} %get-tuple-element.16), channel_id=1, source_target_pairs={{0,16},{1,17},{2,18},{3,19},{4,20},{5,21},{6,22},{7,23},{8,24},{9,... | collective-permute-start | bytes 1585160 | tf_op jit(solution)/shard_map/ppermute | solution.py:244
  25.9 45.3 %collective-permute-start.4 = (bf16[2064,128]{1,0:T(8,128)(2,1)}, bf16[2064,128]{1,0:T(8,128)(2,1)S(1)}, u32[]{:S(2)}, u32[]{:S(2)}) collective-permute-start(bf16[2064,128]{1,0:T(8,128)(2,1)} %get-tuple-element.17), channel_id=1, source_target_pairs={{0,8},{1,9},{2,10},{3,11},{4,12},{5,13},{6,14},{7,15},{8,16},{9,17... | collective-permute-start | bytes 1585160 | tf_op jit(solution)/shard_map/ppermute | solution.py:244
  28.7 44.1 %collective-permute-start.5 = (bf16[2064,128]{1,0:T(8,128)(2,1)}, bf16[2064,128]{1,0:T(8,128)(2,1)}, u32[]{:S(2)}, u32[]{:S(2)}) collective-permute-start(bf16[2064,128]{1,0:T(8,128)(2,1)} %get-tuple-element.18), channel_id=1, source_target_pairs={{0,24},{1,25},{2,26},{3,27},{4,28},{5,29},{6,30},{7,31},{8,0},{9,1... | collective-permute-start | bytes 1585160 | tf_op jit(solution)/shard_map/ppermute | solution.py:244
  37.3 52.3 %copy-start.7 = (s32[8,112]{1,0:T(8,128)S(1)}, s32[8,112]{1,0:T(8,128)}, u32[]{:S(2)}) copy-start(s32[8,112]{1,0:T(8,128)} %exps.1) | copy-start | bytes 10756
  50.1 22.6 %copy-start.2 = (bf16[2064,128]{1,0:T(8,128)(2,1)}, bf16[2064,128]{1,0:T(8,128)(2,1)S(1)}, u32[]{:S(2)}) copy-start(bf16[2064,128]{1,0:T(8,128)(2,1)S(1)} %collective-permute-done.3.lhs2.q2) | copy-start | bytes 1585156
  71.3 1.5 %copy-start.3 = (bf16[2064,128]{1,0:T(8,128)(2,1)}, bf16[2064,128]{1,0:T(8,128)(2,1)S(1)}, u32[]{:S(2)}) copy-start(bf16[2064,128]{1,0:T(8,128)(2,1)S(1)} %collective-permute-done.4.lhs1.q1) | copy-start | bytes 1585156
  79.9 11.3 %copy-start = (bf16[8,1168,128]{2,1,0:T(8,128)(2,1)}, bf16[8,1168,128]{2,1,0:T(8,128)(2,1)S(1)}, u32[]{:S(2)}) copy-start(bf16[8,1168,128]{2,1,0:T(8,128)(2,1)S(1)} %all-to-all-done.lhs.parts) | copy-start | bytes 7176196
  79.9 33.1 %all-to-all-start.1 = ((s16[8,32,1792]{2,1,0:T(8,128)(2,1)}), s16[8,32,1792]{2,1,0:T(8,128)(2,1)S(1)}, u32[]{:S(2)}, u32[]{:S(2)}) async-start(s16[8,32,1792]{2,1,0:T(8,128)(2,1)} %shard_map.49), calls=%async_computation.1 | async-start | bytes 1835008 | tf_op jit(solution)/shard_map/all_to_all | solution.py:261
  98.3 14.7 %collective-permute-start = (s16[64,896]{1,0:T(8,128)(2,1)}, s16[64,896]{1,0:T(8,128)(2,1)S(1)}, u32[]{:S(2)}, u32[]{:S(2)}) collective-permute-start(s16[64,896]{1,0:T(8,128)(2,1)} %get-tuple-element.13), channel_id=1, source_target_pairs={{0,16},{1,17},{2,18},{3,19},{4,20},{5,21},{6,22},{7,23},{8,24},{9,... | collective-permute-start | bytes 344072 | tf_op jit(solution)/shard_map/ppermute | solution.py:263
  102.9 11.4 %collective-permute-start.1 = (s16[64,896]{1,0:T(8,128)(2,1)}, s16[64,896]{1,0:T(8,128)(2,1)S(1)}, u32[]{:S(2)}, u32[]{:S(2)}) collective-permute-start(s16[64,896]{1,0:T(8,128)(2,1)} %get-tuple-element.14), channel_id=1, source_target_pairs={{0,8},{1,9},{2,10},{3,11},{4,12},{5,13},{6,14},{7,15},{8,16},{9,17... | collective-permute-start | bytes 344072 | tf_op jit(solution)/shard_map/ppermute | solution.py:263
  107.7 9.8 %collective-permute-start.2 = (s16[64,896]{1,0:T(8,128)(2,1)}, s16[64,896]{1,0:T(8,128)(2,1)S(1)}, u32[]{:S(2)}, u32[]{:S(2)}) collective-permute-start(s16[64,896]{1,0:T(8,128)(2,1)} %get-tuple-element.15), channel_id=1, source_target_pairs={{0,24},{1,25},{2,26},{3,27},{4,28},{5,29},{6,30},{7,31},{8,0},{9,1... | collective-permute-start | bytes 344072 | tf_op jit(solution)/shard_map/ppermute | solution.py:263
  113.0 4.6 %copy-start.1 = (s16[8,32,1792]{2,1,0:T(8,128)(2,1)}, s16[8,32,1792]{2,1,0:T(8,128)(2,1)S(1)}, u32[]{:S(2)}) copy-start(s16[8,32,1792]{2,1,0:T(8,128)(2,1)S(1)} %all-to-all-done.1.sy) | copy-start | bytes 2752516
  113.0 4.6 %copy-start.4 = (s16[64,896]{1,0:T(8,128)(2,1)}, s16[64,896]{1,0:T(8,128)(2,1)S(1)}, u32[]{:S(2)}) copy-start(s16[64,896]{1,0:T(8,128)(2,1)S(1)} %collective-permute-done.s2) | copy-start | bytes 344068
  114.3 3.2 %copy-start.5 = (s16[64,896]{1,0:T(8,128)(2,1)}, s16[64,896]{1,0:T(8,128)(2,1)S(1)}, u32[]{:S(2)}) copy-start(s16[64,896]{1,0:T(8,128)(2,1)S(1)} %collective-permute-done.1.s1) | copy-start | bytes 344068
  117.5 0.7 copy-start.6
  120.7 10.2 %all-to-all-start.2 = ((bf16[16,8,896]{2,1,0:T(8,128)(2,1)}), bf16[16,8,896]{2,1,0:T(8,128)(2,1)S(1)}, u32[]{:S(2)}, u32[]{:S(2)}) async-start(bf16[16,8,896]{2,1,0:T(8,128)(2,1)} %shard_map.50), calls=%async_computation.2 | async-start | bytes 458752 | tf_op jit(solution)/shard_map/all_to_all | solution.py:266
  131.0 10.6 %collective-permute-start.6 = (f32[8,896]{1,0:T(8,128)S(1)}, f32[8,896]{1,0:T(8,128)S(1)}, u32[]{:S(2)}, u32[]{:S(2)}) collective-permute-start(f32[8,896]{1,0:T(8,128)S(1)} %convert_reduce_fusion), channel_id=1, source_target_pairs={{0,0},{1,32},{2,64},{3,96},{4,128},{5,160},{6,192},{7,224},{8,8},{... | collective-permute-start | bytes 86024 | tf_op jit(solution)/shard_map/ppermute | solution.py:268

commit v3 on v2

v3 whole, which is shorter than its diff:
```python
import jax
import jax.numpy as jnp
from jax import lax
from jax.experimental import pallas as pl
from jax.experimental.pallas import tpu as pltpu
from jax.sharding import PartitionSpec as P

BLK = 128
NY = 4
NZ = 8
NG = 16
NM = NY * NZ
HALF = 7168
CZ = HALF // NZ
CY = HALF // NY
OFFS = (2, 1, -1)
MAGIC = 12582912.0
Z_GROUPS = [[y * NZ + z for z in range(NZ)] for y in range(NY)]


def y_shift(step):
    return [(y * NZ + z, ((y + step) % NY) * NZ + z) for y in range(NY) for z in range(NZ)]


def last_moves():
    moves = []
    for group in range(NG):
        for y in range(NY):
            for z in range(NZ):
                if group < 8:
                    target = z * NM + y * NZ + group
                else:
                    target = (8 + 2 * y + group % 2) * NM + ((group - 8) // 2) * NZ + z
                moves.append((group * NM + y * NZ + z, target))
    return moves


def power_two(expo):
    total = jnp.zeros(expo.shape, jnp.float32)
    for power in range(-8, 9):
        total = total + jnp.where(expo == power, jnp.float32(2.0**power), jnp.float32(0.0))
    return total


def round_clip(values):
    return (jnp.clip(values, -127.0, 127.0) + MAGIC) - MAGIC


def pack_z_kernel(acts, exps, cot, out, held, padded, into, outof):
    loads = []
    for j in range(NZ):
        for b in range(CZ // BLK):
            column = j * CZ + b * BLK
            rows = pl.ds(256 + b * BLK, BLK)
            loads.append(
                pltpu.make_async_copy(cot.at[:, column : column + BLK], held.at[j, rows, :], into.at[len(loads)])
            )
    for load in loads:
        load.start()
    turned = acts[...].T
    padded[...] = jnp.zeros((16, BLK), jnp.float32)
    padded[0:8, 0 : exps.shape[1]] = exps[...].astype(jnp.float32)
    tail = padded[...].astype(jnp.bfloat16)
    for j in range(NZ):
        held[j, 0:256, :] = turned
        held[j, 256 + CZ : 256 + CZ + 16, :] = tail
    stores = [pltpu.make_async_copy(held.at[j], out.at[j], outof.at[j]) for j in range(NZ)]
    for j in range(NZ):
        for b in range(CZ // BLK):
            loads[j * (CZ // BLK) + b].wait()
        stores[j].start()
    for store in stores:
        store.wait()


def pack_z(acts, exps, cot):
    shape = (NZ, 256 + CZ + 16, BLK)
    any_spec = pl.BlockSpec(memory_space=pl.ANY)
    vmem_spec = pl.BlockSpec(memory_space=pltpu.VMEM)
    return pl.pallas_call(
        pack_z_kernel,
        out_shape=jax.ShapeDtypeStruct(shape, jnp.bfloat16),
        in_specs=[vmem_spec, vmem_spec, any_spec],
        out_specs=any_spec,
        scratch_shapes=[
            pltpu.VMEM(shape, jnp.bfloat16),
            pltpu.VMEM((16, BLK), jnp.float32),
            pltpu.SemaphoreType.DMA((HALF // BLK,)),
            pltpu.SemaphoreType.DMA((NZ,)),
        ],
        cost_estimate=pl.CostEstimate(flops=0, bytes_accessed=4000000, transcendentals=0),
    )(acts, exps, cot)


def pack_y_kernel(hz, cot, p2, p1, p3, held, into, outof):
    y = lax.axis_index("intra") // NZ
    loads, stores = [], []
    per = CY // BLK + 2
    for i, (step, out) in enumerate(zip(OFFS, (p2, p1, p3))):
        start = HALF + CY * lax.rem(y + step + NY, NY)
        moves = [(hz.at[0, 0:256], held.at[i, 0:256]), (hz.at[0, pl.ds(256 + CZ, 16)], held.at[i, pl.ds(256 + CY, 16)])]
        for b in range(CY // BLK):
            column = pl.multiple_of(start + b * BLK, BLK)
            moves.append((cot.at[:, pl.ds(column, BLK)], held.at[i, pl.ds(256 + b * BLK, BLK), :]))
        loads += [pltpu.make_async_copy(src, dst, into.at[i * per + k]) for k, (src, dst) in enumerate(moves)]
        stores.append(pltpu.make_async_copy(held.at[i], out, outof.at[i]))
    for load in loads:
        load.start()
    for i in range(3):
        for k in range(per):
            loads[i * per + k].wait()
        stores[i].start()
    for store in stores:
        store.wait()


def pack_y(hz, cot):
    any_spec = pl.BlockSpec(memory_space=pl.ANY)
    piece = jax.ShapeDtypeStruct((256 + CY + 16, BLK), jnp.bfloat16)
    return pl.pallas_call(
        pack_y_kernel,
        out_shape=[piece, piece, piece],
        in_specs=[any_spec, any_spec],
        out_specs=[any_spec] * 3,
        scratch_shapes=[
            pltpu.VMEM((3, 256 + CY + 16, BLK), jnp.bfloat16),
            pltpu.SemaphoreType.DMA((3 * (CY // BLK + 2),)),
            pltpu.SemaphoreType.DMA((3,)),
        ],
        cost_estimate=pl.CostEstimate(flops=0, bytes_accessed=3000000, transcendentals=0),
    )(hz, cot)


def spread(inverse, first_block, width):
    block = lax.broadcasted_iota(jnp.int32, (BLK, width), 0)
    column = lax.broadcasted_iota(jnp.int32, (BLK, width), 1)
    pick = jnp.where(block == first_block + column // BLK, 1.0, 0.0).astype(jnp.bfloat16)
    return jnp.dot(inverse, pick, preferred_element_type=jnp.float32)


def sum_y_kernel(pos, inverse, hz, cot, q2, q1, q3, out, lhs, own, sems):
    start = HALF + CY * pos[0]
    loads = [
        pltpu.make_async_copy(hz.at[0, 0:256], lhs, sems.at[0]),
        pltpu.make_async_copy(cot.at[:, pl.ds(pl.multiple_of(start, CY), CY)], own, sems.at[1]),
    ]
    for load in loads:
        load.start()
    for load in loads:
        load.wait()
    for i in range(CY // 256):
        scale = spread(inverse[...], HALF // BLK + pos[0] * (CY // BLK) + 2 * i, 256)
        local = jnp.dot(lhs[...], own[:, 256 * i : 256 * i + 256], preferred_element_type=jnp.float32)
        total = round_clip(local * scale)
        for part in (q2, q1, q3):
            row = 256 + 256 * i
            both = jnp.concatenate([part[row : row + BLK], part[row + BLK : row + 2 * BLK]], axis=1)
            local = jnp.dot(part[0:256], both, preferred_element_type=jnp.float32)
            total = total + round_clip(local * scale)
        for z in range(NZ):
            rows = [total[64 * y + 8 * z : 64 * y + 8 * z + 8] for y in range(NY)]
            out[z, :, 256 * i : 256 * i + 256] = jnp.concatenate(rows, axis=0).astype(jnp.int16)


def sum_y(pos, inverse, hz, cot, q2, q1, q3):
    any_spec = pl.BlockSpec(memory_space=pl.ANY)
    vmem_spec = pl.BlockSpec(memory_space=pltpu.VMEM)
    return pl.pallas_call(
        sum_y_kernel,
        out_shape=jax.ShapeDtypeStruct((NZ, 32, CY), jnp.int16),
        in_specs=[pl.BlockSpec(memory_space=pltpu.SMEM), vmem_spec, any_spec, any_spec] + [vmem_spec] * 3,
        out_specs=vmem_spec,
        scratch_shapes=[
            pltpu.VMEM((256, BLK), jnp.bfloat16),
            pltpu.VMEM((128, CY), jnp.bfloat16),
            pltpu.SemaphoreType.DMA((2,)),
        ],
        cost_estimate=pl.CostEstimate(flops=2 * 4 * 256 * 128 * CY, bytes_accessed=3000000, transcendentals=0),
    )(pos, inverse, hz, cot, q2, q1, q3)


def sum_z_kernel(pos, inverse, parts, own, s2, s1, s3, held, total_ref, sems):
    loads = [pltpu.make_async_copy(parts.at[:, 0:256], held.at[:, 0:256], sems.at[0])]
    for b in range(CZ // BLK):
        rows = pl.ds(256 + b * BLK, BLK)
        loads.append(pltpu.make_async_copy(parts.at[:, rows], held.at[:, rows], sems.at[1 + b]))
    for load in loads:
        load.start()
    loads[0].wait()
    for b in range(CZ // BLK):
        loads[1 + b].wait()
        scale = spread(inverse[...], pos[1] * (CZ // BLK) + b, BLK)
        for h in range(2):
            total = jnp.zeros((BLK, BLK), jnp.float32)
            for r in range(NZ):
                local = jnp.dot(
                    held[r, h * BLK : h * BLK + BLK],
                    held[r, 256 + b * BLK : 256 + b * BLK + BLK],
                    preferred_element_type=jnp.float32,
                )
                total = total + round_clip(local * scale[h * BLK : h * BLK + BLK])
            total_ref[h * BLK : h * BLK + BLK, b * BLK : b * BLK + BLK] = total
    for step, out in zip((0,) + OFFS, (own, s2, s1, s3)):
        start = 64 * lax.rem(pos[0] + step + NY, NY)
        out[...] = total_ref[pl.ds(pl.multiple_of(start, 64), 64), :].astype(jnp.int16)


def sum_z(pos, inverse, parts):
    vmem_spec = pl.BlockSpec(memory_space=pltpu.VMEM)
    return pl.pallas_call(
        sum_z_kernel,
        out_shape=[jax.ShapeDtypeStruct((64, CZ), jnp.int16)] * 4,
        in_specs=[pl.BlockSpec(memory_space=pltpu.SMEM), vmem_spec, pl.BlockSpec(memory_space=pl.ANY)],
        out_specs=[vmem_spec] * 4,
        scratch_shapes=[
            pltpu.VMEM((NZ, 256 + CZ, BLK), jnp.bfloat16),
            pltpu.VMEM((256, CZ), jnp.float32),
            pltpu.SemaphoreType.DMA((1 + CZ // BLK,)),
        ],
        cost_estimate=pl.CostEstimate(flops=2 * 8 * 256 * 128 * CZ, bytes_accessed=3000000, transcendentals=0),
    )(pos, inverse, parts)


def second_kernel(pos, first, second, rz, q2, q1, q3, own, s2, s1, s3, sy, out, tail_z, tail_y, diff, sems):
    y, z = pos[0], pos[1]
    loads = [pltpu.make_async_copy(rz.at[:, pl.ds(256 + CZ, 16)], tail_z, sems.at[0])]
    for i, part in enumerate((q3, q2, q1)):
        loads.append(pltpu.make_async_copy(part.at[pl.ds(256 + CY, 16)], tail_y.at[i], sems.at[1 + i]))
    for load in loads:
        load.start()
    for load in loads:
        load.wait()

    for r in range(NZ):
        rows = pl.ds(pl.multiple_of(64 * y + 8 * r, 8), 8)
        diff[8 * r : 8 * r + 8] = first[rows].astype(jnp.float32) - tail_z[r].astype(jnp.float32)[0:8]
    scale = spread(power_two(diff[...]).astype(jnp.bfloat16), z * (CZ // BLK), CZ)
    total = own[...].astype(jnp.int32)
    for part in (s2, s1, s3):
        total = total + part[...].astype(jnp.int32)
    codes = round_clip(total.astype(jnp.float32) * scale)
    for k in range(8):
        out[k] = codes[8 * k : 8 * k + 8].astype(jnp.bfloat16)

    for step in range(NY):
        member = lax.rem(y + step, NY)
        expo = second[...].astype(jnp.float32) if step == 0 else tail_y[step - 1].astype(jnp.float32)[0:8]
        rows = pl.ds(pl.multiple_of(64 * member + 8 * z, 8), 8)
        diff[pl.ds(pl.multiple_of(8 * member, 8), 8)] = first[rows].astype(jnp.float32) - expo
    factor = power_two(diff[0:32]).astype(jnp.bfloat16)
    for c in range(2):
        scale = spread(factor, HALF // BLK + y * (CY // BLK) + c * (CZ // BLK), CZ)
        total = sy[0, :, c * CZ : c * CZ + CZ].astype(jnp.int32)
        for r in range(1, NZ):
            total = total + sy[r, :, c * CZ : c * CZ + CZ].astype(jnp.int32)
        codes = round_clip(total.astype(jnp.float32) * scale)
        for k in range(NY):
            out[8 + 2 * k + c] = codes[8 * k : 8 * k + 8].astype(jnp.bfloat16)


def second_codes(pos, first, second, rz, q2, q1, q3, own, s2, s1, s3, sy):
    any_spec = pl.BlockSpec(memory_space=pl.ANY)
    vmem_spec = pl.BlockSpec(memory_space=pltpu.VMEM)
    return pl.pallas_call(
        second_kernel,
        out_shape=jax.ShapeDtypeStruct((NG, 8, CZ), jnp.bfloat16),
        in_specs=[pl.BlockSpec(memory_space=pltpu.SMEM), vmem_spec, vmem_spec] + [any_spec] * 4 + [vmem_spec] * 5,
        out_specs=vmem_spec,
        scratch_shapes=[
            pltpu.VMEM((NZ, 16, BLK), jnp.bfloat16),
            pltpu.VMEM((3, 16, BLK), jnp.bfloat16),
            pltpu.VMEM((64, BLK), jnp.float32),
            pltpu.SemaphoreType.DMA((4,)),
        ],
        cost_estimate=pl.CostEstimate(flops=4000000, bytes_accessed=2500000, transcendentals=0),
    )(pos, first, second, rz, q2, q1, q3, own, s2, s1, s3, sy)


def body(acts, cotangent, first_exp, second_exp):
    member = lax.axis_index("intra")
    group = lax.axis_index("inter")
    y, z = member // NZ, member % NZ
    pos = jnp.stack([y, z]).astype(jnp.int32)

    hz = pack_z(acts, second_exp, cotangent)
    rz = lax.all_to_all(hz, "intra", 0, 0, axis_index_groups=Z_GROUPS, tiled=True)
    q2, q1, q3 = [lax.ppermute(p, "intra", y_shift(step)) for step, p in zip(OFFS, pack_y(hz, cotangent))]
    room = ((0, 0), (0, BLK - first_exp.shape[1]))
    first, second = jnp.pad(first_exp, room), jnp.pad(second_exp, room)
    inverse = power_two(-first).astype(jnp.bfloat16)

    sy = sum_y(pos, inverse, hz, cotangent, q2, q1, q3)
    ry = lax.all_to_all(sy, "intra", 0, 0, axis_index_groups=Z_GROUPS, tiled=True)
    own, s2, s1, s3 = sum_z(pos, inverse, rz)
    t2, t1, t3 = [lax.ppermute(s, "intra", y_shift(step)) for step, s in zip(OFFS, (s2, s1, s3))]
    codes = second_codes(pos, first, second, rz, q2, q1, q3, own, t2, t1, t3, ry)

    received = lax.all_to_all(codes, "inter", 0, 0, tiled=True)
    total = jnp.sum(received, axis=0, dtype=jnp.float32)
    rows = lax.ppermute(total, ("inter", "intra"), last_moves())
    my_exp = lax.dynamic_slice_in_dim(second_exp, group * (CZ // BLK), CZ // BLK, 1)
    return rows * (jnp.repeat(power_two(my_exp), BLK, axis=1) * (1.0 / (NG * NM)))


def solution(mesh):
    return jax.shard_map(
        body,
        mesh=mesh,
        in_specs=(P(("inter", "intra"), None), P(("inter", "intra"), None), P(), P("intra", None)),
        out_specs=P("intra", "inter"),
        check_vma=False,
    )
```

time: 145 us -> 138 us (0.952); the launches traced: 142 us -> 137 us
  Pallas kernels: 24 us -> 20.3 us
  other arithmetic: 5.6 us -> 3.2 us
  local copies, waits for them, and re-layouts: 6.06 us -> 4.07 us
  starting transfers between devices: 55.7 us -> 57.5 us
    all_to_all x1, waiting for transfers between devices: 0.29 us -> 6.8 us  [body(): lax.all_to_all(sy, 'intra', 0, 0, axis_index_groups=Z_GROUPS, tiled=True)]
    ppermute x3, waiting for transfers between devices: 4.55 us -> 0.01 us  [body(): lax.ppermute(s, 'intra', y_shift(step))]
    another operation x5 -> x0, other arithmetic: 3.14 us -> none  [the longest x4 2 us: body(): jnp.stack([second_exp] + [q[256 + CY:264 + CY, :count].astype(jnp.int32)...]
    pallas_call x1, Pallas kernels: 7.13 us -> 5.11 us  [sum_y(): pl.pallas_call(sum_y_kernel, out_shape=jax.ShapeDtypeStruct((NZ, 32, CY),...]
    pallas_call x1, Pallas kernels: 7.09 us -> 5.3 us  [sum_z(): pl.pallas_call(sum_z_kernel, out_shape=[jax.ShapeDtypeStruct((64, CZ), jn...]
    convert_element_type x0 -> x1, other arithmetic: none -> 1.77 us  [body(): inverse = power_two(-first).astype(jnp.bfloat16)]
  transfers between devices with their start and end apart: 10 -> 10, of which waited for: 8 -> 6; matrix products, arithmetic and copies ran while one was open for 7% -> 4% of each run, Pallas kernels for 12% -> 10%
where the time goes in v3:
time: 138 us; the launch traced here: 137 us
  starting transfers between devices  57.5 us (42%)
  waiting for transfers between devices  51.5 us (37%)
  Pallas kernels  20.3 us (15%)
  local copies, waits for them, and re-layouts  4.07 us (3%)
  other arithmetic  3.2 us (2%)
    ppermute x3, waiting for transfers between devices, body(): lax.ppermute(p, 'intra', y_shift(step))  34.7 us
    ppermute x3, starting transfers between devices, body(): lax.ppermute(p, 'intra', y_shift(step))  15.8 us
    ppermute x3, starting transfers between devices, body(): lax.ppermute(s, 'intra', y_shift(step))  12.7 us
    all_to_all x1, starting transfers between devices, body(): lax.all_to_all(hz, 'intra', 0, 0, axis_index_groups=Z_GROUPS, tiled=True)  10.3 us
    all_to_all x1, starting transfers between devices, body(): lax.all_to_all(sy, 'intra', 0, 0, axis_index_groups=Z_GROUPS, tiled=True)  7.07 us
    all_to_all x1, waiting for transfers between devices, body(): lax.all_to_all(sy, 'intra', 0, 0, axis_index_groups=Z_GROUPS, tiled=True)  6.8 us
    ppermute x1, starting transfers between devices, body(): rows = lax.ppermute(total, ('inter', 'intra'), last_moves())  5.8 us
    all_to_all x1, starting transfers between devices, body(): received = lax.all_to_all(codes, 'inter', 0, 0, tiled=True)  5.78 us
  transfers between devices with their start and end apart: 10, of which 6 were waited for; matrix products, arithmetic and copies ran while one was open for 4% of the time, Pallas kernels for 10%

profile of v3, /device:TPU:6, one launch (start us, length us, event | category | flops | bytes accessed | tf_op | source)
XLA Modules:
  0.0 136.7 jit_solution(11407158994006257596)
XLA Ops:
  0.0 3.8 %shard_map.46.hz = bf16[8,1168,128]{2,1,0:T(8,128)(2,1)} custom-call(bf16[128,256]{1,0:T(8,128)(2,1)} %acts.1, s32[8,112]{1,0:T(8,128)} %exps.1, bf16[128,14336]{1,0:T(8,128)(2,1)} %cot.5), custom_call_target="tpu_custom_call" | custom-call | bytes 4000000 | tf_op jit(solution)/shard_map/pallas_call | solution.py:80
  3.8 10.3 %all-to-all-start = ((bf16[8,1168,128]{2,1,0:T(8,128)(2,1)}), bf16[8,1168,128]{2,1,0:T(8,128)(2,1)S(1)}, u32[]{:S(2)}, u32[]{:S(2)}) async-start(bf16[8,1168,128]{2,1,0:T(8,128)(2,1)} %shard_map.46.hz), calls=%async_computation | async-start | bytes 4784128 | tf_op jit(solution)/shard_map/all_to_all | solution.py:286
  14.1 2.7 %shard_map.47 = (bf16[2064,128]{1,0:T(8,128)(2,1)}, bf16[2064,128]{1,0:T(8,128)(2,1)}, bf16[2064,128]{1,0:T(8,128)(2,1)}) custom-call(bf16[8,1168,128]{2,1,0:T(8,128)(2,1)} %shard_map.46.hz, bf16[128,14336]{1,0:T(8,128)(2,1)} %cot.5), custom_call_target="tpu_custom_call" | custom-call | bytes 3000000 | tf_op jit(solution)/shard_map/pallas_call | solution.py:120
  16.8 7.9 %collective-permute-start = (bf16[2064,128]{1,0:T(8,128)(2,1)}, bf16[2064,128]{1,0:T(8,128)(2,1)S(1)}, u32[]{:S(2)}, u32[]{:S(2)}) collective-permute-start(bf16[2064,128]{1,0:T(8,128)(2,1)} %get-tuple-element.12), channel_id=1, source_target_pairs={{0,16},{1,17},{2,18},{3,19},{4,20},{5,21},{6,22},{7,23},{8,24},{9,... | collective-permute-start | bytes 1585160 | tf_op jit(solution)/shard_map/ppermute | solution.py:287
  24.7 2.6 %collective-permute-start.1 = (bf16[2064,128]{1,0:T(8,128)(2,1)}, bf16[2064,128]{1,0:T(8,128)(2,1)S(1)}, u32[]{:S(2)}, u32[]{:S(2)}) collective-permute-start(bf16[2064,128]{1,0:T(8,128)(2,1)} %get-tuple-element.13), channel_id=1, source_target_pairs={{0,8},{1,9},{2,10},{3,11},{4,12},{5,13},{6,14},{7,15},{8,16},{9,17... | collective-permute-start | bytes 1585160 | tf_op jit(solution)/shard_map/ppermute | solution.py:287
  27.3 5.3 %collective-permute-start.2 = (bf16[2064,128]{1,0:T(8,128)(2,1)}, bf16[2064,128]{1,0:T(8,128)(2,1)}, u32[]{:S(2)}, u32[]{:S(2)}) collective-permute-start(bf16[2064,128]{1,0:T(8,128)(2,1)} %get-tuple-element.14), channel_id=1, source_target_pairs={{0,24},{1,25},{2,26},{3,27},{4,28},{5,29},{6,30},{7,31},{8,0},{9,1... | collective-permute-start | bytes 1585160 | tf_op jit(solution)/shard_map/ppermute | solution.py:287
  32.6 1.6 %copy.5 = s32[256,112]{1,0:T(8,128)} copy(s32[256,112]{0,1:T(8,128)} %param.6) | data formatting | bytes 229376 | tf_op args[2]
  34.3 0.6 pad_add_fusion.pos
  34.9 1.8 %add_convert_fusion.inverse = bf16[256,128]{1,0:T(8,128)(2,1)} fusion(s32[256,112]{1,0:T(8,128)} %copy.5), kind=kLoop, calls=%fused_computation.1 | loop fusion | flops 1703936 | bytes 180224 | tf_op jit(solution)/shard_map/convert_element_type | solution.py:290
  36.7 12.1 %collective-permute-done.q2 = bf16[2064,128]{1,0:T(8,128)(2,1)S(1)} collective-permute-done((bf16[2064,128]{1,0:T(8,128)(2,1)}, bf16[2064,128]{1,0:T(8,128)(2,1)S(1)}, u32[]{:S(2)}, u32[]{:S(2)}) %collective-permute-start) | collective-permute-done | bytes 528416 | tf_op jit(solution)/shard_map/ppermute | solution.py:287
  48.8 0.0 copy-start.2
  48.8 21.2 %collective-permute-done.1.q1 = bf16[2064,128]{1,0:T(8,128)(2,1)S(1)} collective-permute-done((bf16[2064,128]{1,0:T(8,128)(2,1)}, bf16[2064,128]{1,0:T(8,128)(2,1)S(1)}, u32[]{:S(2)}, u32[]{:S(2)}) %collective-permute-start.1) | collective-permute-done | bytes 528416 | tf_op jit(solution)/shard_map/ppermute | solution.py:287
  70.0 1.4 collective-permute-done.2.q3
  71.4 0.0 copy-done.2
  71.4 0.0 copy-done.3
  71.4 5.1 %shard_map.49 = s16[8,32,1792]{2,1,0:T(8,128)(2,1)} custom-call(s32[2]{0:T(128)} %pad_add_fusion.pos, bf16[256,128]{1,0:T(8,128)(2,1)} %add_convert_fusion.inverse, bf16[8,1168,128]{2,1,0:T(8,128)(2,1)} %shard_map.46.hz, bf16[128,14336]{1,0:T(8,128)(2,1)} %cot.5, bf16[2064,128]{1,0:T(8,128)(2,1)} %copy-done.2, bf16[2064,128]{1,0:T(8,128)(2,1)} %copy-done.3, ...), custom_call_target="tpu_custom_call" | custom-call | flops 469762048 | bytes 3000000 | tf_op jit(solution)/shard_map/pallas_call | solution.py:168
  76.5 0.0 copy-start.4
  76.5 0.0 copy-start.8
  76.5 0.0 all-to-all-done.parts.rz
  76.5 0.0 copy-start
  76.5 7.1 %all-to-all-start.1 = ((s16[8,32,1792]{2,1,0:T(8,128)(2,1)}), s16[8,32,1792]{2,1,0:T(8,128)(2,1)S(1)}, u32[]{:S(2)}, u32[]{:S(2)}) async-start(s16[8,32,1792]{2,1,0:T(8,128)(2,1)} %shard_map.49), calls=%async_computation.1 | async-start | bytes 1835008 | tf_op jit(solution)/shard_map/all_to_all | solution.py:293
  83.6 0.0 copy-done
  83.6 5.3 %shard_map.48 = (s16[64,896]{1,0:T(8,128)(2,1)}, s16[64,896]{1,0:T(8,128)(2,1)}, s16[64,896]{1,0:T(8,128)(2,1)}, s16[64,896]{1,0:T(8,128)(2,1)}) custom-call(s32[2]{0:T(128)} %pad_add_fusion.pos, bf16[256,128]{1,0:T(8,128)(2,1)} %add_convert_fusion.inverse, bf16[8,1168,128]{2,1,0:T(8,128)(2,1)} %copy-done), custom_call_target="tpu_custom_call" | custom-call | flops 469762048 | bytes 3000000 | tf_op jit(solution)/shard_map/pallas_call | solution.py:210
  88.9 4.7 %collective-permute-start.3 = (s16[64,896]{1,0:T(8,128)(2,1)}, s16[64,896]{1,0:T(8,128)(2,1)S(1)}, u32[]{:S(2)}, u32[]{:S(2)}) collective-permute-start(s16[64,896]{1,0:T(8,128)(2,1)} %get-tuple-element.16), channel_id=1, source_target_pairs={{0,16},{1,17},{2,18},{3,19},{4,20},{5,21},{6,22},{7,23},{8,24},{9,... | collective-permute-start | bytes 344072 | tf_op jit(solution)/shard_map/ppermute | solution.py:295
  93.6 4.8 %collective-permute-start.4 = (s16[64,896]{1,0:T(8,128)(2,1)}, s16[64,896]{1,0:T(8,128)(2,1)S(1)}, u32[]{:S(2)}, u32[]{:S(2)}) collective-permute-start(s16[64,896]{1,0:T(8,128)(2,1)} %get-tuple-element.17), channel_id=1, source_target_pairs={{0,8},{1,9},{2,10},{3,11},{4,12},{5,13},{6,14},{7,15},{8,16},{9,17... | collective-permute-start | bytes 344072 | tf_op jit(solution)/shard_map/ppermute | solution.py:295
  98.5 3.1 %collective-permute-start.5 = (s16[64,896]{1,0:T(8,128)(2,1)}, s16[64,896]{1,0:T(8,128)(2,1)S(1)}, u32[]{:S(2)}, u32[]{:S(2)}) collective-permute-start(s16[64,896]{1,0:T(8,128)(2,1)} %get-tuple-element.18), channel_id=1, source_target_pairs={{0,24},{1,25},{2,26},{3,27},{4,28},{5,29},{6,30},{7,31},{8,0},{9,1... | collective-permute-start | bytes 344072 | tf_op jit(solution)/shard_map/ppermute | solution.py:295
  101.6 0.0 copy-done.4
  101.6 0.7 pad.8.first
  102.3 0.0 copy-done.8
  102.3 0.6 pad.9.second
  102.9 6.8 %all-to-all-done.1.sy = s16[8,32,1792]{2,1,0:T(8,128)(2,1)S(1)} async-done(((s16[8,32,1792]{2,1,0:T(8,128)(2,1)}), s16[8,32,1792]{2,1,0:T(8,128)(2,1)S(1)}, u32[]{:S(2)}, u32[]{:S(2)}) %all-to-all-start.1) | async-done | bytes 917536 | tf_op jit(solution)/shard_map/all_to_all | solution.py:293
  109.7 0.0 collective-permute-done.3.s2
  109.7 0.0 collective-permute-done.4.s1
  109.7 0.0 copy-start.6
  109.7 0.0 collective-permute-done.5.s3
  109.7 0.0 copy-start.7
  109.8 0.9 copy-done.1
  110.7 0.0 copy-done.5
  110.7 0.1 copy-done.6
  110.8 0.0 copy-done.7
  110.8 3.5 %shard_map.50 = bf16[16,8,896]{2,1,0:T(8,128)(2,1)} custom-call(s32[2]{0:T(128)} %pad_add_fusion.pos, s32[256,128]{1,0:T(8,128)} %pad.8.first, s32[8,128]{1,0:T(8,128)} %pad.9.second, bf16[8,1168,128]{2,1,0:T(8,128)(2,1)} %copy-done, bf16[2064,128]{1,0:T(8,128)(2,1)} %copy-done.2, bf16[2064,128]{1,0:T(8,128)(2,1)} %copy-done.3, ...), custom_call_target="tpu_custom_call" | custom-call | flops 4000000 | bytes 2500000 | tf_op jit(solution)/shard_map/pallas_call | solution.py:264
  114.3 5.8 %all-to-all-start.2 = ((bf16[16,8,896]{2,1,0:T(8,128)(2,1)}), bf16[16,8,896]{2,1,0:T(8,128)(2,1)S(1)}, u32[]{:S(2)}, u32[]{:S(2)}) async-start(bf16[16,8,896]{2,1,0:T(8,128)(2,1)} %shard_map.50), calls=%async_computation.2 | async-start | bytes 458752 | tf_op jit(solution)/shard_map/all_to_all | solution.py:298
  120.0 5.4 %all-to-all-done.2 = bf16[16,8,896]{2,1,0:T(8,128)(2,1)S(1)} async-done(((bf16[16,8,896]{2,1,0:T(8,128)(2,1)}), bf16[16,8,896]{2,1,0:T(8,128)(2,1)S(1)}, u32[]{:S(2)}, u32[]{:S(2)}) %all-to-all-start.2) | async-done | bytes 229408 | tf_op jit(solution)/shard_map/all_to_all | solution.py:298
  125.5 5.8 %collective-permute-start.6 = (f32[8,896]{1,0:T(8,128)S(1)}, f32[8,896]{1,0:T(8,128)S(1)}, u32[]{:S(2)}, u32[]{:S(2)}) collective-permute-start(f32[8,896]{1,0:T(8,128)S(1)} %convert_reduce_fusion), channel_id=1, source_target_pairs={{0,0},{1,32},{2,64},{3,96},{4,128},{5,160},{6,192},{7,224},{8,8},{... | collective-permute-start | bytes 86024 | tf_op jit(solution)/shard_map/ppermute | solution.py:300
  131.3 0.1 add_multiply_fusion
  131.4 0.1 copy.6
  131.5 4.6 %collective-permute-done.6 = f32[8,896]{1,0:T(8,128)S(1)} collective-permute-done((f32[8,896]{1,0:T(8,128)S(1)}, f32[8,896]{1,0:T(8,128)S(1)}, u32[]{:S(2)}, u32[]{:S(2)}) %collective-permute-start.6) | collective-permute-done | bytes 28704 | tf_op jit(solution)/shard_map/ppermute | solution.py:300
  136.1 0.7 bitcast_multiply_fusion
  (4 shorter events, 0.0 us)
Async XLA Ops:
  3.8 72.8 %all-to-all-start = ((bf16[8,1168,128]{2,1,0:T(8,128)(2,1)}), bf16[8,1168,128]{2,1,0:T(8,128)(2,1)S(1)}, u32[]{:S(2)}, u32[]{:S(2)}) async-start(bf16[8,1168,128]{2,1,0:T(8,128)(2,1)} %shard_map.46.hz), calls=%async_computation | async-start | bytes 4784128 | tf_op jit(solution)/shard_map/all_to_all | solution.py:286
  16.8 32.0 %collective-permute-start = (bf16[2064,128]{1,0:T(8,128)(2,1)}, bf16[2064,128]{1,0:T(8,128)(2,1)S(1)}, u32[]{:S(2)}, u32[]{:S(2)}) collective-permute-start(bf16[2064,128]{1,0:T(8,128)(2,1)} %get-tuple-element.12), channel_id=1, source_target_pairs={{0,16},{1,17},{2,18},{3,19},{4,20},{5,21},{6,22},{7,23},{8,24},{9,... | collective-permute-start | bytes 1585160 | tf_op jit(solution)/shard_map/ppermute | solution.py:287
  24.7 45.3 %collective-permute-start.1 = (bf16[2064,128]{1,0:T(8,128)(2,1)}, bf16[2064,128]{1,0:T(8,128)(2,1)S(1)}, u32[]{:S(2)}, u32[]{:S(2)}) collective-permute-start(bf16[2064,128]{1,0:T(8,128)(2,1)} %get-tuple-element.13), channel_id=1, source_target_pairs={{0,8},{1,9},{2,10},{3,11},{4,12},{5,13},{6,14},{7,15},{8,16},{9,17... | collective-permute-start | bytes 1585160 | tf_op jit(solution)/shard_map/ppermute | solution.py:287
  27.3 44.1 %collective-permute-start.2 = (bf16[2064,128]{1,0:T(8,128)(2,1)}, bf16[2064,128]{1,0:T(8,128)(2,1)}, u32[]{:S(2)}, u32[]{:S(2)}) collective-permute-start(bf16[2064,128]{1,0:T(8,128)(2,1)} %get-tuple-element.14), channel_id=1, source_target_pairs={{0,24},{1,25},{2,26},{3,27},{4,28},{5,29},{6,30},{7,31},{8,0},{9,1... | collective-permute-start | bytes 1585160 | tf_op jit(solution)/shard_map/ppermute | solution.py:287
  48.8 22.6 %copy-start.2 = (bf16[2064,128]{1,0:T(8,128)(2,1)}, bf16[2064,128]{1,0:T(8,128)(2,1)S(1)}, u32[]{:S(2)}) copy-start(bf16[2064,128]{1,0:T(8,128)(2,1)S(1)} %collective-permute-done.q2) | copy-start | bytes 1585156
  70.0 1.4 copy-start.3
  76.5 25.1 %copy-start.4 = (s32[256,112]{1,0:T(8,128)S(1)}, s32[256,112]{1,0:T(8,128)}, u32[]{:S(2)}) copy-start(s32[256,112]{1,0:T(8,128)} %copy.5) | copy-start | bytes 344068
  76.5 25.8 %copy-start.8 = (s32[8,112]{1,0:T(8,128)S(1)}, s32[8,112]{1,0:T(8,128)}, u32[]{:S(2)}) copy-start(s32[8,112]{1,0:T(8,128)} %exps.1) | copy-start | bytes 10756
  76.5 7.1 %copy-start = (bf16[8,1168,128]{2,1,0:T(8,128)(2,1)}, bf16[8,1168,128]{2,1,0:T(8,128)(2,1)S(1)}, u32[]{:S(2)}) copy-start(bf16[8,1168,128]{2,1,0:T(8,128)(2,1)S(1)} %all-to-all-done.parts.rz) | copy-start | bytes 7176196
  76.5 33.2 %all-to-all-start.1 = ((s16[8,32,1792]{2,1,0:T(8,128)(2,1)}), s16[8,32,1792]{2,1,0:T(8,128)(2,1)S(1)}, u32[]{:S(2)}, u32[]{:S(2)}) async-start(s16[8,32,1792]{2,1,0:T(8,128)(2,1)} %shard_map.49), calls=%async_computation.1 | async-start | bytes 1835008 | tf_op jit(solution)/shard_map/all_to_all | solution.py:293
  88.9 20.8 %collective-permute-start.3 = (s16[64,896]{1,0:T(8,128)(2,1)}, s16[64,896]{1,0:T(8,128)(2,1)S(1)}, u32[]{:S(2)}, u32[]{:S(2)}) collective-permute-start(s16[64,896]{1,0:T(8,128)(2,1)} %get-tuple-element.16), channel_id=1, source_target_pairs={{0,16},{1,17},{2,18},{3,19},{4,20},{5,21},{6,22},{7,23},{8,24},{9,... | collective-permute-start | bytes 344072 | tf_op jit(solution)/shard_map/ppermute | solution.py:295
  93.6 16.1 %collective-permute-start.4 = (s16[64,896]{1,0:T(8,128)(2,1)}, s16[64,896]{1,0:T(8,128)(2,1)S(1)}, u32[]{:S(2)}, u32[]{:S(2)}) collective-permute-start(s16[64,896]{1,0:T(8,128)(2,1)} %get-tuple-element.17), channel_id=1, source_target_pairs={{0,8},{1,9},{2,10},{3,11},{4,12},{5,13},{6,14},{7,15},{8,16},{9,17... | collective-permute-start | bytes 344072 | tf_op jit(solution)/shard_map/ppermute | solution.py:295
  98.5 11.3 %collective-permute-start.5 = (s16[64,896]{1,0:T(8,128)(2,1)}, s16[64,896]{1,0:T(8,128)(2,1)S(1)}, u32[]{:S(2)}, u32[]{:S(2)}) collective-permute-start(s16[64,896]{1,0:T(8,128)(2,1)} %get-tuple-element.18), channel_id=1, source_target_pairs={{0,24},{1,25},{2,26},{3,27},{4,28},{5,29},{6,30},{7,31},{8,0},{9,1... | collective-permute-start | bytes 344072 | tf_op jit(solution)/shard_map/ppermute | solution.py:295
  109.7 0.9 copy-start.1
  109.7 1.0 copy-start.5
  109.7 1.0 copy-start.6
  109.7 1.0 copy-start.7
  114.3 11.2 %all-to-all-start.2 = ((bf16[16,8,896]{2,1,0:T(8,128)(2,1)}), bf16[16,8,896]{2,1,0:T(8,128)(2,1)S(1)}, u32[]{:S(2)}, u32[]{:S(2)}) async-start(bf16[16,8,896]{2,1,0:T(8,128)(2,1)} %shard_map.50), calls=%async_computation.2 | async-start | bytes 458752 | tf_op jit(solution)/shard_map/all_to_all | solution.py:298
  125.5 10.6 %collective-permute-start.6 = (f32[8,896]{1,0:T(8,128)S(1)}, f32[8,896]{1,0:T(8,128)S(1)}, u32[]{:S(2)}, u32[]{:S(2)}) collective-permute-start(f32[8,896]{1,0:T(8,128)S(1)} %convert_reduce_fusion), channel_id=1, source_target_pairs={{0,0},{1,32},{2,64},{3,96},{4,128},{5,160},{6,192},{7,224},{8,8},{... | collective-permute-start | bytes 86024 | tf_op jit(solution)/shard_map/ppermute | solution.py:300

commit v4 on v3

v4 whole, which is shorter than its diff:
```python
import jax
import jax.numpy as jnp
from jax import lax
from jax.experimental import pallas as pl
from jax.experimental.pallas import tpu as pltpu
from jax.sharding import PartitionSpec as P

BLK = 128
NY = 4
NZ = 8
NG = 16
NM = NY * NZ
HALF = 7168
CZ = HALF // NZ
CY = HALF // NY
OFFS = (2, 1, -1)
MAGIC = 12582912.0
SMALL = pltpu.CompilerParams(vmem_limit_bytes=8 * 1024 * 1024)
Z_GROUPS = [[y * NZ + z for z in range(NZ)] for y in range(NY)]


def y_shift(step):
    return [(y * NZ + z, ((y + step) % NY) * NZ + z) for y in range(NY) for z in range(NZ)]


def last_moves():
    moves = []
    for group in range(NG):
        for y in range(NY):
            for z in range(NZ):
                if group < 8:
                    target = z * NM + y * NZ + group
                else:
                    target = (8 + 2 * y + group % 2) * NM + ((group - 8) // 2) * NZ + z
                moves.append((group * NM + y * NZ + z, target))
    return moves


def power_two(expo):
    total = jnp.zeros(expo.shape, jnp.float32)
    for power in range(-8, 9):
        total = total + jnp.where(expo == power, jnp.float32(2.0**power), jnp.float32(0.0))
    return total


def in_vmem(*arrays):
    return [pltpu.with_memory_space_constraint(array, pltpu.VMEM) for array in arrays]


def place():
    member = lax.axis_index("intra")
    return member // NZ, lax.rem(member, NZ)


def round_clip(values):
    return (jnp.clip(values, -127.0, 127.0) + MAGIC) - MAGIC


def pack_z_kernel(acts, exps, cot, out, held, padded, into, outof):
    loads = []
    for j in range(NZ):
        for b in range(CZ // BLK):
            column = j * CZ + b * BLK
            rows = pl.ds(256 + b * BLK, BLK)
            loads.append(
                pltpu.make_async_copy(cot.at[:, column : column + BLK], held.at[j, rows, :], into.at[len(loads)])
            )
    for load in loads:
        load.start()
    turned = acts[...].T
    padded[...] = jnp.zeros((16, BLK), jnp.float32)
    padded[0:8, 0 : exps.shape[1]] = exps[...].astype(jnp.float32)
    tail = padded[...].astype(jnp.bfloat16)
    for j in range(NZ):
        held[j, 0:256, :] = turned
        held[j, 256 + CZ : 256 + CZ + 16, :] = tail
    stores = [pltpu.make_async_copy(held.at[j], out.at[j], outof.at[j]) for j in range(NZ)]
    for j in range(NZ):
        for b in range(CZ // BLK):
            loads[j * (CZ // BLK) + b].wait()
        stores[j].start()
    for store in stores:
        store.wait()


def pack_z(acts, exps, cot):
    shape = (NZ, 256 + CZ + 16, BLK)
    any_spec = pl.BlockSpec(memory_space=pl.ANY)
    vmem_spec = pl.BlockSpec(memory_space=pltpu.VMEM)
    return pl.pallas_call(
        pack_z_kernel,
        out_shape=jax.ShapeDtypeStruct(shape, jnp.bfloat16),
        in_specs=[vmem_spec, vmem_spec, any_spec],
        out_specs=any_spec,
        scratch_shapes=[
            pltpu.VMEM(shape, jnp.bfloat16),
            pltpu.VMEM((16, BLK), jnp.float32),
            pltpu.SemaphoreType.DMA((HALF // BLK,)),
            pltpu.SemaphoreType.DMA((NZ,)),
        ],
        cost_estimate=pl.CostEstimate(flops=0, bytes_accessed=4000000, transcendentals=0),
    )(acts, exps, cot)


def pack_y_kernel(hz, cot, p2, p1, p3, held, into, outof):
    y, _ = place()
    loads, stores = [], []
    per = CY // BLK + 2
    for i, (step, out) in enumerate(zip(OFFS, (p2, p1, p3))):
        start = HALF + CY * lax.rem(y + step + NY, NY)
        moves = [(hz.at[0, 0:256], held.at[i, 0:256]), (hz.at[0, pl.ds(256 + CZ, 16)], held.at[i, pl.ds(256 + CY, 16)])]
        for b in range(CY // BLK):
            column = pl.multiple_of(start + b * BLK, BLK)
            moves.append((cot.at[:, pl.ds(column, BLK)], held.at[i, pl.ds(256 + b * BLK, BLK), :]))
        loads += [pltpu.make_async_copy(src, dst, into.at[i * per + k]) for k, (src, dst) in enumerate(moves)]
        stores.append(pltpu.make_async_copy(held.at[i], out, outof.at[i]))
    for load in loads:
        load.start()
    for i in range(3):
        for k in range(per):
            loads[i * per + k].wait()
        stores[i].start()
    for store in stores:
        store.wait()


def pack_y(hz, cot):
    any_spec = pl.BlockSpec(memory_space=pl.ANY)
    piece = jax.ShapeDtypeStruct((256 + CY + 16, BLK), jnp.bfloat16)
    return pl.pallas_call(
        pack_y_kernel,
        out_shape=[piece, piece, piece],
        in_specs=[any_spec, any_spec],
        out_specs=[any_spec] * 3,
        scratch_shapes=[
            pltpu.VMEM((3, 256 + CY + 16, BLK), jnp.bfloat16),
            pltpu.SemaphoreType.DMA((3 * (CY // BLK + 2),)),
            pltpu.SemaphoreType.DMA((3,)),
        ],
        cost_estimate=pl.CostEstimate(flops=0, bytes_accessed=3000000, transcendentals=0),
    )(hz, cot)


def spread(inverse, first_block, width):
    block = lax.broadcasted_iota(jnp.int32, (BLK, width), 0)
    column = lax.broadcasted_iota(jnp.int32, (BLK, width), 1)
    pick = jnp.where(block == first_block + column // BLK, 1.0, 0.0).astype(jnp.bfloat16)
    return jnp.dot(inverse, pick, preferred_element_type=jnp.float32)


def codes_y(lhs, part, i, scale):
    row = 256 + 256 * i
    both = jnp.concatenate([part[row : row + BLK], part[row + BLK : row + 2 * BLK]], axis=1)
    return round_clip(jnp.dot(lhs, both, preferred_element_type=jnp.float32) * scale)


def early_y_kernel(inverse, hz, cot, q2, out, lhs, own, sems):
    y, _ = place()
    start = HALF + CY * y
    loads = [
        pltpu.make_async_copy(hz.at[0, 0:256], lhs, sems.at[0]),
        pltpu.make_async_copy(cot.at[:, pl.ds(pl.multiple_of(start, CY), CY)], own, sems.at[1]),
    ]
    for load in loads:
        load.start()
    for load in loads:
        load.wait()
    for i in range(CY // 256):
        columns = slice(256 * i, 256 * i + 256)
        scale = spread(inverse[...], HALF // BLK + y * (CY // BLK) + 2 * i, 256)
        local = jnp.dot(lhs[...], own[:, columns], preferred_element_type=jnp.float32)
        total = round_clip(local * scale) + codes_y(q2[0:256], q2, i, scale)
        out[:, columns] = total.astype(jnp.bfloat16)


def early_y(inverse, hz, cot, q2):
    any_spec = pl.BlockSpec(memory_space=pl.ANY)
    vmem_spec = pl.BlockSpec(memory_space=pltpu.VMEM)
    return pl.pallas_call(
        early_y_kernel,
        out_shape=jax.ShapeDtypeStruct((256, CY), jnp.bfloat16),
        in_specs=[vmem_spec, any_spec, any_spec, vmem_spec],
        out_specs=vmem_spec,
        scratch_shapes=[
            pltpu.VMEM((256, BLK), jnp.bfloat16),
            pltpu.VMEM((128, CY), jnp.bfloat16),
            pltpu.SemaphoreType.DMA((2,)),
        ],
        compiler_params=SMALL,
        cost_estimate=pl.CostEstimate(flops=2 * 2 * 256 * 128 * CY, bytes_accessed=2000000, transcendentals=0),
    )(inverse, hz, cot, *in_vmem(q2))


def late_y_kernel(inverse, first, second, early, q2, q1, q3, out, factor, diff):
    y, z = place()
    for i in range(CY // 256):
        columns = slice(256 * i, 256 * i + 256)
        scale = spread(inverse[...], HALF // BLK + y * (CY // BLK) + 2 * i, 256)
        total = early[:, columns].astype(jnp.float32)
        total = total + codes_y(q1[0:256], q1, i, scale) + codes_y(q3[0:256], q3, i, scale)
        for k in range(NZ):
            rows = [total[64 * j + 8 * k : 64 * j + 8 * k + 8] for j in range(NY)]
            out[k, :, columns] = jnp.concatenate(rows, axis=0).astype(jnp.int16)
    for step in range(NY):
        member = lax.rem(y + step, NY)
        expo = second[...].astype(jnp.float32)
        if step > 0:
            expo = (q3, q2, q1)[step - 1][256 + CY : 256 + CY + 16].astype(jnp.float32)[0:8]
        rows = pl.ds(pl.multiple_of(64 * member + 8 * z, 8), 8)
        diff[pl.ds(pl.multiple_of(8 * member, 8), 8)] = first[rows].astype(jnp.float32) - expo
    factor[...] = power_two(diff[...])


def late_y(inverse, first, second, early, q2, q1, q3):
    vmem_spec = pl.BlockSpec(memory_space=pltpu.VMEM)
    return pl.pallas_call(
        late_y_kernel,
        out_shape=[
            jax.ShapeDtypeStruct((NZ, 32, CY), jnp.int16),
            jax.ShapeDtypeStruct((32, BLK), jnp.float32),
        ],
        in_specs=[vmem_spec] * 7,
        out_specs=[vmem_spec] * 2,
        scratch_shapes=[pltpu.VMEM((32, BLK), jnp.float32)],
        compiler_params=SMALL,
        cost_estimate=pl.CostEstimate(flops=2 * 2 * 256 * 128 * CY, bytes_accessed=2000000, transcendentals=0),
    )(inverse, first, second, *in_vmem(early, q2, q1, q3))


def sum_z_kernel(inverse, first, parts, own, s2, s1, s3, factor, total_ref, diff):
    y, z = place()
    for b in range(CZ // BLK):
        scale = spread(inverse[...], z * (CZ // BLK) + b, BLK)
        for h in range(2):
            total = jnp.zeros((BLK, BLK), jnp.float32)
            for r in range(NZ):
                local = jnp.dot(
                    parts[r, h * BLK : h * BLK + BLK],
                    parts[r, 256 + b * BLK : 256 + b * BLK + BLK],
                    preferred_element_type=jnp.float32,
                )
                total = total + round_clip(local * scale[h * BLK : h * BLK + BLK])
            total_ref[h * BLK : h * BLK + BLK, b * BLK : b * BLK + BLK] = total
    for step, out in zip((0,) + OFFS, (own, s2, s1, s3)):
        start = 64 * lax.rem(y + step + NY, NY)
        out[...] = total_ref[pl.ds(pl.multiple_of(start, 64), 64), :].astype(jnp.int16)
    for r in range(NZ):
        rows = pl.ds(pl.multiple_of(64 * y + 8 * r, 8), 8)
        expo = parts[r, 256 + CZ : 256 + CZ + 16].astype(jnp.float32)[0:8]
        diff[8 * r : 8 * r + 8] = first[rows].astype(jnp.float32) - expo
    factor[...] = power_two(diff[...])


def sum_z(inverse, first, parts):
    vmem_spec = pl.BlockSpec(memory_space=pltpu.VMEM)
    return pl.pallas_call(
        sum_z_kernel,
        out_shape=[jax.ShapeDtypeStruct((64, CZ), jnp.int16)] * 4 + [jax.ShapeDtypeStruct((64, BLK), jnp.float32)],
        in_specs=[vmem_spec] * 3,
        out_specs=[vmem_spec] * 5,
        scratch_shapes=[pltpu.VMEM((256, CZ), jnp.float32), pltpu.VMEM((64, BLK), jnp.float32)],
        compiler_params=SMALL,
        cost_estimate=pl.CostEstimate(flops=2 * 8 * 256 * 128 * CZ, bytes_accessed=3000000, transcendentals=0),
    )(inverse, first, *in_vmem(parts))


def second_kernel(factor_z, factor_y, own, s2, s1, s3, sy, out):
    y, z = place()
    scale = spread(factor_z[...].astype(jnp.bfloat16), z * (CZ // BLK), CZ)
    total = own[...].astype(jnp.int32)
    for part in (s2, s1, s3):
        total = total + part[...].astype(jnp.int32)
    codes = round_clip(total.astype(jnp.float32) * scale)
    for k in range(8):
        out[k] = codes[8 * k : 8 * k + 8].astype(jnp.bfloat16)
    scale = spread(factor_y[...].astype(jnp.bfloat16), HALF // BLK + y * (CY // BLK), CY)
    total = sy[0].astype(jnp.int32)
    for r in range(1, NZ):
        total = total + sy[r].astype(jnp.int32)
    codes = round_clip(total.astype(jnp.float32) * scale)
    for k in range(NY):
        for c in range(2):
            out[8 + 2 * k + c] = codes[8 * k : 8 * k + 8, c * CZ : c * CZ + CZ].astype(jnp.bfloat16)


def second_codes(factor_z, factor_y, *arrays):
    vmem_spec = pl.BlockSpec(memory_space=pltpu.VMEM)
    return pl.pallas_call(
        second_kernel,
        out_shape=jax.ShapeDtypeStruct((NG, 8, CZ), jnp.bfloat16),
        in_specs=[vmem_spec] * 7,
        out_specs=vmem_spec,
        compiler_params=SMALL,
        cost_estimate=pl.CostEstimate(flops=4000000, bytes_accessed=2500000, transcendentals=0),
    )(*in_vmem(factor_z, factor_y, *arrays))


def body(acts, cotangent, first_exp, second_exp):
    group = lax.axis_index("inter")
    far = pltpu.with_memory_space_constraint(cotangent, pltpu.HBM)

    hz = pack_z(acts, second_exp, far)
    rz = lax.all_to_all(hz, "intra", 0, 0, axis_index_groups=Z_GROUPS, tiled=True)
    q2, q1, q3 = [lax.ppermute(p, "intra", y_shift(step)) for step, p in zip(OFFS, pack_y(hz, far))]
    room = ((0, 0), (0, BLK - first_exp.shape[1]))
    first, second = jnp.pad(first_exp, room), jnp.pad(second_exp, room)
    inverse = power_two(-first).astype(jnp.bfloat16)

    early = early_y(inverse, hz, far, q2)
    sy, factor_y = late_y(inverse, first, second, early, q2, q1, q3)
    ry = lax.all_to_all(sy, "intra", 0, 0, axis_index_groups=Z_GROUPS, tiled=True)
    own, s2, s1, s3, factor_z = sum_z(inverse, first, rz)
    t2, t1, t3 = [lax.ppermute(s, "intra", y_shift(step)) for step, s in zip(OFFS, (s2, s1, s3))]
    codes = second_codes(factor_z, factor_y, own, t2, t1, t3, ry)

    received = lax.all_to_all(codes, "inter", 0, 0, tiled=True)
    total = jnp.sum(received, axis=0, dtype=jnp.float32)
    rows = lax.ppermute(total, ("inter", "intra"), last_moves())
    my_exp = lax.dynamic_slice_in_dim(second_exp, group * (CZ // BLK), CZ // BLK, 1)
    return rows * (jnp.repeat(power_two(my_exp), BLK, axis=1) * (1.0 / (NG * NM)))


def solution(mesh):
    return jax.shard_map(
        body,
        mesh=mesh,
        in_specs=(P(("inter", "intra"), None), P(("inter", "intra"), None), P(), P("intra", None)),
        out_specs=P("intra", "inter"),
        check_vma=False,
    )
```

time: 138 us -> 131 us (0.949)
  waiting for transfers between devices: 51.5 us -> 56.6 us
  Pallas kernels: 20.3 us -> 16.3 us
  local copies, waits for them, and re-layouts: 4.07 us -> 0.2 us
  other arithmetic: 3.2 us -> 1.05 us
    all_to_all x1, waiting for transfers between devices: 6.8 us -> 10.3 us  [body(): lax.all_to_all(sy, 'intra', 0, 0, axis_index_groups=Z_GROUPS, tiled=True)]
    unnamed x19 -> x7, local copies, waits for them, and re-layouts: 2.69 us -> 0.1 us
    pallas_call x1, Pallas kernels: 3.48 us -> 1.11 us  [second_codes(): pl.pallas_call(second_kernel, out_shape=jax.ShapeDtypeStruct((NG, 8, CZ),...]
    pallas_call x1, Pallas kernels: 5.3 us -> 3.3 us  [sum_z(): pl.pallas_call(sum_z_kernel, out_shape=[jax.ShapeDtypeStruct((64, CZ), jn...]
    ppermute x3, waiting for transfers between devices: 34.7 us -> 36.4 us  [body(): lax.ppermute(p, 'intra', y_shift(step))]
    convert_element_type x1, other arithmetic: 1.77 us -> 0.24 us  [body(): inverse = power_two(-first).astype(jnp.bfloat16)]
    pallas_call x1 -> x2, Pallas kernels: 5.11 us -> 5.34 us  [the longest x1 3.33 us: late_y(): pl.pallas_call(late_y_kernel, out_shape=[jax.ShapeDtypeStruct((NZ, 32, CY...]
  transfers between devices with their start and end apart: 10 -> 10, of which waited for: 6 -> 6; matrix products, arithmetic and copies ran while one was open for 4% -> 0% of each run, Pallas kernels for 10% -> 9%
where the time goes in v4:
time: 131 us
  waiting for transfers between devices  56.6 us (43%)
  starting transfers between devices  56.4 us (43%)
  Pallas kernels  16.3 us (12%)
    ppermute x3, waiting for transfers between devices, body(): lax.ppermute(p, 'intra', y_shift(step))  36.4 us
    ppermute x3, starting transfers between devices, body(): lax.ppermute(p, 'intra', y_shift(step))  15.8 us
    ppermute x3, starting transfers between devices, body(): lax.ppermute(s, 'intra', y_shift(step))  12.5 us
    all_to_all x1, starting transfers between devices, body(): lax.all_to_all(hz, 'intra', 0, 0, axis_index_groups=Z_GROUPS, tiled=True)  10.3 us
    all_to_all x1, waiting for transfers between devices, body(): lax.all_to_all(sy, 'intra', 0, 0, axis_index_groups=Z_GROUPS, tiled=True)  10.3 us
    all_to_all x1, starting transfers between devices, body(): lax.all_to_all(sy, 'intra', 0, 0, axis_index_groups=Z_GROUPS, tiled=True)  6.89 us
    ppermute x1, starting transfers between devices, body(): rows = lax.ppermute(total, ('inter', 'intra'), last_moves())  5.92 us
    all_to_all x1, waiting for transfers between devices, body(): received = lax.all_to_all(codes, 'inter', 0, 0, tiled=True)  5.41 us
  transfers between devices with their start and end apart: 10, of which 6 were waited for; matrix products, arithmetic and copies ran while one was open for 0% of the time, Pallas kernels for 9%

profile of v4, /device:TPU:6, one launch (start us, length us, event | category | flops | bytes accessed | tf_op | source)
XLA Modules:
  0.0 130.6 jit_solution(3903357888409446054)
XLA Ops:
  0.0 3.7 %shard_map.46.hz = bf16[8,1168,128]{2,1,0:T(8,128)(2,1)} custom-call(bf16[128,256]{1,0:T(8,128)(2,1)} %acts.1, s32[8,112]{1,0:T(8,128)} %exps.1, bf16[128,14336]{1,0:T(8,128)(2,1)} %cot.5), custom_call_target="tpu_custom_call" | custom-call | bytes 4000000 | tf_op jit(solution)/shard_map/pallas_call | solution.py:90
  3.7 10.3 %all-to-all-start = ((bf16[8,1168,128]{2,1,0:T(8,128)(2,1)}), bf16[8,1168,128]{2,1,0:T(8,128)(2,1)}, u32[]{:S(2)}, u32[]{:S(2)}) async-start(bf16[8,1168,128]{2,1,0:T(8,128)(2,1)} %shard_map.46.hz), calls=%async_computation | async-start | bytes 4784128 | tf_op jit(solution)/shard_map/all_to_all | solution.py:303
  14.1 0.0 copy-start.1
  14.1 0.0 copy-start.2
  14.1 0.0 copy-start
  14.1 2.8 %shard_map.48 = (bf16[2064,128]{1,0:T(8,128)(2,1)}, bf16[2064,128]{1,0:T(8,128)(2,1)}, bf16[2064,128]{1,0:T(8,128)(2,1)}) custom-call(bf16[8,1168,128]{2,1,0:T(8,128)(2,1)} %shard_map.46.hz, bf16[128,14336]{1,0:T(8,128)(2,1)} %cot.5), custom_call_target="tpu_custom_call" | custom-call | bytes 3000000 | tf_op jit(solution)/shard_map/pallas_call | solution.py:130
  16.9 7.8 %collective-permute-start = (bf16[2064,128]{1,0:T(8,128)(2,1)}, bf16[2064,128]{1,0:T(8,128)(2,1)S(1)}, u32[]{:S(2)}, u32[]{:S(2)}) collective-permute-start(bf16[2064,128]{1,0:T(8,128)(2,1)} %get-tuple-element.16), channel_id=1, source_target_pairs={{0,16},{1,17},{2,18},{3,19},{4,20},{5,21},{6,22},{7,23},{8,24},{9,... | collective-permute-start | bytes 1585160 | tf_op jit(solution)/shard_map/ppermute | solution.py:304
  24.7 2.7 %collective-permute-start.1 = (bf16[2064,128]{1,0:T(8,128)(2,1)}, bf16[2064,128]{1,0:T(8,128)(2,1)}, u32[]{:S(2)}, u32[]{:S(2)}) collective-permute-start(bf16[2064,128]{1,0:T(8,128)(2,1)} %get-tuple-element.17), channel_id=1, source_target_pairs={{0,8},{1,9},{2,10},{3,11},{4,12},{5,13},{6,14},{7,15},{8,16},{9,17... | collective-permute-start | bytes 1585160 | tf_op jit(solution)/shard_map/ppermute | solution.py:304
  27.4 5.3 %collective-permute-start.2 = (bf16[2064,128]{1,0:T(8,128)(2,1)}, bf16[2064,128]{1,0:T(8,128)(2,1)}, u32[]{:S(2)}, u32[]{:S(2)}) collective-permute-start(bf16[2064,128]{1,0:T(8,128)(2,1)} %get-tuple-element.18), channel_id=1, source_target_pairs={{0,24},{1,25},{2,26},{3,27},{4,28},{5,29},{6,30},{7,31},{8,0},{9,1... | collective-permute-start | bytes 1585160 | tf_op jit(solution)/shard_map/ppermute | solution.py:304
  32.7 0.0 copy-done.1
  32.7 0.1 copy.5
  32.8 0.0 copy-done.2
  32.9 0.2 add_convert_fusion.inverse
  33.1 15.8 %collective-permute-done.q2 = bf16[2064,128]{1,0:T(8,128)(2,1)S(1)} collective-permute-done((bf16[2064,128]{1,0:T(8,128)(2,1)}, bf16[2064,128]{1,0:T(8,128)(2,1)S(1)}, u32[]{:S(2)}, u32[]{:S(2)}) %collective-permute-start) | collective-permute-done | bytes 528416 | tf_op jit(solution)/shard_map/ppermute | solution.py:304
  48.9 0.0 copy-done
  48.9 2.0 %shard_map.49.early = bf16[256,1792]{1,0:T(8,128)(2,1)S(1)} custom-call(bf16[256,128]{1,0:T(8,128)(2,1)S(1)} %add_convert_fusion.inverse, bf16[8,1168,128]{2,1,0:T(8,128)(2,1)S(1)} %copy-done, bf16[128,14336]{1,0:T(8,128)(2,1)} %cot.5, bf16[2064,128]{1,0:T(8,128)(2,1)S(1)} %collective-permute-done.q2), custom_call_target="tpu_custom_call" | custom-call | flops 234881024 | bytes 2000000 | tf_op jit(solution)/shard_map/pallas_call | solution.py:179
  50.9 8.6 %collective-permute-done.1.q1 = bf16[2064,128]{1,0:T(8,128)(2,1)} collective-permute-done((bf16[2064,128]{1,0:T(8,128)(2,1)}, bf16[2064,128]{1,0:T(8,128)(2,1)}, u32[]{:S(2)}, u32[]{:S(2)}) %collective-permute-start.1) | collective-permute-done | bytes 528416 | tf_op jit(solution)/shard_map/ppermute | solution.py:304
  59.5 12.1 %collective-permute-done.2.q3 = bf16[2064,128]{1,0:T(8,128)(2,1)} collective-permute-done((bf16[2064,128]{1,0:T(8,128)(2,1)}, bf16[2064,128]{1,0:T(8,128)(2,1)}, u32[]{:S(2)}, u32[]{:S(2)}) %collective-permute-start.2) | collective-permute-done | bytes 528416 | tf_op jit(solution)/shard_map/ppermute | solution.py:304
  71.6 3.3 %shard_map.50 = (s16[8,32,1792]{2,1,0:T(8,128)(2,1)}, f32[32,128]{1,0:T(8,128)S(1)}) custom-call(bf16[256,128]{1,0:T(8,128)(2,1)S(1)} %add_convert_fusion.inverse, s32[256,128]{1,0:T(8,128)S(1)} %pad.8.first, s32[8,128]{1,0:T(8,128)S(1)} %pad.9.second, bf16[256,1792]{1,0:T(8,128)(2,1)S(1)} %shard_map.49.early, ...), custom_call_target="tpu_custom_call" | custom-call | flops 234881024 | bytes 2000000 | tf_op jit(solution)/shard_map/pallas_call | solution.py:216
  74.9 0.0 all-to-all-done.parts
  74.9 6.9 %all-to-all-start.1 = ((s16[8,32,1792]{2,1,0:T(8,128)(2,1)}), s16[8,32,1792]{2,1,0:T(8,128)(2,1)S(1)}, u32[]{:S(2)}, u32[]{:S(2)}) async-start(s16[8,32,1792]{2,1,0:T(8,128)(2,1)} %get-tuple-element.24), calls=%async_computation.1 | async-start | bytes 1835008 | tf_op jit(solution)/shard_map/all_to_all | solution.py:311
  81.8 3.3 %shard_map.47 = (s16[64,896]{1,0:T(8,128)(2,1)S(1)}, s16[64,896]{1,0:T(8,128)(2,1)S(1)}, s16[64,896]{1,0:T(8,128)(2,1)S(1)}, s16[64,896]{1,0:T(8,128)(2,1)S(1)}, f32[64,128]{1,0:T(8,128)S(1)}) custom-call(bf16[256,128]{1,0:T(8,128)(2,1)S(1)} %add_convert_fusion.inverse, s32[256,128]{1,0:T(8,128)S(1)} %pad.8.first, bf16[8,1168,128]{2,1,0:T(8,128)(2,1)} %all-to-all-done.parts), custom_call_target="tpu_custom_call" | custom-call | flops 469762048 | bytes 3000000 | tf_op jit(solution)/shard_map/pallas_call | solution.py:256
  85.1 4.5 %collective-permute-start.3 = (s16[64,896]{1,0:T(8,128)(2,1)S(1)}, s16[64,896]{1,0:T(8,128)(2,1)S(1)}, u32[]{:S(2)}, u32[]{:S(2)}) collective-permute-start(s16[64,896]{1,0:T(8,128)(2,1)S(1)} %get-tuple-element.21), channel_id=1, source_target_pairs={{0,16},{1,17},{2,18},{3,19},{4,20},{5,21},{6,22},{7,23},{8,24},{9,... | collective-permute-start | bytes 344072 | tf_op jit(solution)/shard_map/ppermute | solution.py:313
  89.7 4.9 %collective-permute-start.4 = (s16[64,896]{1,0:T(8,128)(2,1)S(1)}, s16[64,896]{1,0:T(8,128)(2,1)S(1)}, u32[]{:S(2)}, u32[]{:S(2)}) collective-permute-start(s16[64,896]{1,0:T(8,128)(2,1)S(1)} %get-tuple-element.22), channel_id=1, source_target_pairs={{0,8},{1,9},{2,10},{3,11},{4,12},{5,13},{6,14},{7,15},{8,16},{9,17... | collective-permute-start | bytes 344072 | tf_op jit(solution)/shard_map/ppermute | solution.py:313
  94.6 3.0 %collective-permute-start.5 = (s16[64,896]{1,0:T(8,128)(2,1)S(1)}, s16[64,896]{1,0:T(8,128)(2,1)S(1)}, u32[]{:S(2)}, u32[]{:S(2)}) collective-permute-start(s16[64,896]{1,0:T(8,128)(2,1)S(1)} %get-tuple-element.23), channel_id=1, source_target_pairs={{0,24},{1,25},{2,26},{3,27},{4,28},{5,29},{6,30},{7,31},{8,0},{9,1... | collective-permute-start | bytes 344072 | tf_op jit(solution)/shard_map/ppermute | solution.py:313
  97.6 10.3 %all-to-all-done.1.sy = s16[8,32,1792]{2,1,0:T(8,128)(2,1)S(1)} async-done(((s16[8,32,1792]{2,1,0:T(8,128)(2,1)}), s16[8,32,1792]{2,1,0:T(8,128)(2,1)S(1)}, u32[]{:S(2)}, u32[]{:S(2)}) %all-to-all-start.1) | async-done | bytes 917536 | tf_op jit(solution)/shard_map/all_to_all | solution.py:311
  107.9 0.0 collective-permute-done.3.s2
  107.9 0.0 collective-permute-done.4.s1
  107.9 0.0 collective-permute-done.5.s3
  107.9 1.1 shard_map.51
  109.0 4.9 %all-to-all-start.2 = ((bf16[16,8,896]{2,1,0:T(8,128)(2,1)}), bf16[16,8,896]{2,1,0:T(8,128)(2,1)S(1)}, u32[]{:S(2)}, u32[]{:S(2)}) async-start(bf16[16,8,896]{2,1,0:T(8,128)(2,1)} %shard_map.51), calls=%async_computation.2 | async-start | bytes 458752 | tf_op jit(solution)/shard_map/all_to_all | solution.py:316
  113.9 5.4 %all-to-all-done.2 = bf16[16,8,896]{2,1,0:T(8,128)(2,1)S(1)} async-done(((bf16[16,8,896]{2,1,0:T(8,128)(2,1)}), bf16[16,8,896]{2,1,0:T(8,128)(2,1)S(1)}, u32[]{:S(2)}, u32[]{:S(2)}) %all-to-all-start.2) | async-done | bytes 229408 | tf_op jit(solution)/shard_map/all_to_all | solution.py:316
  119.4 5.9 %collective-permute-start.6 = (f32[8,896]{1,0:T(8,128)S(1)}, f32[8,896]{1,0:T(8,128)S(1)}, u32[]{:S(2)}, u32[]{:S(2)}) collective-permute-start(f32[8,896]{1,0:T(8,128)S(1)} %convert_reduce_fusion), channel_id=1, source_target_pairs={{0,0},{1,32},{2,64},{3,96},{4,128},{5,160},{6,192},{7,224},{8,8},{... | collective-permute-start | bytes 86024 | tf_op jit(solution)/shard_map/ppermute | solution.py:318
  125.3 0.1 add_multiply_fusion
  125.4 0.1 copy.6
  125.5 4.5 %collective-permute-done.6 = f32[8,896]{1,0:T(8,128)S(1)} collective-permute-done((f32[8,896]{1,0:T(8,128)S(1)}, f32[8,896]{1,0:T(8,128)S(1)}, u32[]{:S(2)}, u32[]{:S(2)}) %collective-permute-start.6) | collective-permute-done | bytes 28704 | tf_op jit(solution)/shard_map/ppermute | solution.py:318
  130.0 0.7 bitcast_multiply_fusion
  (3 shorter events, 0.1 us)
Async XLA Ops:
  3.7 71.2 %all-to-all-start = ((bf16[8,1168,128]{2,1,0:T(8,128)(2,1)}), bf16[8,1168,128]{2,1,0:T(8,128)(2,1)}, u32[]{:S(2)}, u32[]{:S(2)}) async-start(bf16[8,1168,128]{2,1,0:T(8,128)(2,1)} %shard_map.46.hz), calls=%async_computation | async-start | bytes 4784128 | tf_op jit(solution)/shard_map/all_to_all | solution.py:303
  14.1 18.7 %copy-start.1 = (s32[256,112]{0,1:T(8,128)S(1)}, s32[256,112]{0,1:T(8,128)}, u32[]{:S(2)}) copy-start(s32[256,112]{0,1:T(8,128)} %param.6) | copy-start | bytes 344068
  14.1 18.8 %copy-start.2 = (s32[8,112]{1,0:T(8,128)S(1)}, s32[8,112]{1,0:T(8,128)}, u32[]{:S(2)}) copy-start(s32[8,112]{1,0:T(8,128)} %exps.1) | copy-start | bytes 10756
  14.1 34.8 %copy-start = (bf16[8,1168,128]{2,1,0:T(8,128)(2,1)S(1)}, bf16[8,1168,128]{2,1,0:T(8,128)(2,1)}, u32[]{:S(2)}) copy-start(bf16[8,1168,128]{2,1,0:T(8,128)(2,1)} %shard_map.46.hz) | copy-start | bytes 7176196
  16.9 32.0 %collective-permute-start = (bf16[2064,128]{1,0:T(8,128)(2,1)}, bf16[2064,128]{1,0:T(8,128)(2,1)S(1)}, u32[]{:S(2)}, u32[]{:S(2)}) collective-permute-start(bf16[2064,128]{1,0:T(8,128)(2,1)} %get-tuple-element.16), channel_id=1, source_target_pairs={{0,16},{1,17},{2,18},{3,19},{4,20},{5,21},{6,22},{7,23},{8,24},{9,... | collective-permute-start | bytes 1585160 | tf_op jit(solution)/shard_map/ppermute | solution.py:304
  24.7 34.8 %collective-permute-start.1 = (bf16[2064,128]{1,0:T(8,128)(2,1)}, bf16[2064,128]{1,0:T(8,128)(2,1)}, u32[]{:S(2)}, u32[]{:S(2)}) collective-permute-start(bf16[2064,128]{1,0:T(8,128)(2,1)} %get-tuple-element.17), channel_id=1, source_target_pairs={{0,8},{1,9},{2,10},{3,11},{4,12},{5,13},{6,14},{7,15},{8,16},{9,17... | collective-permute-start | bytes 1585160 | tf_op jit(solution)/shard_map/ppermute | solution.py:304
  27.4 44.2 %collective-permute-start.2 = (bf16[2064,128]{1,0:T(8,128)(2,1)}, bf16[2064,128]{1,0:T(8,128)(2,1)}, u32[]{:S(2)}, u32[]{:S(2)}) collective-permute-start(bf16[2064,128]{1,0:T(8,128)(2,1)} %get-tuple-element.18), channel_id=1, source_target_pairs={{0,24},{1,25},{2,26},{3,27},{4,28},{5,29},{6,30},{7,31},{8,0},{9,1... | collective-permute-start | bytes 1585160 | tf_op jit(solution)/shard_map/ppermute | solution.py:304
  74.9 33.0 %all-to-all-start.1 = ((s16[8,32,1792]{2,1,0:T(8,128)(2,1)}), s16[8,32,1792]{2,1,0:T(8,128)(2,1)S(1)}, u32[]{:S(2)}, u32[]{:S(2)}) async-start(s16[8,32,1792]{2,1,0:T(8,128)(2,1)} %get-tuple-element.24), calls=%async_computation.1 | async-start | bytes 1835008 | tf_op jit(solution)/shard_map/all_to_all | solution.py:311
  85.1 22.8 %collective-permute-start.3 = (s16[64,896]{1,0:T(8,128)(2,1)S(1)}, s16[64,896]{1,0:T(8,128)(2,1)S(1)}, u32[]{:S(2)}, u32[]{:S(2)}) collective-permute-start(s16[64,896]{1,0:T(8,128)(2,1)S(1)} %get-tuple-element.21), channel_id=1, source_target_pairs={{0,16},{1,17},{2,18},{3,19},{4,20},{5,21},{6,22},{7,23},{8,24},{9,... | collective-permute-start | bytes 344072 | tf_op jit(solution)/shard_map/ppermute | solution.py:313
  89.7 18.2 %collective-permute-start.4 = (s16[64,896]{1,0:T(8,128)(2,1)S(1)}, s16[64,896]{1,0:T(8,128)(2,1)S(1)}, u32[]{:S(2)}, u32[]{:S(2)}) collective-permute-start(s16[64,896]{1,0:T(8,128)(2,1)S(1)} %get-tuple-element.22), channel_id=1, source_target_pairs={{0,8},{1,9},{2,10},{3,11},{4,12},{5,13},{6,14},{7,15},{8,16},{9,17... | collective-permute-start | bytes 344072 | tf_op jit(solution)/shard_map/ppermute | solution.py:313
  94.6 13.3 %collective-permute-start.5 = (s16[64,896]{1,0:T(8,128)(2,1)S(1)}, s16[64,896]{1,0:T(8,128)(2,1)S(1)}, u32[]{:S(2)}, u32[]{:S(2)}) collective-permute-start(s16[64,896]{1,0:T(8,128)(2,1)S(1)} %get-tuple-element.23), channel_id=1, source_target_pairs={{0,24},{1,25},{2,26},{3,27},{4,28},{5,29},{6,30},{7,31},{8,0},{9,1... | collective-permute-start | bytes 344072 | tf_op jit(solution)/shard_map/ppermute | solution.py:313
  109.0 10.3 %all-to-all-start.2 = ((bf16[16,8,896]{2,1,0:T(8,128)(2,1)}), bf16[16,8,896]{2,1,0:T(8,128)(2,1)S(1)}, u32[]{:S(2)}, u32[]{:S(2)}) async-start(bf16[16,8,896]{2,1,0:T(8,128)(2,1)} %shard_map.51), calls=%async_computation.2 | async-start | bytes 458752 | tf_op jit(solution)/shard_map/all_to_all | solution.py:316
  119.4 10.6 %collective-permute-start.6 = (f32[8,896]{1,0:T(8,128)S(1)}, f32[8,896]{1,0:T(8,128)S(1)}, u32[]{:S(2)}, u32[]{:S(2)}) collective-permute-start(f32[8,896]{1,0:T(8,128)S(1)} %convert_reduce_fusion), channel_id=1, source_target_pairs={{0,0},{1,32},{2,64},{3,96},{4,128},{5,160},{6,192},{7,224},{8,8},{... | collective-permute-start | bytes 86024 | tf_op jit(solution)/shard_map/ppermute | solution.py:318

commit v5 on v4

v5 whole, which is shorter than its diff:
```python
import jax
import jax.numpy as jnp
from jax import lax
from jax.experimental import pallas as pl
from jax.experimental.pallas import tpu as pltpu
from jax.sharding import PartitionSpec as P

BLK = 128
NY = 4
NZ = 8
NG = 16
NM = NY * NZ
HALF = 7168
CZ = HALF // NZ
CY = HALF // NY
OFFS = (2, 1, -1)
MAGIC = 12582912.0
SMALL = pltpu.CompilerParams(vmem_limit_bytes=8 * 1024 * 1024)
Z_GROUPS = [[y * NZ + z for z in range(NZ)] for y in range(NY)]


def y_shift(step):
    return [(y * NZ + z, ((y + step) % NY) * NZ + z) for y in range(NY) for z in range(NZ)]


def last_moves():
    moves = []
    for group in range(NG):
        for y in range(NY):
            for z in range(NZ):
                if group < 8:
                    target = z * NM + y * NZ + group
                else:
                    target = (8 + 2 * y + group % 2) * NM + ((group - 8) // 2) * NZ + z
                moves.append((group * NM + y * NZ + z, target))
    return moves


def power_two(expo):
    total = jnp.zeros(expo.shape, jnp.float32)
    for power in range(-8, 9):
        total = total + jnp.where(expo == power, jnp.float32(2.0**power), jnp.float32(0.0))
    return total


def in_vmem(*arrays):
    return [pltpu.with_memory_space_constraint(array, pltpu.VMEM) for array in arrays]


def in_hbm(*arrays):
    return [pltpu.with_memory_space_constraint(array, pltpu.HBM) for array in arrays]


def place():
    member = lax.axis_index("intra")
    return member // NZ, lax.rem(member, NZ)


def round_clip(values):
    return (jnp.clip(values, -127.0, 127.0) + MAGIC) - MAGIC


def pack_z_kernel(acts, exps, cot, out, wide, held, acts_here, exps_here, padded, into, outof):
    loads = [pltpu.make_async_copy(cot.at[:, j * CZ : (j + 1) * CZ], wide.at[j], into.at[j]) for j in range(NZ)]
    stores = [pltpu.make_async_copy(held.at[j], out.at[j], outof.at[j]) for j in range(NZ)]
    small = [
        pltpu.make_async_copy(acts, acts_here, into.at[NZ]),
        pltpu.make_async_copy(exps, exps_here, into.at[NZ + 1]),
    ]
    for load in small + loads:
        load.start()
    padded[...] = jnp.zeros((16, BLK), jnp.float32)
    for load in small:
        load.wait()
    turned = acts_here[...].T
    padded[0:8, 0 : exps.shape[1]] = exps_here[...].astype(jnp.float32)
    tail = padded[...].astype(jnp.bfloat16)
    for j in range(NZ):
        held[j, 0:256, :] = turned
        held[j, 256 + CZ : 256 + CZ + 16, :] = tail
        loads[j].wait()
        for b in range(CZ // BLK):
            held[j, 256 + b * BLK : 256 + b * BLK + BLK, :] = wide[j, :, b * BLK : b * BLK + BLK]
        stores[j].start()
    for store in stores:
        store.wait()


def pack_z(acts, exps, cot):
    shape = (NZ, 256 + CZ + 16, BLK)
    any_spec = pl.BlockSpec(memory_space=pl.ANY)
    return pl.pallas_call(
        pack_z_kernel,
        out_shape=jax.ShapeDtypeStruct(shape, jnp.bfloat16),
        in_specs=[any_spec, any_spec, any_spec],
        out_specs=any_spec,
        scratch_shapes=[
            pltpu.VMEM((NZ, 128, CZ), jnp.bfloat16),
            pltpu.VMEM(shape, jnp.bfloat16),
            pltpu.VMEM(acts.shape, jnp.bfloat16),
            pltpu.VMEM(exps.shape, jnp.int32),
            pltpu.VMEM((16, BLK), jnp.float32),
            pltpu.SemaphoreType.DMA((NZ + 2,)),
            pltpu.SemaphoreType.DMA((NZ,)),
        ],
        compiler_params=SMALL,
        cost_estimate=pl.CostEstimate(flops=0, bytes_accessed=4000000, transcendentals=0),
    )(*in_hbm(acts, exps, cot))


def pack_y_kernel(hz, cot, p2, p1, p3, wide, held, into, outof):
    y, _ = place()
    loads, stores = [], []
    for i, (step, out) in enumerate(zip(OFFS, (p2, p1, p3))):
        start = pl.multiple_of(HALF + CY * lax.rem(y + step + NY, NY), CY)
        moves = (
            (cot.at[:, pl.ds(start, CY)], wide.at[i]),
            (hz.at[0, 0:256], held.at[i, 0:256]),
            (hz.at[0, pl.ds(256 + CZ, 16)], held.at[i, pl.ds(256 + CY, 16)]),
        )
        loads += [pltpu.make_async_copy(src, dst, into.at[3 * i + k]) for k, (src, dst) in enumerate(moves)]
        stores.append(pltpu.make_async_copy(held.at[i], out, outof.at[i]))
    for load in loads:
        load.start()
    for i in range(3):
        for k in range(3):
            loads[3 * i + k].wait()
        for b in range(CY // BLK):
            held[i, 256 + b * BLK : 256 + b * BLK + BLK, :] = wide[i, :, b * BLK : b * BLK + BLK]
        stores[i].start()
    for store in stores:
        store.wait()


def pack_y(hz, cot):
    any_spec = pl.BlockSpec(memory_space=pl.ANY)
    piece = jax.ShapeDtypeStruct((256 + CY + 16, BLK), jnp.bfloat16)
    return pl.pallas_call(
        pack_y_kernel,
        out_shape=[piece, piece, piece],
        in_specs=[any_spec, any_spec],
        out_specs=[any_spec] * 3,
        scratch_shapes=[
            pltpu.VMEM((3, 128, CY), jnp.bfloat16),
            pltpu.VMEM((3, 256 + CY + 16, BLK), jnp.bfloat16),
            pltpu.SemaphoreType.DMA((9,)),
            pltpu.SemaphoreType.DMA((3,)),
        ],
        compiler_params=SMALL,
        cost_estimate=pl.CostEstimate(flops=0, bytes_accessed=3000000, transcendentals=0),
    )(hz, cot)


def spread(inverse, first_block, width):
    block = lax.broadcasted_iota(jnp.int32, (BLK, width), 0)
    column = lax.broadcasted_iota(jnp.int32, (BLK, width), 1)
    pick = jnp.where(block == first_block + column // BLK, 1.0, 0.0).astype(jnp.bfloat16)
    return jnp.dot(inverse, pick, preferred_element_type=jnp.float32)


def codes_y(lhs, part, i, scale):
    row = 256 + 256 * i
    both = jnp.concatenate([part[row : row + BLK], part[row + BLK : row + 2 * BLK]], axis=1)
    return round_clip(jnp.dot(lhs, both, preferred_element_type=jnp.float32) * scale)


def early_y_kernel(turned, hz, cot, q2, out, inverse, first, second, lhs, own, expo, sems):
    y, _ = place()
    start = HALF + CY * y
    loads = [
        pltpu.make_async_copy(hz.at[0, 0:256], lhs, sems.at[0]),
        pltpu.make_async_copy(hz.at[0, pl.ds(256 + CZ, 16)], expo, sems.at[1]),
        pltpu.make_async_copy(cot.at[:, pl.ds(pl.multiple_of(start, CY), CY)], own, sems.at[2]),
    ]
    for load in loads:
        load.start()
    count = turned.shape[0]
    exponent = jnp.concatenate([turned[...].astype(jnp.float32), jnp.zeros((BLK - count, 256), jnp.float32)], axis=0).T
    first[...] = exponent
    inverse[...] = power_two(-exponent).astype(jnp.bfloat16)
    for load in loads:
        load.wait()
    second[...] = expo[...].astype(jnp.float32)[0:8]
    for i in range(CY // 256):
        columns = slice(256 * i, 256 * i + 256)
        scale = spread(inverse[...], HALF // BLK + y * (CY // BLK) + 2 * i, 256)
        local = jnp.dot(lhs[...], own[:, columns], preferred_element_type=jnp.float32)
        total = round_clip(local * scale) + codes_y(q2[0:256], q2, i, scale)
        out[:, columns] = total.astype(jnp.bfloat16)


def early_y(turned, hz, cot, q2):
    any_spec = pl.BlockSpec(memory_space=pl.ANY)
    vmem_spec = pl.BlockSpec(memory_space=pltpu.VMEM)
    return pl.pallas_call(
        early_y_kernel,
        out_shape=[
            jax.ShapeDtypeStruct((256, CY), jnp.bfloat16),
            jax.ShapeDtypeStruct((256, BLK), jnp.bfloat16),
            jax.ShapeDtypeStruct((256, BLK), jnp.float32),
            jax.ShapeDtypeStruct((8, BLK), jnp.float32),
        ],
        in_specs=[vmem_spec, any_spec, any_spec, vmem_spec],
        out_specs=[vmem_spec] * 4,
        scratch_shapes=[
            pltpu.VMEM((256, BLK), jnp.bfloat16),
            pltpu.VMEM((128, CY), jnp.bfloat16),
            pltpu.VMEM((16, BLK), jnp.bfloat16),
            pltpu.SemaphoreType.DMA((3,)),
        ],
        compiler_params=SMALL,
        cost_estimate=pl.CostEstimate(flops=2 * 2 * 256 * 128 * CY, bytes_accessed=2000000, transcendentals=0),
    )(turned, hz, cot, *in_vmem(q2))


def late_y_kernel(inverse, first, second, early, q2, q1, q3, out, factor, diff, sums, sems):
    y, z = place()
    stores = []
    for i in range(CY // 256):
        columns = slice(256 * i, 256 * i + 256)
        scale = spread(inverse[...], HALF // BLK + y * (CY // BLK) + 2 * i, 256)
        total = early[:, columns].astype(jnp.float32)
        total = total + codes_y(q1[0:256], q1, i, scale) + codes_y(q3[0:256], q3, i, scale)
        for k in range(NZ):
            rows = [total[64 * j + 8 * k : 64 * j + 8 * k + 8] for j in range(NY)]
            sums[k, :, columns] = jnp.concatenate(rows, axis=0).astype(jnp.int16)
        stores.append(pltpu.make_async_copy(sums.at[:, :, columns], out.at[:, :, columns], sems.at[i]))
        stores[i].start()
    for step in range(NY):
        member = lax.rem(y + step, NY)
        expo = second[...]
        if step > 0:
            expo = (q3, q2, q1)[step - 1][256 + CY : 256 + CY + 16].astype(jnp.float32)[0:8]
        rows = pl.ds(pl.multiple_of(64 * member + 8 * z, 8), 8)
        diff[pl.ds(pl.multiple_of(8 * member, 8), 8)] = first[rows] - expo
    factor[...] = power_two(diff[...])
    for store in stores:
        store.wait()


def late_y(inverse, first, second, early, q2, q1, q3):
    vmem_spec = pl.BlockSpec(memory_space=pltpu.VMEM)
    shape = (NZ, 32, CY)
    return pl.pallas_call(
        late_y_kernel,
        out_shape=[pltpu.HBM(shape, jnp.int16), jax.ShapeDtypeStruct((32, BLK), jnp.float32)],
        in_specs=[vmem_spec] * 7,
        out_specs=[pl.BlockSpec(memory_space=pl.ANY), vmem_spec],
        scratch_shapes=[
            pltpu.VMEM((32, BLK), jnp.float32),
            pltpu.VMEM(shape, jnp.int16),
            pltpu.SemaphoreType.DMA((CY // 256,)),
        ],
        compiler_params=SMALL,
        cost_estimate=pl.CostEstimate(flops=2 * 2 * 256 * 128 * CY, bytes_accessed=2000000, transcendentals=0),
    )(inverse, first, second, *in_vmem(early, q2, q1, q3))


def sum_z_kernel(inverse, first, parts, own, s2, s1, s3, factor, total_ref, diff):
    y, z = place()
    for b in range(CZ // BLK):
        scale = spread(inverse[...], z * (CZ // BLK) + b, BLK)
        for h in range(2):
            total = jnp.zeros((BLK, BLK), jnp.float32)
            for r in range(NZ):
                local = jnp.dot(
                    parts[r, h * BLK : h * BLK + BLK],
                    parts[r, 256 + b * BLK : 256 + b * BLK + BLK],
                    preferred_element_type=jnp.float32,
                )
                total = total + round_clip(local * scale[h * BLK : h * BLK + BLK])
            total_ref[h * BLK : h * BLK + BLK, b * BLK : b * BLK + BLK] = total
    for step, out in zip((0,) + OFFS, (own, s2, s1, s3)):
        start = 64 * lax.rem(y + step + NY, NY)
        out[...] = total_ref[pl.ds(pl.multiple_of(start, 64), 64), :].astype(jnp.int16)
    for r in range(NZ):
        rows = pl.ds(pl.multiple_of(64 * y + 8 * r, 8), 8)
        expo = parts[r, 256 + CZ : 256 + CZ + 16].astype(jnp.float32)[0:8]
        diff[8 * r : 8 * r + 8] = first[rows] - expo
    factor[...] = power_two(diff[...])


def sum_z(inverse, first, parts):
    vmem_spec = pl.BlockSpec(memory_space=pltpu.VMEM)
    return pl.pallas_call(
        sum_z_kernel,
        out_shape=[pltpu.HBM((64, CZ), jnp.int16)]
        + [jax.ShapeDtypeStruct((64, CZ), jnp.int16)] * 3
        + [jax.ShapeDtypeStruct((64, BLK), jnp.float32)],
        in_specs=[vmem_spec] * 3,
        out_specs=[vmem_spec] * 5,
        scratch_shapes=[pltpu.VMEM((256, CZ), jnp.float32), pltpu.VMEM((64, BLK), jnp.float32)],
        compiler_params=SMALL,
        cost_estimate=pl.CostEstimate(flops=2 * 8 * 256 * 128 * CZ, bytes_accessed=3000000, transcendentals=0),
    )(inverse, first, *in_vmem(parts))


def second_kernel(factor_z, factor_y, own, s2, s1, s3, sy, out, own_here, sem):
    y, z = place()
    load = pltpu.make_async_copy(own, own_here, sem)
    load.start()
    scale = spread(factor_y[...].astype(jnp.bfloat16), HALF // BLK + y * (CY // BLK), CY)
    total = sy[0].astype(jnp.int32)
    for r in range(1, NZ):
        total = total + sy[r].astype(jnp.int32)
    codes = round_clip(total.astype(jnp.float32) * scale)
    for k in range(NY):
        for c in range(2):
            out[8 + 2 * k + c] = codes[8 * k : 8 * k + 8, c * CZ : c * CZ + CZ].astype(jnp.bfloat16)
    scale = spread(factor_z[...].astype(jnp.bfloat16), z * (CZ // BLK), CZ)
    total = s2[...].astype(jnp.int32) + s1[...].astype(jnp.int32) + s3[...].astype(jnp.int32)
    load.wait()
    total = total + own_here[...].astype(jnp.int32)
    codes = round_clip(total.astype(jnp.float32) * scale)
    for k in range(8):
        out[k] = codes[8 * k : 8 * k + 8].astype(jnp.bfloat16)


def second_codes(factor_z, factor_y, own, *arrays):
    vmem_spec = pl.BlockSpec(memory_space=pltpu.VMEM)
    return pl.pallas_call(
        second_kernel,
        out_shape=jax.ShapeDtypeStruct((NG, 8, CZ), jnp.bfloat16),
        in_specs=[vmem_spec, vmem_spec, pl.BlockSpec(memory_space=pl.ANY)] + [vmem_spec] * 4,
        out_specs=vmem_spec,
        scratch_shapes=[pltpu.VMEM((64, CZ), jnp.int16), pltpu.SemaphoreType.DMA],
        compiler_params=SMALL,
        cost_estimate=pl.CostEstimate(flops=4000000, bytes_accessed=2500000, transcendentals=0),
    )(*in_vmem(factor_z, factor_y), *in_hbm(own), *in_vmem(*arrays))


def body(acts, cotangent, first_exp, second_exp):
    group = lax.axis_index("inter")
    (far,) = in_hbm(cotangent)

    hz = pack_z(acts, second_exp, far)
    rz = lax.all_to_all(hz, "intra", 0, 0, axis_index_groups=Z_GROUPS, tiled=True)
    (near,) = in_hbm(hz)
    q2, q1, q3 = [lax.ppermute(p, "intra", y_shift(step)) for step, p in zip(OFFS, pack_y(near, far))]
    early, inverse, first, second = early_y(first_exp.T, near, far, q2)
    sy, factor_y = late_y(inverse, first, second, early, q2, q1, q3)
    ry = lax.all_to_all(sy, "intra", 0, 0, axis_index_groups=Z_GROUPS, tiled=True)
    own, s2, s1, s3, factor_z = sum_z(inverse, first, rz)
    t2, t1, t3 = [lax.ppermute(s, "intra", y_shift(step)) for step, s in zip(OFFS, (s2, s1, s3))]
    codes = second_codes(factor_z, factor_y, own, t2, t1, t3, ry)

    received = lax.all_to_all(codes, "inter", 0, 0, tiled=True)
    total = jnp.sum(received, axis=0, dtype=jnp.float32)
    rows = lax.ppermute(total, ("inter", "intra"), last_moves())
    my_exp = lax.dynamic_slice_in_dim(second_exp, group * (CZ // BLK), CZ // BLK, 1)
    return rows * (jnp.repeat(power_two(my_exp), BLK, axis=1) * (1.0 / (NG * NM)))


def solution(mesh):
    return jax.shard_map(
        body,
        mesh=mesh,
        in_specs=(P(("inter", "intra"), None), P(("inter", "intra"), None), P(), P("intra", None)),
        out_specs=P("intra", "inter"),
        check_vma=False,
    )
```

time: 131 us -> 128 us (0.977)
  Pallas kernels: 16.3 us -> 12.3 us
    pallas_call x3, Pallas kernels: 8.65 us -> 6.31 us  [the longest x1 2.42 us: sum_z(): pl.pallas_call(sum_z_kernel, out_shape=[pltpu.HBM((64, CZ), jnp.int16)] +...]
  transfers between devices with their start and end apart: 10 -> 10, of which waited for: 6 -> 6; matrix products, arithmetic and copies ran while one was open for 0% -> 0% of each run, Pallas kernels for 9% -> 6%
where the time goes in v5:
time: 128 us; the launch traced here: 127 us
  waiting for transfers between devices  57.5 us (45%)
  starting transfers between devices  56.4 us (44%)
  Pallas kernels  12.3 us (10%)
    ppermute x3, waiting for transfers between devices, body(): lax.ppermute(p, 'intra', y_shift(step))  36.6 us
    ppermute x3, starting transfers between devices, body(): lax.ppermute(p, 'intra', y_shift(step))  15.7 us
    ppermute x3, starting transfers between devices, body(): lax.ppermute(s, 'intra', y_shift(step))  12.6 us
    all_to_all x1, waiting for transfers between devices, body(): lax.all_to_all(sy, 'intra', 0, 0, axis_index_groups=Z_GROUPS, tiled=True)  11 us
    all_to_all x1, starting transfers between devices, body(): lax.all_to_all(hz, 'intra', 0, 0, axis_index_groups=Z_GROUPS, tiled=True)  10.3 us
    all_to_all x1, starting transfers between devices, body(): lax.all_to_all(sy, 'intra', 0, 0, axis_index_groups=Z_GROUPS, tiled=True)  6.91 us
    ppermute x1, starting transfers between devices, body(): rows = lax.ppermute(total, ('inter', 'intra'), last_moves())  5.88 us
    all_to_all x1, waiting for transfers between devices, body(): received = lax.all_to_all(codes, 'inter', 0, 0, tiled=True)  5.41 us
  transfers between devices with their start and end apart: 10, of which 6 were waited for; matrix products, arithmetic and copies ran while one was open for 0% of the time, Pallas kernels for 6%

profile of v5, /device:TPU:6, one launch (start us, length us, event | category | flops | bytes accessed | tf_op | source)
XLA Modules:
  0.0 127.2 jit_solution(2025996699746686560)
XLA Ops:
  0.0 2.7 %shard_map.46.hz = bf16[8,1168,128]{2,1,0:T(8,128)(2,1)} custom-call(bf16[128,256]{1,0:T(8,128)(2,1)} %acts.1, s32[8,112]{1,0:T(8,128)} %exps.1, bf16[128,14336]{1,0:T(8,128)(2,1)} %cot.5), custom_call_target="tpu_custom_call" | custom-call | bytes 4000000 | tf_op jit(solution)/shard_map/pallas_call | solution.py:92
  2.7 10.3 %all-to-all-start = ((bf16[8,1168,128]{2,1,0:T(8,128)(2,1)}), bf16[8,1168,128]{2,1,0:T(8,128)(2,1)S(1)}, u32[]{:S(2)}, u32[]{:S(2)}) async-start(bf16[8,1168,128]{2,1,0:T(8,128)(2,1)} %shard_map.46.hz), calls=%async_computation | async-start | bytes 4784128 | tf_op jit(solution)/shard_map/all_to_all | solution.py:337
  13.0 0.0 copy-start
  13.0 1.6 %shard_map.47 = (bf16[2064,128]{1,0:T(8,128)(2,1)S(1)}, bf16[2064,128]{1,0:T(8,128)(2,1)S(1)}, bf16[2064,128]{1,0:T(8,128)(2,1)S(1)}) custom-call(bf16[8,1168,128]{2,1,0:T(8,128)(2,1)} %shard_map.46.hz, bf16[128,14336]{1,0:T(8,128)(2,1)} %cot.5), custom_call_target="tpu_custom_call" | custom-call | bytes 3000000 | tf_op jit(solution)/shard_map/pallas_call | solution.py:138
  14.7 7.7 %collective-permute-start = (bf16[2064,128]{1,0:T(8,128)(2,1)S(1)}, bf16[2064,128]{1,0:T(8,128)(2,1)S(1)}, u32[]{:S(2)}, u32[]{:S(2)}) collective-permute-start(bf16[2064,128]{1,0:T(8,128)(2,1)S(1)} %get-tuple-element.19), channel_id=1, source_target_pairs={{0,16},{1,17},{2,18},{3,19},{4,20},{5,21},{6,22},{7,23},{8,24},{9,... | collective-permute-start | bytes 1585160 | tf_op jit(solution)/shard_map/ppermute | solution.py:339
  22.4 2.7 %collective-permute-start.1 = (bf16[2064,128]{1,0:T(8,128)(2,1)S(1)}, bf16[2064,128]{1,0:T(8,128)(2,1)S(1)}, u32[]{:S(2)}, u32[]{:S(2)}) collective-permute-start(bf16[2064,128]{1,0:T(8,128)(2,1)S(1)} %get-tuple-element.25), channel_id=1, source_target_pairs={{0,8},{1,9},{2,10},{3,11},{4,12},{5,13},{6,14},{7,15},{8,16},{9,17... | collective-permute-start | bytes 1585160 | tf_op jit(solution)/shard_map/ppermute | solution.py:339
  25.1 5.3 %collective-permute-start.2 = (bf16[2064,128]{1,0:T(8,128)(2,1)S(1)}, bf16[2064,128]{1,0:T(8,128)(2,1)S(1)}, u32[]{:S(2)}, u32[]{:S(2)}) collective-permute-start(bf16[2064,128]{1,0:T(8,128)(2,1)S(1)} %get-tuple-element.26), channel_id=1, source_target_pairs={{0,24},{1,25},{2,26},{3,27},{4,28},{5,29},{6,30},{7,31},{8,0},{9,1... | collective-permute-start | bytes 1585160 | tf_op jit(solution)/shard_map/ppermute | solution.py:339
  30.4 15.9 %collective-permute-done.q2 = bf16[2064,128]{1,0:T(8,128)(2,1)S(1)} collective-permute-done((bf16[2064,128]{1,0:T(8,128)(2,1)S(1)}, bf16[2064,128]{1,0:T(8,128)(2,1)S(1)}, u32[]{:S(2)}, u32[]{:S(2)}) %collective-permute-start) | collective-permute-done | bytes 528416 | tf_op jit(solution)/shard_map/ppermute | solution.py:339
  46.2 0.0 copy-done
  46.2 2.0 %shard_map.48 = (bf16[256,1792]{1,0:T(8,128)(2,1)S(1)}, bf16[256,128]{1,0:T(8,128)(2,1)S(1)}, f32[256,128]{1,0:T(8,128)S(1)}, f32[8,128]{1,0:T(8,128)S(1)}) custom-call(s32[112,256]{1,0:T(8,128)S(1)} %bitcast.3, bf16[8,1168,128]{2,1,0:T(8,128)(2,1)} %shard_map.46.hz, bf16[128,14336]{1,0:T(8,128)(2,1)} %cot.5, bf16[2064,128]{1,0:T(8,128)(2,1)S(1)} %collective-permute-done.q2), custom_call_target="tpu_custom_call" | custom-call | flops 234881024 | bytes 2000000 | tf_op jit(solution)/shard_map/pallas_call | solution.py:195
  48.2 8.7 %collective-permute-done.1.q1 = bf16[2064,128]{1,0:T(8,128)(2,1)S(1)} collective-permute-done((bf16[2064,128]{1,0:T(8,128)(2,1)S(1)}, bf16[2064,128]{1,0:T(8,128)(2,1)S(1)}, u32[]{:S(2)}, u32[]{:S(2)}) %collective-permute-start.1) | collective-permute-done | bytes 528416 | tf_op jit(solution)/shard_map/ppermute | solution.py:339
  56.9 12.0 %collective-permute-done.2.q3 = bf16[2064,128]{1,0:T(8,128)(2,1)S(1)} collective-permute-done((bf16[2064,128]{1,0:T(8,128)(2,1)S(1)}, bf16[2064,128]{1,0:T(8,128)(2,1)S(1)}, u32[]{:S(2)}, u32[]{:S(2)}) %collective-permute-start.2) | collective-permute-done | bytes 528416 | tf_op jit(solution)/shard_map/ppermute | solution.py:339
  69.0 1.9 %shard_map.50 = (s16[8,32,1792]{2,1,0:T(8,128)(2,1)}, f32[32,128]{1,0:T(8,128)S(1)}) custom-call(bf16[256,128]{1,0:T(8,128)(2,1)S(1)} %get-tuple-element.20.inverse, f32[256,128]{1,0:T(8,128)S(1)} %get-tuple-element.21.first, f32[8,128]{1,0:T(8,128)S(1)} %get-tuple-element.23.second, bf16[256,1792]{1,0:T(8,128)(2,1)S(1)} %get-tuple-element.24.early, ...), custom_call_target="tpu_custom_call" | custom-call | flops 234881024 | bytes 2000000 | tf_op jit(solution)/shard_map/pallas_call | solution.py:244
  70.9 0.0 all-to-all-done.parts
  70.9 6.9 %all-to-all-start.1 = ((s16[8,32,1792]{2,1,0:T(8,128)(2,1)}), s16[8,32,1792]{2,1,0:T(8,128)(2,1)S(1)}, u32[]{:S(2)}, u32[]{:S(2)}) async-start(s16[8,32,1792]{2,1,0:T(8,128)(2,1)} %get-tuple-element.32), calls=%async_computation.1 | async-start | bytes 1835008 | tf_op jit(solution)/shard_map/all_to_all | solution.py:342
  77.8 2.4 %shard_map.49 = (s16[64,896]{1,0:T(8,128)(2,1)}, s16[64,896]{1,0:T(8,128)(2,1)}, s16[64,896]{1,0:T(8,128)(2,1)}, s16[64,896]{1,0:T(8,128)(2,1)}, f32[64,128]{1,0:T(8,128)S(1)}) custom-call(bf16[256,128]{1,0:T(8,128)(2,1)S(1)} %get-tuple-element.20.inverse, f32[256,128]{1,0:T(8,128)S(1)} %get-tuple-element.21.first, bf16[8,1168,128]{2,1,0:T(8,128)(2,1)S(1)} %all-to-all-done.parts), custom_call_target="tpu_custom_call" | custom-call | flops 469762048 | bytes 3000000 | tf_op jit(solution)/shard_map/pallas_call | solution.py:285
  80.2 0.0 copy-start.1
  80.2 4.7 %collective-permute-start.3 = (s16[64,896]{1,0:T(8,128)(2,1)}, s16[64,896]{1,0:T(8,128)(2,1)S(1)}, u32[]{:S(2)}, u32[]{:S(2)}) collective-permute-start(s16[64,896]{1,0:T(8,128)(2,1)} %get-tuple-element.29), channel_id=1, source_target_pairs={{0,16},{1,17},{2,18},{3,19},{4,20},{5,21},{6,22},{7,23},{8,24},{9,... | collective-permute-start | bytes 344072 | tf_op jit(solution)/shard_map/ppermute | solution.py:344
  84.9 4.9 %collective-permute-start.4 = (s16[64,896]{1,0:T(8,128)(2,1)}, s16[64,896]{1,0:T(8,128)(2,1)S(1)}, u32[]{:S(2)}, u32[]{:S(2)}) collective-permute-start(s16[64,896]{1,0:T(8,128)(2,1)} %get-tuple-element.30), channel_id=1, source_target_pairs={{0,8},{1,9},{2,10},{3,11},{4,12},{5,13},{6,14},{7,15},{8,16},{9,17... | collective-permute-start | bytes 344072 | tf_op jit(solution)/shard_map/ppermute | solution.py:344
  89.8 3.1 %collective-permute-start.5 = (s16[64,896]{1,0:T(8,128)(2,1)}, s16[64,896]{1,0:T(8,128)(2,1)S(1)}, u32[]{:S(2)}, u32[]{:S(2)}) collective-permute-start(s16[64,896]{1,0:T(8,128)(2,1)} %get-tuple-element.31), channel_id=1, source_target_pairs={{0,24},{1,25},{2,26},{3,27},{4,28},{5,29},{6,30},{7,31},{8,0},{9,1... | collective-permute-start | bytes 344072 | tf_op jit(solution)/shard_map/ppermute | solution.py:344
  92.9 11.0 %all-to-all-done.1.sy = s16[8,32,1792]{2,1,0:T(8,128)(2,1)S(1)} async-done(((s16[8,32,1792]{2,1,0:T(8,128)(2,1)}), s16[8,32,1792]{2,1,0:T(8,128)(2,1)S(1)}, u32[]{:S(2)}, u32[]{:S(2)}) %all-to-all-start.1) | async-done | bytes 917536 | tf_op jit(solution)/shard_map/all_to_all | solution.py:342
  103.9 0.0 collective-permute-done.3.s2
  103.9 0.0 collective-permute-done.4.s1
  103.9 0.0 collective-permute-done.5.s3
  103.9 1.7 %shard_map.51 = bf16[16,8,896]{2,1,0:T(8,128)(2,1)} custom-call(f32[64,128]{1,0:T(8,128)S(1)} %get-tuple-element.22.factor_z, f32[32,128]{1,0:T(8,128)S(1)} %get-tuple-element.27.factor_y, s16[64,896]{1,0:T(8,128)(2,1)} %get-tuple-element.28.own, s16[64,896]{1,0:T(8,128)(2,1)S(1)} %collective-permute-done.3.s2, ...), custom_call_target="tpu_custom_call" | custom-call | flops 4000000 | bytes 2500000 | tf_op jit(solution)/shard_map/pallas_call | solution.py:321
  105.6 4.9 %all-to-all-start.2 = ((bf16[16,8,896]{2,1,0:T(8,128)(2,1)}), bf16[16,8,896]{2,1,0:T(8,128)(2,1)S(1)}, u32[]{:S(2)}, u32[]{:S(2)}) async-start(bf16[16,8,896]{2,1,0:T(8,128)(2,1)} %shard_map.51), calls=%async_computation.2 | async-start | bytes 458752 | tf_op jit(solution)/shard_map/all_to_all | solution.py:347
  110.5 5.4 %all-to-all-done.2 = bf16[16,8,896]{2,1,0:T(8,128)(2,1)S(1)} async-done(((bf16[16,8,896]{2,1,0:T(8,128)(2,1)}), bf16[16,8,896]{2,1,0:T(8,128)(2,1)S(1)}, u32[]{:S(2)}, u32[]{:S(2)}) %all-to-all-start.2) | async-done | bytes 229408 | tf_op jit(solution)/shard_map/all_to_all | solution.py:347
  116.0 5.9 %collective-permute-start.6 = (f32[8,896]{1,0:T(8,128)S(1)}, f32[8,896]{1,0:T(8,128)S(1)}, u32[]{:S(2)}, u32[]{:S(2)}) collective-permute-start(f32[8,896]{1,0:T(8,128)S(1)} %convert_reduce_fusion), channel_id=1, source_target_pairs={{0,0},{1,32},{2,64},{3,96},{4,128},{5,160},{6,192},{7,224},{8,8},{... | collective-permute-start | bytes 86024 | tf_op jit(solution)/shard_map/ppermute | solution.py:349
  121.9 0.0 copy-done.1
  121.9 0.1 add_multiply_fusion
  122.0 0.1 copy.5
  122.1 4.5 %collective-permute-done.6 = f32[8,896]{1,0:T(8,128)S(1)} collective-permute-done((f32[8,896]{1,0:T(8,128)S(1)}, f32[8,896]{1,0:T(8,128)S(1)}, u32[]{:S(2)}, u32[]{:S(2)}) %collective-permute-start.6) | collective-permute-done | bytes 28704 | tf_op jit(solution)/shard_map/ppermute | solution.py:349
  126.6 0.7 bitcast_multiply_fusion
  (1 shorter events, 0.0 us)
Async XLA Ops:
  2.7 68.2 %all-to-all-start = ((bf16[8,1168,128]{2,1,0:T(8,128)(2,1)}), bf16[8,1168,128]{2,1,0:T(8,128)(2,1)S(1)}, u32[]{:S(2)}, u32[]{:S(2)}) async-start(bf16[8,1168,128]{2,1,0:T(8,128)(2,1)} %shard_map.46.hz), calls=%async_computation | async-start | bytes 4784128 | tf_op jit(solution)/shard_map/all_to_all | solution.py:337
  13.0 33.2 %copy-start = (s32[256,112]{0,1:T(8,128)S(1)}, s32[256,112]{0,1:T(8,128)}, u32[]{:S(2)}) copy-start(s32[256,112]{0,1:T(8,128)} %param.6) | copy-start | bytes 344068
  14.7 31.6 %collective-permute-start = (bf16[2064,128]{1,0:T(8,128)(2,1)S(1)}, bf16[2064,128]{1,0:T(8,128)(2,1)S(1)}, u32[]{:S(2)}, u32[]{:S(2)}) collective-permute-start(bf16[2064,128]{1,0:T(8,128)(2,1)S(1)} %get-tuple-element.19), channel_id=1, source_target_pairs={{0,16},{1,17},{2,18},{3,19},{4,20},{5,21},{6,22},{7,23},{8,24},{9,... | collective-permute-start | bytes 1585160 | tf_op jit(solution)/shard_map/ppermute | solution.py:339
  22.4 34.5 %collective-permute-start.1 = (bf16[2064,128]{1,0:T(8,128)(2,1)S(1)}, bf16[2064,128]{1,0:T(8,128)(2,1)S(1)}, u32[]{:S(2)}, u32[]{:S(2)}) collective-permute-start(bf16[2064,128]{1,0:T(8,128)(2,1)S(1)} %get-tuple-element.25), channel_id=1, source_target_pairs={{0,8},{1,9},{2,10},{3,11},{4,12},{5,13},{6,14},{7,15},{8,16},{9,17... | collective-permute-start | bytes 1585160 | tf_op jit(solution)/shard_map/ppermute | solution.py:339
  25.1 43.8 %collective-permute-start.2 = (bf16[2064,128]{1,0:T(8,128)(2,1)S(1)}, bf16[2064,128]{1,0:T(8,128)(2,1)S(1)}, u32[]{:S(2)}, u32[]{:S(2)}) collective-permute-start(bf16[2064,128]{1,0:T(8,128)(2,1)S(1)} %get-tuple-element.26), channel_id=1, source_target_pairs={{0,24},{1,25},{2,26},{3,27},{4,28},{5,29},{6,30},{7,31},{8,0},{9,1... | collective-permute-start | bytes 1585160 | tf_op jit(solution)/shard_map/ppermute | solution.py:339
  70.9 33.0 %all-to-all-start.1 = ((s16[8,32,1792]{2,1,0:T(8,128)(2,1)}), s16[8,32,1792]{2,1,0:T(8,128)(2,1)S(1)}, u32[]{:S(2)}, u32[]{:S(2)}) async-start(s16[8,32,1792]{2,1,0:T(8,128)(2,1)} %get-tuple-element.32), calls=%async_computation.1 | async-start | bytes 1835008 | tf_op jit(solution)/shard_map/all_to_all | solution.py:342
  80.2 41.7 %copy-start.1 = (s32[8,112]{1,0:T(8,128)S(1)}, s32[8,112]{1,0:T(8,128)}, u32[]{:S(2)}) copy-start(s32[8,112]{1,0:T(8,128)} %exps.1) | copy-start | bytes 10756
  80.2 23.7 %collective-permute-start.3 = (s16[64,896]{1,0:T(8,128)(2,1)}, s16[64,896]{1,0:T(8,128)(2,1)S(1)}, u32[]{:S(2)}, u32[]{:S(2)}) collective-permute-start(s16[64,896]{1,0:T(8,128)(2,1)} %get-tuple-element.29), channel_id=1, source_target_pairs={{0,16},{1,17},{2,18},{3,19},{4,20},{5,21},{6,22},{7,23},{8,24},{9,... | collective-permute-start | bytes 344072 | tf_op jit(solution)/shard_map/ppermute | solution.py:344
  84.9 19.0 %collective-permute-start.4 = (s16[64,896]{1,0:T(8,128)(2,1)}, s16[64,896]{1,0:T(8,128)(2,1)S(1)}, u32[]{:S(2)}, u32[]{:S(2)}) collective-permute-start(s16[64,896]{1,0:T(8,128)(2,1)} %get-tuple-element.30), channel_id=1, source_target_pairs={{0,8},{1,9},{2,10},{3,11},{4,12},{5,13},{6,14},{7,15},{8,16},{9,17... | collective-permute-start | bytes 344072 | tf_op jit(solution)/shard_map/ppermute | solution.py:344
  89.8 14.1 %collective-permute-start.5 = (s16[64,896]{1,0:T(8,128)(2,1)}, s16[64,896]{1,0:T(8,128)(2,1)S(1)}, u32[]{:S(2)}, u32[]{:S(2)}) collective-permute-start(s16[64,896]{1,0:T(8,128)(2,1)} %get-tuple-element.31), channel_id=1, source_target_pairs={{0,24},{1,25},{2,26},{3,27},{4,28},{5,29},{6,30},{7,31},{8,0},{9,1... | collective-permute-start | bytes 344072 | tf_op jit(solution)/shard_map/ppermute | solution.py:344
  105.6 10.3 %all-to-all-start.2 = ((bf16[16,8,896]{2,1,0:T(8,128)(2,1)}), bf16[16,8,896]{2,1,0:T(8,128)(2,1)S(1)}, u32[]{:S(2)}, u32[]{:S(2)}) async-start(bf16[16,8,896]{2,1,0:T(8,128)(2,1)} %shard_map.51), calls=%async_computation.2 | async-start | bytes 458752 | tf_op jit(solution)/shard_map/all_to_all | solution.py:347
  116.0 10.6 %collective-permute-start.6 = (f32[8,896]{1,0:T(8,128)S(1)}, f32[8,896]{1,0:T(8,128)S(1)}, u32[]{:S(2)}, u32[]{:S(2)}) collective-permute-start(f32[8,896]{1,0:T(8,128)S(1)} %convert_reduce_fusion), channel_id=1, source_target_pairs={{0,0},{1,32},{2,64},{3,96},{4,128},{5,160},{6,192},{7,224},{8,8},{... | collective-permute-start | bytes 86024 | tf_op jit(solution)/shard_map/ppermute | solution.py:349

commit v6 on v5

--- a/solution.py
+++ b/solution.py
@@ -16,7 +16,9 @@
 OFFS = (2, 1, -1)
 MAGIC = 12582912.0
 SMALL = pltpu.CompilerParams(vmem_limit_bytes=8 * 1024 * 1024)
-Z_GROUPS = [[y * NZ + z for z in range(NZ)] for y in range(NY)]
+FIRST_Z = 5
+Z_ORDER = [(FIRST_Z + i) % NZ for i in range(NZ)]
+Z_GROUPS = [[y * NZ + z for z in Z_ORDER] for y in range(NY)]
 
 
 def y_shift(step):
@@ -61,7 +63,9 @@
 
 
 def pack_z_kernel(acts, exps, cot, out, wide, held, acts_here, exps_here, padded, into, outof):
-    loads = [pltpu.make_async_copy(cot.at[:, j * CZ : (j + 1) * CZ], wide.at[j], into.at[j]) for j in range(NZ)]
+    loads = [
+        pltpu.make_async_copy(cot.at[:, z * CZ : (z + 1) * CZ], wide.at[j], into.at[j]) for j, z in enumerate(Z_ORDER)
+    ]
     stores = [pltpu.make_async_copy(held.at[j], out.at[j], outof.at[j]) for j in range(NZ)]
     small = [
         pltpu.make_async_copy(acts, acts_here, into.at[NZ]),
@@ -222,7 +226,7 @@
         total = early[:, columns].astype(jnp.float32)
         total = total + codes_y(q1[0:256], q1, i, scale) + codes_y(q3[0:256], q3, i, scale)
         for k in range(NZ):
-            rows = [total[64 * j + 8 * k : 64 * j + 8 * k + 8] for j in range(NY)]
+            rows = [total[64 * j + 8 * Z_ORDER[k] : 64 * j + 8 * Z_ORDER[k] + 8] for j in range(NY)]
             sums[k, :, columns] = jnp.concatenate(rows, axis=0).astype(jnp.int16)
         stores.append(pltpu.make_async_copy(sums.at[:, :, columns], out.at[:, :, columns], sems.at[i]))
         stores[i].start()
@@ -274,9 +278,9 @@
         start = 64 * lax.rem(y + step + NY, NY)
         out[...] = total_ref[pl.ds(pl.multiple_of(start, 64), 64), :].astype(jnp.int16)
     for r in range(NZ):
-        rows = pl.ds(pl.multiple_of(64 * y + 8 * r, 8), 8)
+        rows = pl.ds(pl.multiple_of(64 * y + 8 * Z_ORDER[r], 8), 8)
         expo = parts[r, 256 + CZ : 256 + CZ + 16].astype(jnp.float32)[0:8]
-        diff[8 * r : 8 * r + 8] = first[rows] - expo
+        diff[8 * Z_ORDER[r] : 8 * Z_ORDER[r] + 8] = first[rows] - expo
     factor[...] = power_two(diff[...])
 
 

time: 128 us -> 126 us (0.984)
  waiting for transfers between devices: 57.5 us -> 52.9 us
  starting transfers between devices: 56.4 us -> 58.2 us
    all_to_all x1, waiting for transfers between devices: 11 us -> 4.79 us  [body(): lax.all_to_all(sy, 'intra', 0, 0, axis_index_groups=Z_GROUPS, tiled=True)]
    all_to_all x1, starting transfers between devices: 10.3 us -> 12.7 us  [body(): lax.all_to_all(hz, 'intra', 0, 0, axis_index_groups=Z_GROUPS, tiled=True)]
  transfers between devices with their start and end apart: 10 -> 10, of which waited for: 6 -> 7; matrix products, arithmetic and copies ran while one was open for 0% -> 0% of each run, Pallas kernels for 6% -> 6%
where the time goes in v6:
time: 126 us; the launch traced here: 124 us
  starting transfers between devices  58.2 us (46%)
  waiting for transfers between devices  52.9 us (42%)
  Pallas kernels  12.3 us (10%)
    ppermute x3, waiting for transfers between devices, body(): lax.ppermute(p, 'intra', y_shift(step))  36.5 us
    ppermute x3, starting transfers between devices, body(): lax.ppermute(p, 'intra', y_shift(step))  15.7 us
    all_to_all x1, starting transfers between devices, body(): lax.all_to_all(hz, 'intra', 0, 0, axis_index_groups=Z_GROUPS, tiled=True)  12.7 us
    ppermute x3, starting transfers between devices, body(): lax.ppermute(s, 'intra', y_shift(step))  12.6 us
    all_to_all x1, starting transfers between devices, body(): lax.all_to_all(sy, 'intra', 0, 0, axis_index_groups=Z_GROUPS, tiled=True)  7.23 us
    all_to_all x1, waiting for transfers between devices, body(): received = lax.all_to_all(codes, 'inter', 0, 0, tiled=True)  5.41 us
    ppermute x1, waiting for transfers between devices, body(): rows = lax.ppermute(total, ('inter', 'intra'), last_moves())  5.34 us
    ppermute x1, starting transfers between devices, body(): rows = lax.ppermute(total, ('inter', 'intra'), last_moves())  5.03 us
  transfers between devices with their start and end apart: 10, of which 7 were waited for; matrix products, arithmetic and copies ran while one was open for 0% of the time, Pallas kernels for 6%

profile of v6, /device:TPU:6, one launch (start us, length us, event | category | flops | bytes accessed | tf_op | source)
XLA Modules:
  0.0 124.4 jit_solution(4180166563002353127)
XLA Ops:
  0.0 2.7 %shard_map.46.hz = bf16[8,1168,128]{2,1,0:T(8,128)(2,1)} custom-call(bf16[128,256]{1,0:T(8,128)(2,1)} %acts.1, s32[8,112]{1,0:T(8,128)} %exps.1, bf16[128,14336]{1,0:T(8,128)(2,1)} %cot.5), custom_call_target="tpu_custom_call" | custom-call | bytes 4000000 | tf_op jit(solution)/shard_map/pallas_call | solution.py:96
  2.7 12.7 %all-to-all-start = ((bf16[8,1168,128]{2,1,0:T(8,128)(2,1)}), bf16[8,1168,128]{2,1,0:T(8,128)(2,1)S(1)}, u32[]{:S(2)}, u32[]{:S(2)}) async-start(bf16[8,1168,128]{2,1,0:T(8,128)(2,1)} %shard_map.46.hz), calls=%async_computation | async-start | bytes 4784128 | tf_op jit(solution)/shard_map/all_to_all | solution.py:341
  15.4 0.0 copy-start
  15.4 1.6 %shard_map.47 = (bf16[2064,128]{1,0:T(8,128)(2,1)S(1)}, bf16[2064,128]{1,0:T(8,128)(2,1)S(1)}, bf16[2064,128]{1,0:T(8,128)(2,1)S(1)}) custom-call(bf16[8,1168,128]{2,1,0:T(8,128)(2,1)} %shard_map.46.hz, bf16[128,14336]{1,0:T(8,128)(2,1)} %cot.5), custom_call_target="tpu_custom_call" | custom-call | bytes 3000000 | tf_op jit(solution)/shard_map/pallas_call | solution.py:142
  17.0 7.7 %collective-permute-start = (bf16[2064,128]{1,0:T(8,128)(2,1)S(1)}, bf16[2064,128]{1,0:T(8,128)(2,1)S(1)}, u32[]{:S(2)}, u32[]{:S(2)}) collective-permute-start(bf16[2064,128]{1,0:T(8,128)(2,1)S(1)} %get-tuple-element.19), channel_id=1, source_target_pairs={{0,16},{1,17},{2,18},{3,19},{4,20},{5,21},{6,22},{7,23},{8,24},{9,... | collective-permute-start | bytes 1585160 | tf_op jit(solution)/shard_map/ppermute | solution.py:343
  24.7 2.7 %collective-permute-start.1 = (bf16[2064,128]{1,0:T(8,128)(2,1)S(1)}, bf16[2064,128]{1,0:T(8,128)(2,1)S(1)}, u32[]{:S(2)}, u32[]{:S(2)}) collective-permute-start(bf16[2064,128]{1,0:T(8,128)(2,1)S(1)} %get-tuple-element.25), channel_id=1, source_target_pairs={{0,8},{1,9},{2,10},{3,11},{4,12},{5,13},{6,14},{7,15},{8,16},{9,17... | collective-permute-start | bytes 1585160 | tf_op jit(solution)/shard_map/ppermute | solution.py:343
  27.5 5.3 %collective-permute-start.2 = (bf16[2064,128]{1,0:T(8,128)(2,1)S(1)}, bf16[2064,128]{1,0:T(8,128)(2,1)S(1)}, u32[]{:S(2)}, u32[]{:S(2)}) collective-permute-start(bf16[2064,128]{1,0:T(8,128)(2,1)S(1)} %get-tuple-element.26), channel_id=1, source_target_pairs={{0,24},{1,25},{2,26},{3,27},{4,28},{5,29},{6,30},{7,31},{8,0},{9,1... | collective-permute-start | bytes 1585160 | tf_op jit(solution)/shard_map/ppermute | solution.py:343
  32.7 15.9 %collective-permute-done.q2 = bf16[2064,128]{1,0:T(8,128)(2,1)S(1)} collective-permute-done((bf16[2064,128]{1,0:T(8,128)(2,1)S(1)}, bf16[2064,128]{1,0:T(8,128)(2,1)S(1)}, u32[]{:S(2)}, u32[]{:S(2)}) %collective-permute-start) | collective-permute-done | bytes 528416 | tf_op jit(solution)/shard_map/ppermute | solution.py:343
  48.6 0.0 copy-done
  48.6 2.0 %shard_map.48 = (bf16[256,1792]{1,0:T(8,128)(2,1)S(1)}, bf16[256,128]{1,0:T(8,128)(2,1)S(1)}, f32[256,128]{1,0:T(8,128)S(1)}, f32[8,128]{1,0:T(8,128)S(1)}) custom-call(s32[112,256]{1,0:T(8,128)S(1)} %bitcast.3, bf16[8,1168,128]{2,1,0:T(8,128)(2,1)} %shard_map.46.hz, bf16[128,14336]{1,0:T(8,128)(2,1)} %cot.5, bf16[2064,128]{1,0:T(8,128)(2,1)S(1)} %collective-permute-done.q2), custom_call_target="tpu_custom_call" | custom-call | flops 234881024 | bytes 2000000 | tf_op jit(solution)/shard_map/pallas_call | solution.py:199
  50.6 8.5 %collective-permute-done.1.q1 = bf16[2064,128]{1,0:T(8,128)(2,1)S(1)} collective-permute-done((bf16[2064,128]{1,0:T(8,128)(2,1)S(1)}, bf16[2064,128]{1,0:T(8,128)(2,1)S(1)}, u32[]{:S(2)}, u32[]{:S(2)}) %collective-permute-start.1) | collective-permute-done | bytes 528416 | tf_op jit(solution)/shard_map/ppermute | solution.py:343
  59.1 12.0 %collective-permute-done.2.q3 = bf16[2064,128]{1,0:T(8,128)(2,1)S(1)} collective-permute-done((bf16[2064,128]{1,0:T(8,128)(2,1)S(1)}, bf16[2064,128]{1,0:T(8,128)(2,1)S(1)}, u32[]{:S(2)}, u32[]{:S(2)}) %collective-permute-start.2) | collective-permute-done | bytes 528416 | tf_op jit(solution)/shard_map/ppermute | solution.py:343
  71.2 1.9 %shard_map.50 = (s16[8,32,1792]{2,1,0:T(8,128)(2,1)}, f32[32,128]{1,0:T(8,128)S(1)}) custom-call(bf16[256,128]{1,0:T(8,128)(2,1)S(1)} %get-tuple-element.20.inverse, f32[256,128]{1,0:T(8,128)S(1)} %get-tuple-element.21.first, f32[8,128]{1,0:T(8,128)S(1)} %get-tuple-element.23.second, bf16[256,1792]{1,0:T(8,128)(2,1)S(1)} %get-tuple-element.24.early, ...), custom_call_target="tpu_custom_call" | custom-call | flops 234881024 | bytes 2000000 | tf_op jit(solution)/shard_map/pallas_call | solution.py:248
  73.1 0.0 all-to-all-done.parts
  73.1 7.2 %all-to-all-start.1 = ((s16[8,32,1792]{2,1,0:T(8,128)(2,1)}), s16[8,32,1792]{2,1,0:T(8,128)(2,1)S(1)}, u32[]{:S(2)}, u32[]{:S(2)}) async-start(s16[8,32,1792]{2,1,0:T(8,128)(2,1)} %get-tuple-element.32), calls=%async_computation.1 | async-start | bytes 1835008 | tf_op jit(solution)/shard_map/all_to_all | solution.py:346
  80.3 2.4 %shard_map.49 = (s16[64,896]{1,0:T(8,128)(2,1)}, s16[64,896]{1,0:T(8,128)(2,1)}, s16[64,896]{1,0:T(8,128)(2,1)}, s16[64,896]{1,0:T(8,128)(2,1)}, f32[64,128]{1,0:T(8,128)S(1)}) custom-call(bf16[256,128]{1,0:T(8,128)(2,1)S(1)} %get-tuple-element.20.inverse, f32[256,128]{1,0:T(8,128)S(1)} %get-tuple-element.21.first, bf16[8,1168,128]{2,1,0:T(8,128)(2,1)S(1)} %all-to-all-done.parts), custom_call_target="tpu_custom_call" | custom-call | flops 469762048 | bytes 3000000 | tf_op jit(solution)/shard_map/pallas_call | solution.py:289
  82.7 0.0 copy-start.1
  82.7 4.7 %collective-permute-start.3 = (s16[64,896]{1,0:T(8,128)(2,1)}, s16[64,896]{1,0:T(8,128)(2,1)S(1)}, u32[]{:S(2)}, u32[]{:S(2)}) collective-permute-start(s16[64,896]{1,0:T(8,128)(2,1)} %get-tuple-element.29), channel_id=1, source_target_pairs={{0,16},{1,17},{2,18},{3,19},{4,20},{5,21},{6,22},{7,23},{8,24},{9,... | collective-permute-start | bytes 344072 | tf_op jit(solution)/shard_map/ppermute | solution.py:348
  87.4 4.9 %collective-permute-start.4 = (s16[64,896]{1,0:T(8,128)(2,1)}, s16[64,896]{1,0:T(8,128)(2,1)S(1)}, u32[]{:S(2)}, u32[]{:S(2)}) collective-permute-start(s16[64,896]{1,0:T(8,128)(2,1)} %get-tuple-element.30), channel_id=1, source_target_pairs={{0,8},{1,9},{2,10},{3,11},{4,12},{5,13},{6,14},{7,15},{8,16},{9,17... | collective-permute-start | bytes 344072 | tf_op jit(solution)/shard_map/ppermute | solution.py:348
  92.3 3.1 %collective-permute-start.5 = (s16[64,896]{1,0:T(8,128)(2,1)}, s16[64,896]{1,0:T(8,128)(2,1)S(1)}, u32[]{:S(2)}, u32[]{:S(2)}) collective-permute-start(s16[64,896]{1,0:T(8,128)(2,1)} %get-tuple-element.31), channel_id=1, source_target_pairs={{0,24},{1,25},{2,26},{3,27},{4,28},{5,29},{6,30},{7,31},{8,0},{9,1... | collective-permute-start | bytes 344072 | tf_op jit(solution)/shard_map/ppermute | solution.py:348
  95.4 4.8 %all-to-all-done.1.sy = s16[8,32,1792]{2,1,0:T(8,128)(2,1)S(1)} async-done(((s16[8,32,1792]{2,1,0:T(8,128)(2,1)}), s16[8,32,1792]{2,1,0:T(8,128)(2,1)S(1)}, u32[]{:S(2)}, u32[]{:S(2)}) %all-to-all-start.1) | async-done | bytes 917536 | tf_op jit(solution)/shard_map/all_to_all | solution.py:346
  100.2 0.0 collective-permute-done.3.s2
  100.2 0.0 collective-permute-done.4.s1
  100.2 0.8 collective-permute-done.5.s3
  101.0 1.7 %shard_map.51 = bf16[16,8,896]{2,1,0:T(8,128)(2,1)} custom-call(f32[64,128]{1,0:T(8,128)S(1)} %get-tuple-element.22.factor_z, f32[32,128]{1,0:T(8,128)S(1)} %get-tuple-element.27.factor_y, s16[64,896]{1,0:T(8,128)(2,1)} %get-tuple-element.28.own, s16[64,896]{1,0:T(8,128)(2,1)S(1)} %collective-permute-done.3.s2, ...), custom_call_target="tpu_custom_call" | custom-call | flops 4000000 | bytes 2500000 | tf_op jit(solution)/shard_map/pallas_call | solution.py:325
  102.7 5.0 %all-to-all-start.2 = ((bf16[16,8,896]{2,1,0:T(8,128)(2,1)}), bf16[16,8,896]{2,1,0:T(8,128)(2,1)S(1)}, u32[]{:S(2)}, u32[]{:S(2)}) async-start(bf16[16,8,896]{2,1,0:T(8,128)(2,1)} %shard_map.51), calls=%async_computation.2 | async-start | bytes 458752 | tf_op jit(solution)/shard_map/all_to_all | solution.py:351
  107.7 5.4 %all-to-all-done.2 = bf16[16,8,896]{2,1,0:T(8,128)(2,1)S(1)} async-done(((bf16[16,8,896]{2,1,0:T(8,128)(2,1)}), bf16[16,8,896]{2,1,0:T(8,128)(2,1)S(1)}, u32[]{:S(2)}, u32[]{:S(2)}) %all-to-all-start.2) | async-done | bytes 229408 | tf_op jit(solution)/shard_map/all_to_all | solution.py:351
  113.1 5.0 %collective-permute-start.6 = (f32[8,896]{1,0:T(8,128)S(1)}, f32[8,896]{1,0:T(8,128)S(1)}, u32[]{:S(2)}, u32[]{:S(2)}) collective-permute-start(f32[8,896]{1,0:T(8,128)S(1)} %convert_reduce_fusion), channel_id=1, source_target_pairs={{0,0},{1,32},{2,64},{3,96},{4,128},{5,160},{6,192},{7,224},{8,8},{... | collective-permute-start | bytes 86024 | tf_op jit(solution)/shard_map/ppermute | solution.py:353
  118.2 0.0 copy-done.1
  118.2 0.1 add_multiply_fusion
  118.3 0.1 copy.5
  118.3 5.3 %collective-permute-done.6 = f32[8,896]{1,0:T(8,128)S(1)} collective-permute-done((f32[8,896]{1,0:T(8,128)S(1)}, f32[8,896]{1,0:T(8,128)S(1)}, u32[]{:S(2)}, u32[]{:S(2)}) %collective-permute-start.6) | collective-permute-done | bytes 28704 | tf_op jit(solution)/shard_map/ppermute | solution.py:353
  123.7 0.7 bitcast_multiply_fusion
  (1 shorter events, 0.0 us)
Async XLA Ops:
  2.7 70.4 %all-to-all-start = ((bf16[8,1168,128]{2,1,0:T(8,128)(2,1)}), bf16[8,1168,128]{2,1,0:T(8,128)(2,1)S(1)}, u32[]{:S(2)}, u32[]{:S(2)}) async-start(bf16[8,1168,128]{2,1,0:T(8,128)(2,1)} %shard_map.46.hz), calls=%async_computation | async-start | bytes 4784128 | tf_op jit(solution)/shard_map/all_to_all | solution.py:341
  15.4 33.2 %copy-start = (s32[256,112]{0,1:T(8,128)S(1)}, s32[256,112]{0,1:T(8,128)}, u32[]{:S(2)}) copy-start(s32[256,112]{0,1:T(8,128)} %param.6) | copy-start | bytes 344068
  17.0 31.6 %collective-permute-start = (bf16[2064,128]{1,0:T(8,128)(2,1)S(1)}, bf16[2064,128]{1,0:T(8,128)(2,1)S(1)}, u32[]{:S(2)}, u32[]{:S(2)}) collective-permute-start(bf16[2064,128]{1,0:T(8,128)(2,1)S(1)} %get-tuple-element.19), channel_id=1, source_target_pairs={{0,16},{1,17},{2,18},{3,19},{4,20},{5,21},{6,22},{7,23},{8,24},{9,... | collective-permute-start | bytes 1585160 | tf_op jit(solution)/shard_map/ppermute | solution.py:343
  24.7 34.4 %collective-permute-start.1 = (bf16[2064,128]{1,0:T(8,128)(2,1)S(1)}, bf16[2064,128]{1,0:T(8,128)(2,1)S(1)}, u32[]{:S(2)}, u32[]{:S(2)}) collective-permute-start(bf16[2064,128]{1,0:T(8,128)(2,1)S(1)} %get-tuple-element.25), channel_id=1, source_target_pairs={{0,8},{1,9},{2,10},{3,11},{4,12},{5,13},{6,14},{7,15},{8,16},{9,17... | collective-permute-start | bytes 1585160 | tf_op jit(solution)/shard_map/ppermute | solution.py:343
  27.5 43.7 %collective-permute-start.2 = (bf16[2064,128]{1,0:T(8,128)(2,1)S(1)}, bf16[2064,128]{1,0:T(8,128)(2,1)S(1)}, u32[]{:S(2)}, u32[]{:S(2)}) collective-permute-start(bf16[2064,128]{1,0:T(8,128)(2,1)S(1)} %get-tuple-element.26), channel_id=1, source_target_pairs={{0,24},{1,25},{2,26},{3,27},{4,28},{5,29},{6,30},{7,31},{8,0},{9,1... | collective-permute-start | bytes 1585160 | tf_op jit(solution)/shard_map/ppermute | solution.py:343
  73.1 27.1 %all-to-all-start.1 = ((s16[8,32,1792]{2,1,0:T(8,128)(2,1)}), s16[8,32,1792]{2,1,0:T(8,128)(2,1)S(1)}, u32[]{:S(2)}, u32[]{:S(2)}) async-start(s16[8,32,1792]{2,1,0:T(8,128)(2,1)} %get-tuple-element.32), calls=%async_computation.1 | async-start | bytes 1835008 | tf_op jit(solution)/shard_map/all_to_all | solution.py:346
  82.7 35.4 %copy-start.1 = (s32[8,112]{1,0:T(8,128)S(1)}, s32[8,112]{1,0:T(8,128)}, u32[]{:S(2)}) copy-start(s32[8,112]{1,0:T(8,128)} %exps.1) | copy-start | bytes 10756
  82.7 17.4 %collective-permute-start.3 = (s16[64,896]{1,0:T(8,128)(2,1)}, s16[64,896]{1,0:T(8,128)(2,1)S(1)}, u32[]{:S(2)}, u32[]{:S(2)}) collective-permute-start(s16[64,896]{1,0:T(8,128)(2,1)} %get-tuple-element.29), channel_id=1, source_target_pairs={{0,16},{1,17},{2,18},{3,19},{4,20},{5,21},{6,22},{7,23},{8,24},{9,... | collective-permute-start | bytes 344072 | tf_op jit(solution)/shard_map/ppermute | solution.py:348
  87.4 12.8 %collective-permute-start.4 = (s16[64,896]{1,0:T(8,128)(2,1)}, s16[64,896]{1,0:T(8,128)(2,1)S(1)}, u32[]{:S(2)}, u32[]{:S(2)}) collective-permute-start(s16[64,896]{1,0:T(8,128)(2,1)} %get-tuple-element.30), channel_id=1, source_target_pairs={{0,8},{1,9},{2,10},{3,11},{4,12},{5,13},{6,14},{7,15},{8,16},{9,17... | collective-permute-start | bytes 344072 | tf_op jit(solution)/shard_map/ppermute | solution.py:348
  92.3 8.7 %collective-permute-start.5 = (s16[64,896]{1,0:T(8,128)(2,1)}, s16[64,896]{1,0:T(8,128)(2,1)S(1)}, u32[]{:S(2)}, u32[]{:S(2)}) collective-permute-start(s16[64,896]{1,0:T(8,128)(2,1)} %get-tuple-element.31), channel_id=1, source_target_pairs={{0,24},{1,25},{2,26},{3,27},{4,28},{5,29},{6,30},{7,31},{8,0},{9,1... | collective-permute-start | bytes 344072 | tf_op jit(solution)/shard_map/ppermute | solution.py:348
  102.7 10.4 %all-to-all-start.2 = ((bf16[16,8,896]{2,1,0:T(8,128)(2,1)}), bf16[16,8,896]{2,1,0:T(8,128)(2,1)S(1)}, u32[]{:S(2)}, u32[]{:S(2)}) async-start(bf16[16,8,896]{2,1,0:T(8,128)(2,1)} %shard_map.51), calls=%async_computation.2 | async-start | bytes 458752 | tf_op jit(solution)/shard_map/all_to_all | solution.py:351
  113.1 10.6 %collective-permute-start.6 = (f32[8,896]{1,0:T(8,128)S(1)}, f32[8,896]{1,0:T(8,128)S(1)}, u32[]{:S(2)}, u32[]{:S(2)}) collective-permute-start(f32[8,896]{1,0:T(8,128)S(1)} %convert_reduce_fusion), channel_id=1, source_target_pairs={{0,0},{1,32},{2,64},{3,96},{4,128},{5,160},{6,192},{7,224},{8,8},{... | collective-permute-start | bytes 86024 | tf_op jit(solution)/shard_map/ppermute | solution.py:353

commit v7 on v6

--- a/solution.py
+++ b/solution.py
@@ -299,38 +299,68 @@
     )(inverse, first, *in_vmem(parts))
 
 
-def second_kernel(factor_z, factor_y, own, s2, s1, s3, sy, out, own_here, sem):
-    y, z = place()
-    load = pltpu.make_async_copy(own, own_here, sem)
+def second_z_kernel(factor, own, s2, s1, s3, out, own_here, codes_here, sems):
+    _, z = place()
+    load = pltpu.make_async_copy(own, own_here, sems.at[0])
     load.start()
-    scale = spread(factor_y[...].astype(jnp.bfloat16), HALF // BLK + y * (CY // BLK), CY)
+    scale = spread(factor[...].astype(jnp.bfloat16), z * (CZ // BLK), CZ)
+    total = s2[...].astype(jnp.int32) + s1[...].astype(jnp.int32) + s3[...].astype(jnp.int32)
+    load.wait()
+    total = total + own_here[...].astype(jnp.int32)
+    codes = round_clip(total.astype(jnp.float32) * scale)
+    for k in range(8):
+        codes_here[k] = codes[8 * k : 8 * k + 8].astype(jnp.bfloat16)
+    store = pltpu.make_async_copy(codes_here, out.at[0:8], sems.at[1])
+    store.start()
+    store.wait()
+
+
+def second_z(factor, own, *arrays):
+    any_spec = pl.BlockSpec(memory_space=pl.ANY)
+    vmem_spec = pl.BlockSpec(memory_space=pltpu.VMEM)
+    return pl.pallas_call(
+        second_z_kernel,
+        out_shape=pltpu.HBM((NG, 8, CZ), jnp.bfloat16),
+        in_specs=[vmem_spec, any_spec] + [vmem_spec] * 3,
+        out_specs=any_spec,
+        scratch_shapes=[
+            pltpu.VMEM((64, CZ), jnp.int16),
+            pltpu.VMEM((8, 8, CZ), jnp.bfloat16),
+            pltpu.SemaphoreType.DMA((2,)),
+        ],
+        compiler_params=SMALL,
+        cost_estimate=pl.CostEstimate(flops=2000000, bytes_accessed=700000, transcendentals=0),
+    )(*in_vmem(factor), *in_hbm(own), *in_vmem(*arrays))
+
+
+def second_y_kernel(factor, sy, rest, out, codes_here, sem):
+    y, _ = place()
+    scale = spread(factor[...].astype(jnp.bfloat16), HALF // BLK + y * (CY // BLK), CY)
     total = sy[0].astype(jnp.int32)
     for r in range(1, NZ):
         total = total + sy[r].astype(jnp.int32)
     codes = round_clip(total.astype(jnp.float32) * scale)
     for k in range(NY):
         for c in range(2):
-            out[8 + 2 * k + c] = codes[8 * k : 8 * k + 8, c * CZ : c * CZ + CZ].astype(jnp.bfloat16)
-    scale = spread(factor_z[...].astype(jnp.bfloat16), z * (CZ // BLK), CZ)
-    total = s2[...].astype(jnp.int32) + s1[...].astype(jnp.int32) + s3[...].astype(jnp.int32)
-    load.wait()
-    total = total + own_here[...].astype(jnp.int32)
-    codes = round_clip(total.astype(jnp.float32) * scale)
-    for k in range(8):
-        out[k] = codes[8 * k : 8 * k + 8].astype(jnp.bfloat16)
-
-
-def second_codes(factor_z, factor_y, own, *arrays):
-    vmem_spec = pl.BlockSpec(memory_space=pltpu.VMEM)
-    return pl.pallas_call(
-        second_kernel,
-        out_shape=jax.ShapeDtypeStruct((NG, 8, CZ), jnp.bfloat16),
-        in_specs=[vmem_spec, vmem_spec, pl.BlockSpec(memory_space=pl.ANY)] + [vmem_spec] * 4,
-        out_specs=vmem_spec,
-        scratch_shapes=[pltpu.VMEM((64, CZ), jnp.int16), pltpu.SemaphoreType.DMA],
-        compiler_params=SMALL,
-        cost_estimate=pl.CostEstimate(flops=4000000, bytes_accessed=2500000, transcendentals=0),
-    )(*in_vmem(factor_z, factor_y), *in_hbm(own), *in_vmem(*arrays))
+            codes_here[2 * k + c] = codes[8 * k : 8 * k + 8, c * CZ : c * CZ + CZ].astype(jnp.bfloat16)
+    store = pltpu.make_async_copy(codes_here, out.at[8:16], sem)
+    store.start()
+    store.wait()
+
+
+def second_y(factor, sy, rest):
+    any_spec = pl.BlockSpec(memory_space=pl.ANY)
+    vmem_spec = pl.BlockSpec(memory_space=pltpu.VMEM)
+    return pl.pallas_call(
+        second_y_kernel,
+        out_shape=pltpu.HBM((NG, 8, CZ), jnp.bfloat16),
+        in_specs=[vmem_spec, vmem_spec, any_spec],
+        out_specs=any_spec,
+        scratch_shapes=[pltpu.VMEM((8, 8, CZ), jnp.bfloat16), pltpu.SemaphoreType.DMA],
+        input_output_aliases={2: 0},
+        compiler_params=SMALL,
+        cost_estimate=pl.CostEstimate(flops=2000000, bytes_accessed=1200000, transcendentals=0),
+    )(*in_vmem(factor, sy), *in_hbm(rest))
 
 
 def body(acts, cotangent, first_exp, second_exp):
@@ -346,11 +376,11 @@
     ry = lax.all_to_all(sy, "intra", 0, 0, axis_index_groups=Z_GROUPS, tiled=True)
     own, s2, s1, s3, factor_z = sum_z(inverse, first, rz)
     t2, t1, t3 = [lax.ppermute(s, "intra", y_shift(step)) for step, s in zip(OFFS, (s2, s1, s3))]
-    codes = second_codes(factor_z, factor_y, own, t2, t1, t3, ry)
+    codes = second_y(factor_y, ry, second_z(factor_z, own, t2, t1, t3))
 
     received = lax.all_to_all(codes, "inter", 0, 0, tiled=True)
-    total = jnp.sum(received, axis=0, dtype=jnp.float32)
-    rows = lax.ppermute(total, ("inter", "intra"), last_moves())
+    total = jnp.sum(received, axis=0, dtype=jnp.float32).astype(jnp.int16)
+    rows = lax.ppermute(total, ("inter", "intra"), last_moves()).astype(jnp.float32)
     my_exp = lax.dynamic_slice_in_dim(second_exp, group * (CZ // BLK), CZ // BLK, 1)
     return rows * (jnp.repeat(power_two(my_exp), BLK, axis=1) * (1.0 / (NG * NM)))
 

time: 126 us -> 125 us (level)
    all_to_all x1, waiting for transfers between devices: 4.79 us -> 0.01 us  [body(): lax.all_to_all(sy, 'intra', 0, 0, axis_index_groups=Z_GROUPS, tiled=True)]
    ppermute x3, waiting for transfers between devices: 0.85 us -> 5.44 us  [body(): lax.ppermute(s, 'intra', y_shift(step))]
    pallas_call x1 -> x2, Pallas kernels: 1.67 us -> 2.59 us  [the longest x1 1.63 us: second_z(): pl.pallas_call(second_z_kernel, out_shape=pltpu.HBM((NG, 8, CZ), jnp.bflo...]
  transfers between devices with their start and end apart: 10 -> 10, of which waited for: 7 -> 8; matrix products, arithmetic and copies ran while one was open for 0% -> 0% of each run, Pallas kernels for 6% -> 8%
where the time goes in v7:
time: 125 us
  starting transfers between devices  58.1 us (46%)
  waiting for transfers between devices  52.4 us (42%)
  Pallas kernels  13.1 us (10%)
    ppermute x3, waiting for transfers between devices, body(): lax.ppermute(p, 'intra', y_shift(step))  36.5 us
    ppermute x3, starting transfers between devices, body(): lax.ppermute(p, 'intra', y_shift(step))  15.7 us
    all_to_all x1, starting transfers between devices, body(): lax.all_to_all(hz, 'intra', 0, 0, axis_index_groups=Z_GROUPS, tiled=True)  12.7 us
    ppermute x3, starting transfers between devices, body(): lax.ppermute(s, 'intra', y_shift(step))  12.5 us
    all_to_all x1, starting transfers between devices, body(): lax.all_to_all(sy, 'intra', 0, 0, axis_index_groups=Z_GROUPS, tiled=True)  7.23 us
    ppermute x3, waiting for transfers between devices, body(): lax.ppermute(s, 'intra', y_shift(step))  5.44 us
    all_to_all x1, waiting for transfers between devices, body(): received = lax.all_to_all(codes, 'inter', 0, 0, tiled=True)  5.41 us
    ppermute x1, starting transfers between devices, body(): lax.ppermute(total, ('inter', 'intra'), last_moves()).astype(jnp.float32)  5.14 us
  transfers between devices with their start and end apart: 10, of which 8 were waited for; matrix products, arithmetic and copies ran while one was open for 0% of the time, Pallas kernels for 8%

profile of v7, /device:TPU:6, one launch (start us, length us, event | category | flops | bytes accessed | tf_op | source)
XLA Modules:
  0.0 124.6 jit_solution(1914086792493873782)
XLA Ops:
  0.0 2.7 %shard_map.46.hz = bf16[8,1168,128]{2,1,0:T(8,128)(2,1)} custom-call(bf16[128,256]{1,0:T(8,128)(2,1)} %acts.1, s32[8,112]{1,0:T(8,128)} %exps.1, bf16[128,14336]{1,0:T(8,128)(2,1)} %cot.5), custom_call_target="tpu_custom_call" | custom-call | bytes 4000000 | tf_op jit(solution)/shard_map/pallas_call | solution.py:96
  2.7 12.7 %all-to-all-start.1 = ((bf16[8,1168,128]{2,1,0:T(8,128)(2,1)}), bf16[8,1168,128]{2,1,0:T(8,128)(2,1)S(1)}, u32[]{:S(2)}, u32[]{:S(2)}) async-start(bf16[8,1168,128]{2,1,0:T(8,128)(2,1)} %shard_map.46.hz), calls=%async_computation.1 | async-start | bytes 4784128 | tf_op jit(solution)/shard_map/all_to_all | solution.py:371
  15.4 0.0 copy-start
  15.4 1.6 %shard_map.47 = (bf16[2064,128]{1,0:T(8,128)(2,1)S(1)}, bf16[2064,128]{1,0:T(8,128)(2,1)S(1)}, bf16[2064,128]{1,0:T(8,128)(2,1)S(1)}) custom-call(bf16[8,1168,128]{2,1,0:T(8,128)(2,1)} %shard_map.46.hz, bf16[128,14336]{1,0:T(8,128)(2,1)} %cot.5), custom_call_target="tpu_custom_call" | custom-call | bytes 3000000 | tf_op jit(solution)/shard_map/pallas_call | solution.py:142
  17.0 7.7 %collective-permute-start = (bf16[2064,128]{1,0:T(8,128)(2,1)S(1)}, bf16[2064,128]{1,0:T(8,128)(2,1)S(1)}, u32[]{:S(2)}, u32[]{:S(2)}) collective-permute-start(bf16[2064,128]{1,0:T(8,128)(2,1)S(1)} %get-tuple-element.19), channel_id=1, source_target_pairs={{0,16},{1,17},{2,18},{3,19},{4,20},{5,21},{6,22},{7,23},{8,24},{9,... | collective-permute-start | bytes 1585160 | tf_op jit(solution)/shard_map/ppermute | solution.py:373
  24.7 2.7 %collective-permute-start.1 = (bf16[2064,128]{1,0:T(8,128)(2,1)S(1)}, bf16[2064,128]{1,0:T(8,128)(2,1)S(1)}, u32[]{:S(2)}, u32[]{:S(2)}) collective-permute-start(bf16[2064,128]{1,0:T(8,128)(2,1)S(1)} %get-tuple-element.24), channel_id=1, source_target_pairs={{0,8},{1,9},{2,10},{3,11},{4,12},{5,13},{6,14},{7,15},{8,16},{9,17... | collective-permute-start | bytes 1585160 | tf_op jit(solution)/shard_map/ppermute | solution.py:373
  27.5 5.3 %collective-permute-start.2 = (bf16[2064,128]{1,0:T(8,128)(2,1)S(1)}, bf16[2064,128]{1,0:T(8,128)(2,1)S(1)}, u32[]{:S(2)}, u32[]{:S(2)}) collective-permute-start(bf16[2064,128]{1,0:T(8,128)(2,1)S(1)} %get-tuple-element.25), channel_id=1, source_target_pairs={{0,24},{1,25},{2,26},{3,27},{4,28},{5,29},{6,30},{7,31},{8,0},{9,1... | collective-permute-start | bytes 1585160 | tf_op jit(solution)/shard_map/ppermute | solution.py:373
  32.7 15.9 %collective-permute-done.q2 = bf16[2064,128]{1,0:T(8,128)(2,1)S(1)} collective-permute-done((bf16[2064,128]{1,0:T(8,128)(2,1)S(1)}, bf16[2064,128]{1,0:T(8,128)(2,1)S(1)}, u32[]{:S(2)}, u32[]{:S(2)}) %collective-permute-start) | collective-permute-done | bytes 528416 | tf_op jit(solution)/shard_map/ppermute | solution.py:373
  48.6 0.0 copy-done
  48.6 2.0 %shard_map.48 = (bf16[256,1792]{1,0:T(8,128)(2,1)S(1)}, bf16[256,128]{1,0:T(8,128)(2,1)S(1)}, f32[256,128]{1,0:T(8,128)S(1)}, f32[8,128]{1,0:T(8,128)S(1)}) custom-call(s32[112,256]{1,0:T(8,128)S(1)} %bitcast.3, bf16[8,1168,128]{2,1,0:T(8,128)(2,1)} %shard_map.46.hz, bf16[128,14336]{1,0:T(8,128)(2,1)} %cot.5, bf16[2064,128]{1,0:T(8,128)(2,1)S(1)} %collective-permute-done.q2), custom_call_target="tpu_custom_call" | custom-call | flops 234881024 | bytes 2000000 | tf_op jit(solution)/shard_map/pallas_call | solution.py:199
  50.6 8.5 %collective-permute-done.1.q1 = bf16[2064,128]{1,0:T(8,128)(2,1)S(1)} collective-permute-done((bf16[2064,128]{1,0:T(8,128)(2,1)S(1)}, bf16[2064,128]{1,0:T(8,128)(2,1)S(1)}, u32[]{:S(2)}, u32[]{:S(2)}) %collective-permute-start.1) | collective-permute-done | bytes 528416 | tf_op jit(solution)/shard_map/ppermute | solution.py:373
  59.1 12.0 %collective-permute-done.2.q3 = bf16[2064,128]{1,0:T(8,128)(2,1)S(1)} collective-permute-done((bf16[2064,128]{1,0:T(8,128)(2,1)S(1)}, bf16[2064,128]{1,0:T(8,128)(2,1)S(1)}, u32[]{:S(2)}, u32[]{:S(2)}) %collective-permute-start.2) | collective-permute-done | bytes 528416 | tf_op jit(solution)/shard_map/ppermute | solution.py:373
  71.2 1.9 %shard_map.49 = (s16[8,32,1792]{2,1,0:T(8,128)(2,1)}, f32[32,128]{1,0:T(8,128)S(1)}) custom-call(bf16[256,128]{1,0:T(8,128)(2,1)S(1)} %get-tuple-element.20.inverse, f32[256,128]{1,0:T(8,128)S(1)} %get-tuple-element.21.first, f32[8,128]{1,0:T(8,128)S(1)} %get-tuple-element.22.second, bf16[256,1792]{1,0:T(8,128)(2,1)S(1)} %get-tuple-element.23.early, ...), custom_call_target="tpu_custom_call" | custom-call | flops 234881024 | bytes 2000000 | tf_op jit(solution)/shard_map/pallas_call | solution.py:248
  73.1 0.0 all-to-all-done.1.parts
  73.1 7.2 %all-to-all-start = ((s16[8,32,1792]{2,1,0:T(8,128)(2,1)}), s16[8,32,1792]{2,1,0:T(8,128)(2,1)S(1)}, u32[]{:S(2)}, u32[]{:S(2)}) async-start(s16[8,32,1792]{2,1,0:T(8,128)(2,1)} %get-tuple-element.27), calls=%async_computation | async-start | bytes 1835008 | tf_op jit(solution)/shard_map/all_to_all | solution.py:376
  80.3 0.0 copy-start.1
  80.3 2.3 %shard_map.50 = (s16[64,896]{1,0:T(8,128)(2,1)}, s16[64,896]{1,0:T(8,128)(2,1)S(1)}, s16[64,896]{1,0:T(8,128)(2,1)S(1)}, s16[64,896]{1,0:T(8,128)(2,1)S(1)}, f32[64,128]{1,0:T(8,128)S(1)}) custom-call(bf16[256,128]{1,0:T(8,128)(2,1)S(1)} %get-tuple-element.20.inverse, f32[256,128]{1,0:T(8,128)S(1)} %get-tuple-element.21.first, ...), custom_call_target="tpu_custom_call" | custom-call | flops 469762048 | bytes 3000000 | tf_op jit(solution)/shard_map/pallas_call | solution.py:289
  82.6 4.5 %collective-permute-start.3 = (s16[64,896]{1,0:T(8,128)(2,1)S(1)}, s16[64,896]{1,0:T(8,128)(2,1)S(1)}, u32[]{:S(2)}, u32[]{:S(2)}) collective-permute-start(s16[64,896]{1,0:T(8,128)(2,1)S(1)} %get-tuple-element.30), channel_id=1, source_target_pairs={{0,16},{1,17},{2,18},{3,19},{4,20},{5,21},{6,22},{7,23},{8,24},{9,... | collective-permute-start | bytes 344072 | tf_op jit(solution)/shard_map/ppermute | solution.py:378
  87.2 4.9 %collective-permute-start.4 = (s16[64,896]{1,0:T(8,128)(2,1)S(1)}, s16[64,896]{1,0:T(8,128)(2,1)S(1)}, u32[]{:S(2)}, u32[]{:S(2)}) collective-permute-start(s16[64,896]{1,0:T(8,128)(2,1)S(1)} %get-tuple-element.31), channel_id=1, source_target_pairs={{0,8},{1,9},{2,10},{3,11},{4,12},{5,13},{6,14},{7,15},{8,16},{9,17... | collective-permute-start | bytes 344072 | tf_op jit(solution)/shard_map/ppermute | solution.py:378
  92.0 3.1 %collective-permute-start.5 = (s16[64,896]{1,0:T(8,128)(2,1)S(1)}, s16[64,896]{1,0:T(8,128)(2,1)S(1)}, u32[]{:S(2)}, u32[]{:S(2)}) collective-permute-start(s16[64,896]{1,0:T(8,128)(2,1)S(1)} %get-tuple-element.32), channel_id=1, source_target_pairs={{0,24},{1,25},{2,26},{3,27},{4,28},{5,29},{6,30},{7,31},{8,0},{9,1... | collective-permute-start | bytes 344072 | tf_op jit(solution)/shard_map/ppermute | solution.py:378
  95.1 0.1 collective-permute-done.3.s2
  95.3 1.9 %collective-permute-done.4.s1 = s16[64,896]{1,0:T(8,128)(2,1)S(1)} collective-permute-done((s16[64,896]{1,0:T(8,128)(2,1)S(1)}, s16[64,896]{1,0:T(8,128)(2,1)S(1)}, u32[]{:S(2)}, u32[]{:S(2)}) %collective-permute-start.4) | collective-permute-done | bytes 114720 | tf_op jit(solution)/shard_map/ppermute | solution.py:378
  97.2 3.4 %collective-permute-done.5.s3 = s16[64,896]{1,0:T(8,128)(2,1)S(1)} collective-permute-done((s16[64,896]{1,0:T(8,128)(2,1)S(1)}, s16[64,896]{1,0:T(8,128)(2,1)S(1)}, u32[]{:S(2)}, u32[]{:S(2)}) %collective-permute-start.5) | collective-permute-done | bytes 114720 | tf_op jit(solution)/shard_map/ppermute | solution.py:378
  100.6 1.6 %shard_map.51.rest = bf16[16,8,896]{2,1,0:T(8,128)(2,1)} custom-call(f32[64,128]{1,0:T(8,128)S(1)} %get-tuple-element.28.factor, s16[64,896]{1,0:T(8,128)(2,1)} %get-tuple-element.29.own, s16[64,896]{1,0:T(8,128)(2,1)S(1)} %collective-permute-done.3.s2, s16[64,896]{1,0:T(8,128)(2,1)S(1)} %collective-permute-done.4.s1, ...), custom_call_target="tpu_custom_call" | custom-call | flops 2000000 | bytes 700000 | tf_op jit(solution)/shard_map/pallas_call | solution.py:321
  102.2 0.0 all-to-all-done.sy
  102.2 1.0 shard_map.52
  103.2 4.8 %all-to-all-start.2 = ((bf16[16,8,896]{2,1,0:T(8,128)(2,1)}), bf16[16,8,896]{2,1,0:T(8,128)(2,1)S(1)}, u32[]{:S(2)}, u32[]{:S(2)}) async-start(bf16[16,8,896]{2,1,0:T(8,128)(2,1)} %shard_map.52), calls=%async_computation.2 | async-start | bytes 458752 | tf_op jit(solution)/shard_map/all_to_all | solution.py:381
  108.0 5.4 %all-to-all-done.2 = bf16[16,8,896]{2,1,0:T(8,128)(2,1)S(1)} async-done(((bf16[16,8,896]{2,1,0:T(8,128)(2,1)}), bf16[16,8,896]{2,1,0:T(8,128)(2,1)S(1)}, u32[]{:S(2)}, u32[]{:S(2)}) %all-to-all-start.2) | async-done | bytes 229408 | tf_op jit(solution)/shard_map/all_to_all | solution.py:381
  113.5 5.1 %collective-permute-start.6 = (s16[8,896]{1,0:T(8,128)(2,1)S(1)}, s16[8,896]{1,0:T(8,128)(2,1)S(1)}, u32[]{:S(2)}, u32[]{:S(2)}) collective-permute-start(s16[8,896]{1,0:T(8,128)(2,1)S(1)} %convert_element_type.10), channel_id=1, source_target_pairs={{0,0},{1,32},{2,64},{3,96},{4,128},{5,160},{6,192},{7,224},{8,8},{... | collective-permute-start | bytes 43016 | tf_op jit(solution)/shard_map/ppermute | solution.py:383
  118.6 0.0 copy-done.1
  118.7 0.1 add_multiply_fusion
  118.8 0.1 copy.6
  118.8 5.1 %collective-permute-done.6 = s16[8,896]{1,0:T(8,128)(2,1)S(1)} collective-permute-done((s16[8,896]{1,0:T(8,128)(2,1)S(1)}, s16[8,896]{1,0:T(8,128)(2,1)S(1)}, u32[]{:S(2)}, u32[]{:S(2)}) %collective-permute-start.6) | collective-permute-done | bytes 14368 | tf_op jit(solution)/shard_map/ppermute | solution.py:383
  123.9 0.7 bitcast_multiply_fusion
  (2 shorter events, 0.0 us)
Async XLA Ops:
  2.7 70.4 %all-to-all-start.1 = ((bf16[8,1168,128]{2,1,0:T(8,128)(2,1)}), bf16[8,1168,128]{2,1,0:T(8,128)(2,1)S(1)}, u32[]{:S(2)}, u32[]{:S(2)}) async-start(bf16[8,1168,128]{2,1,0:T(8,128)(2,1)} %shard_map.46.hz), calls=%async_computation.1 | async-start | bytes 4784128 | tf_op jit(solution)/shard_map/all_to_all | solution.py:371
  15.4 33.2 %copy-start = (s32[256,112]{0,1:T(8,128)S(1)}, s32[256,112]{0,1:T(8,128)}, u32[]{:S(2)}) copy-start(s32[256,112]{0,1:T(8,128)} %param.6) | copy-start | bytes 344068
  17.0 31.6 %collective-permute-start = (bf16[2064,128]{1,0:T(8,128)(2,1)S(1)}, bf16[2064,128]{1,0:T(8,128)(2,1)S(1)}, u32[]{:S(2)}, u32[]{:S(2)}) collective-permute-start(bf16[2064,128]{1,0:T(8,128)(2,1)S(1)} %get-tuple-element.19), channel_id=1, source_target_pairs={{0,16},{1,17},{2,18},{3,19},{4,20},{5,21},{6,22},{7,23},{8,24},{9,... | collective-permute-start | bytes 1585160 | tf_op jit(solution)/shard_map/ppermute | solution.py:373
  24.7 34.4 %collective-permute-start.1 = (bf16[2064,128]{1,0:T(8,128)(2,1)S(1)}, bf16[2064,128]{1,0:T(8,128)(2,1)S(1)}, u32[]{:S(2)}, u32[]{:S(2)}) collective-permute-start(bf16[2064,128]{1,0:T(8,128)(2,1)S(1)} %get-tuple-element.24), channel_id=1, source_target_pairs={{0,8},{1,9},{2,10},{3,11},{4,12},{5,13},{6,14},{7,15},{8,16},{9,17... | collective-permute-start | bytes 1585160 | tf_op jit(solution)/shard_map/ppermute | solution.py:373
  27.5 43.7 %collective-permute-start.2 = (bf16[2064,128]{1,0:T(8,128)(2,1)S(1)}, bf16[2064,128]{1,0:T(8,128)(2,1)S(1)}, u32[]{:S(2)}, u32[]{:S(2)}) collective-permute-start(bf16[2064,128]{1,0:T(8,128)(2,1)S(1)} %get-tuple-element.25), channel_id=1, source_target_pairs={{0,24},{1,25},{2,26},{3,27},{4,28},{5,29},{6,30},{7,31},{8,0},{9,1... | collective-permute-start | bytes 1585160 | tf_op jit(solution)/shard_map/ppermute | solution.py:373
  73.1 29.1 %all-to-all-start = ((s16[8,32,1792]{2,1,0:T(8,128)(2,1)}), s16[8,32,1792]{2,1,0:T(8,128)(2,1)S(1)}, u32[]{:S(2)}, u32[]{:S(2)}) async-start(s16[8,32,1792]{2,1,0:T(8,128)(2,1)} %get-tuple-element.27), calls=%async_computation | async-start | bytes 1835008 | tf_op jit(solution)/shard_map/all_to_all | solution.py:376
  80.3 38.3 %copy-start.1 = (s32[8,112]{1,0:T(8,128)S(1)}, s32[8,112]{1,0:T(8,128)}, u32[]{:S(2)}) copy-start(s32[8,112]{1,0:T(8,128)} %exps.1) | copy-start | bytes 10756
  82.6 12.6 %collective-permute-start.3 = (s16[64,896]{1,0:T(8,128)(2,1)S(1)}, s16[64,896]{1,0:T(8,128)(2,1)S(1)}, u32[]{:S(2)}, u32[]{:S(2)}) collective-permute-start(s16[64,896]{1,0:T(8,128)(2,1)S(1)} %get-tuple-element.30), channel_id=1, source_target_pairs={{0,16},{1,17},{2,18},{3,19},{4,20},{5,21},{6,22},{7,23},{8,24},{9,... | collective-permute-start | bytes 344072 | tf_op jit(solution)/shard_map/ppermute | solution.py:378
  87.2 10.0 %collective-permute-start.4 = (s16[64,896]{1,0:T(8,128)(2,1)S(1)}, s16[64,896]{1,0:T(8,128)(2,1)S(1)}, u32[]{:S(2)}, u32[]{:S(2)}) collective-permute-start(s16[64,896]{1,0:T(8,128)(2,1)S(1)} %get-tuple-element.31), channel_id=1, source_target_pairs={{0,8},{1,9},{2,10},{3,11},{4,12},{5,13},{6,14},{7,15},{8,16},{9,17... | collective-permute-start | bytes 344072 | tf_op jit(solution)/shard_map/ppermute | solution.py:378
  92.0 8.5 %collective-permute-start.5 = (s16[64,896]{1,0:T(8,128)(2,1)S(1)}, s16[64,896]{1,0:T(8,128)(2,1)S(1)}, u32[]{:S(2)}, u32[]{:S(2)}) collective-permute-start(s16[64,896]{1,0:T(8,128)(2,1)S(1)} %get-tuple-element.32), channel_id=1, source_target_pairs={{0,24},{1,25},{2,26},{3,27},{4,28},{5,29},{6,30},{7,31},{8,0},{9,1... | collective-permute-start | bytes 344072 | tf_op jit(solution)/shard_map/ppermute | solution.py:378
  103.2 10.2 %all-to-all-start.2 = ((bf16[16,8,896]{2,1,0:T(8,128)(2,1)}), bf16[16,8,896]{2,1,0:T(8,128)(2,1)S(1)}, u32[]{:S(2)}, u32[]{:S(2)}) async-start(bf16[16,8,896]{2,1,0:T(8,128)(2,1)} %shard_map.52), calls=%async_computation.2 | async-start | bytes 458752 | tf_op jit(solution)/shard_map/all_to_all | solution.py:381
  113.5 10.4 %collective-permute-start.6 = (s16[8,896]{1,0:T(8,128)(2,1)S(1)}, s16[8,896]{1,0:T(8,128)(2,1)S(1)}, u32[]{:S(2)}, u32[]{:S(2)}) collective-permute-start(s16[8,896]{1,0:T(8,128)(2,1)S(1)} %convert_element_type.10), channel_id=1, source_target_pairs={{0,0},{1,32},{2,64},{3,96},{4,128},{5,160},{6,192},{7,224},{8,8},{... | collective-permute-start | bytes 43016 | tf_op jit(solution)/shard_map/ppermute | solution.py:383

commit v8 on v7

--- a/solution.py
+++ b/solution.py
@@ -33,7 +33,7 @@
                 if group < 8:
                     target = z * NM + y * NZ + group
                 else:
-                    target = (8 + 2 * y + group % 2) * NM + ((group - 8) // 2) * NZ + z
+                    target = (8 + 2 * y + group % 2) * NM + (((group - 8) // 2 + 2) % NY) * NZ + z
                 moves.append((group * NM + y * NZ + z, target))
     return moves
 
@@ -299,9 +299,9 @@
     )(inverse, first, *in_vmem(parts))
 
 
-def second_z_kernel(factor, own, s2, s1, s3, out, own_here, codes_here, sems):
+def second_z_kernel(factor, own, s2, s1, s3, out, own_here, sem):
     _, z = place()
-    load = pltpu.make_async_copy(own, own_here, sems.at[0])
+    load = pltpu.make_async_copy(own, own_here, sem)
     load.start()
     scale = spread(factor[...].astype(jnp.bfloat16), z * (CZ // BLK), CZ)
     total = s2[...].astype(jnp.int32) + s1[...].astype(jnp.int32) + s3[...].astype(jnp.int32)
@@ -309,32 +309,26 @@
     total = total + own_here[...].astype(jnp.int32)
     codes = round_clip(total.astype(jnp.float32) * scale)
     for k in range(8):
-        codes_here[k] = codes[8 * k : 8 * k + 8].astype(jnp.bfloat16)
-    store = pltpu.make_async_copy(codes_here, out.at[0:8], sems.at[1])
-    store.start()
-    store.wait()
+        out[k] = codes[8 * k : 8 * k + 8].astype(jnp.bfloat16)
 
 
 def second_z(factor, own, *arrays):
-    any_spec = pl.BlockSpec(memory_space=pl.ANY)
     vmem_spec = pl.BlockSpec(memory_space=pltpu.VMEM)
     return pl.pallas_call(
         second_z_kernel,
-        out_shape=pltpu.HBM((NG, 8, CZ), jnp.bfloat16),
-        in_specs=[vmem_spec, any_spec] + [vmem_spec] * 3,
-        out_specs=any_spec,
-        scratch_shapes=[
-            pltpu.VMEM((64, CZ), jnp.int16),
-            pltpu.VMEM((8, 8, CZ), jnp.bfloat16),
-            pltpu.SemaphoreType.DMA((2,)),
-        ],
+        out_shape=jax.ShapeDtypeStruct((8, 8, CZ), jnp.bfloat16),
+        in_specs=[vmem_spec, pl.BlockSpec(memory_space=pl.ANY)] + [vmem_spec] * 3,
+        out_specs=vmem_spec,
+        scratch_shapes=[pltpu.VMEM((64, CZ), jnp.int16), pltpu.SemaphoreType.DMA],
         compiler_params=SMALL,
         cost_estimate=pl.CostEstimate(flops=2000000, bytes_accessed=700000, transcendentals=0),
     )(*in_vmem(factor), *in_hbm(own), *in_vmem(*arrays))
 
 
-def second_y_kernel(factor, sy, rest, out, codes_here, sem):
+def second_y_kernel(factor, sy, rest, out, codes_here, sems):
     y, _ = place()
+    first_half = pltpu.make_async_copy(rest, out.at[0:8], sems.at[0])
+    first_half.start()
     scale = spread(factor[...].astype(jnp.bfloat16), HALF // BLK + y * (CY // BLK), CY)
     total = sy[0].astype(jnp.int32)
     for r in range(1, NZ):
@@ -342,10 +336,11 @@
     codes = round_clip(total.astype(jnp.float32) * scale)
     for k in range(NY):
         for c in range(2):
-            codes_here[2 * k + c] = codes[8 * k : 8 * k + 8, c * CZ : c * CZ + CZ].astype(jnp.bfloat16)
-    store = pltpu.make_async_copy(codes_here, out.at[8:16], sem)
-    store.start()
-    store.wait()
+            codes_here[(2 * k + 4) % 8 + c] = codes[8 * k : 8 * k + 8, c * CZ : c * CZ + CZ].astype(jnp.bfloat16)
+    second_half = pltpu.make_async_copy(codes_here, out.at[8:16], sems.at[1])
+    second_half.start()
+    first_half.wait()
+    second_half.wait()
 
 
 def second_y(factor, sy, rest):
@@ -354,13 +349,12 @@
     return pl.pallas_call(
         second_y_kernel,
         out_shape=pltpu.HBM((NG, 8, CZ), jnp.bfloat16),
-        in_specs=[vmem_spec, vmem_spec, any_spec],
+        in_specs=[vmem_spec] * 3,
         out_specs=any_spec,
-        scratch_shapes=[pltpu.VMEM((8, 8, CZ), jnp.bfloat16), pltpu.SemaphoreType.DMA],
-        input_output_aliases={2: 0},
+        scratch_shapes=[pltpu.VMEM((8, 8, CZ), jnp.bfloat16), pltpu.SemaphoreType.DMA((2,))],
         compiler_params=SMALL,
         cost_estimate=pl.CostEstimate(flops=2000000, bytes_accessed=1200000, transcendentals=0),
-    )(*in_vmem(factor, sy), *in_hbm(rest))
+    )(*in_vmem(factor, sy, rest))
 
 
 def body(acts, cotangent, first_exp, second_exp):

time: 125 us -> 125 us (level); the launches traced: 125 us -> 123 us
  starting transfers between devices: 58.1 us -> 55.4 us
  waiting for transfers between devices: 52.4 us -> 54.2 us
    ppermute x1, starting transfers between devices: 5.14 us -> 2.47 us  [body(): lax.ppermute(total, ('inter', 'intra'), last_moves()).astype(jnp.float32)]
    ppermute x1, waiting for transfers between devices: 5.07 us -> 6.85 us  [body(): lax.ppermute(total, ('inter', 'intra'), last_moves()).astype(jnp.float32)]
  transfers between devices with their start and end apart: 10 -> 10, of which waited for: 8 -> 8; matrix products, arithmetic and copies ran while one was open for 0% -> 0% of each run, Pallas kernels for 8% -> 7%
where the time goes in v8:
time: 125 us; the launch traced here: 123 us
  starting transfers between devices  55.4 us (44%)
  waiting for transfers between devices  54.2 us (43%)
  Pallas kernels  12.4 us (10%)
    ppermute x3, waiting for transfers between devices, body(): lax.ppermute(p, 'intra', y_shift(step))  36.5 us
    ppermute x3, starting transfers between devices, body(): lax.ppermute(p, 'intra', y_shift(step))  15.7 us
    all_to_all x1, starting transfers between devices, body(): lax.all_to_all(hz, 'intra', 0, 0, axis_index_groups=Z_GROUPS, tiled=True)  12.7 us
    ppermute x3, starting transfers between devices, body(): lax.ppermute(s, 'intra', y_shift(step))  12.5 us
    all_to_all x1, starting transfers between devices, body(): lax.all_to_all(sy, 'intra', 0, 0, axis_index_groups=Z_GROUPS, tiled=True)  7.23 us
    ppermute x1, waiting for transfers between devices, body(): lax.ppermute(total, ('inter', 'intra'), last_moves()).astype(jnp.float32)  6.85 us
    ppermute x3, waiting for transfers between devices, body(): lax.ppermute(s, 'intra', y_shift(step))  5.44 us
    all_to_all x1, waiting for transfers between devices, body(): received = lax.all_to_all(codes, 'inter', 0, 0, tiled=True)  5.41 us
  transfers between devices with their start and end apart: 10, of which 8 were waited for; matrix products, arithmetic and copies ran while one was open for 0% of the time, Pallas kernels for 7%

profile of v8, /device:TPU:6, one launch (start us, length us, event | category | flops | bytes accessed | tf_op | source)
XLA Modules:
  0.0 123.1 jit_solution(12885895887317125175)
XLA Ops:
  0.0 2.7 %shard_map.46.hz = bf16[8,1168,128]{2,1,0:T(8,128)(2,1)} custom-call(bf16[128,256]{1,0:T(8,128)(2,1)} %acts.1, s32[8,112]{1,0:T(8,128)} %exps.1, bf16[128,14336]{1,0:T(8,128)(2,1)} %cot.5), custom_call_target="tpu_custom_call" | custom-call | bytes 4000000 | tf_op jit(solution)/shard_map/pallas_call | solution.py:96
  2.7 12.7 %all-to-all-start.1 = ((bf16[8,1168,128]{2,1,0:T(8,128)(2,1)}), bf16[8,1168,128]{2,1,0:T(8,128)(2,1)S(1)}, u32[]{:S(2)}, u32[]{:S(2)}) async-start(bf16[8,1168,128]{2,1,0:T(8,128)(2,1)} %shard_map.46.hz), calls=%async_computation.1 | async-start | bytes 4784128 | tf_op jit(solution)/shard_map/all_to_all | solution.py:365
  15.4 0.0 copy-start
  15.4 1.6 %shard_map.47 = (bf16[2064,128]{1,0:T(8,128)(2,1)S(1)}, bf16[2064,128]{1,0:T(8,128)(2,1)S(1)}, bf16[2064,128]{1,0:T(8,128)(2,1)S(1)}) custom-call(bf16[8,1168,128]{2,1,0:T(8,128)(2,1)} %shard_map.46.hz, bf16[128,14336]{1,0:T(8,128)(2,1)} %cot.5), custom_call_target="tpu_custom_call" | custom-call | bytes 3000000 | tf_op jit(solution)/shard_map/pallas_call | solution.py:142
  17.0 7.7 %collective-permute-start = (bf16[2064,128]{1,0:T(8,128)(2,1)S(1)}, bf16[2064,128]{1,0:T(8,128)(2,1)S(1)}, u32[]{:S(2)}, u32[]{:S(2)}) collective-permute-start(bf16[2064,128]{1,0:T(8,128)(2,1)S(1)} %get-tuple-element.19), channel_id=1, source_target_pairs={{0,16},{1,17},{2,18},{3,19},{4,20},{5,21},{6,22},{7,23},{8,24},{9,... | collective-permute-start | bytes 1585160 | tf_op jit(solution)/shard_map/ppermute | solution.py:367
  24.7 2.7 %collective-permute-start.1 = (bf16[2064,128]{1,0:T(8,128)(2,1)S(1)}, bf16[2064,128]{1,0:T(8,128)(2,1)S(1)}, u32[]{:S(2)}, u32[]{:S(2)}) collective-permute-start(bf16[2064,128]{1,0:T(8,128)(2,1)S(1)} %get-tuple-element.24), channel_id=1, source_target_pairs={{0,8},{1,9},{2,10},{3,11},{4,12},{5,13},{6,14},{7,15},{8,16},{9,17... | collective-permute-start | bytes 1585160 | tf_op jit(solution)/shard_map/ppermute | solution.py:367
  27.5 5.3 %collective-permute-start.2 = (bf16[2064,128]{1,0:T(8,128)(2,1)S(1)}, bf16[2064,128]{1,0:T(8,128)(2,1)S(1)}, u32[]{:S(2)}, u32[]{:S(2)}) collective-permute-start(bf16[2064,128]{1,0:T(8,128)(2,1)S(1)} %get-tuple-element.25), channel_id=1, source_target_pairs={{0,24},{1,25},{2,26},{3,27},{4,28},{5,29},{6,30},{7,31},{8,0},{9,1... | collective-permute-start | bytes 1585160 | tf_op jit(solution)/shard_map/ppermute | solution.py:367
  32.7 15.9 %collective-permute-done.q2 = bf16[2064,128]{1,0:T(8,128)(2,1)S(1)} collective-permute-done((bf16[2064,128]{1,0:T(8,128)(2,1)S(1)}, bf16[2064,128]{1,0:T(8,128)(2,1)S(1)}, u32[]{:S(2)}, u32[]{:S(2)}) %collective-permute-start) | collective-permute-done | bytes 528416 | tf_op jit(solution)/shard_map/ppermute | solution.py:367
  48.6 0.0 copy-done
  48.6 2.0 %shard_map.48 = (bf16[256,1792]{1,0:T(8,128)(2,1)S(1)}, bf16[256,128]{1,0:T(8,128)(2,1)S(1)}, f32[256,128]{1,0:T(8,128)S(1)}, f32[8,128]{1,0:T(8,128)S(1)}) custom-call(s32[112,256]{1,0:T(8,128)S(1)} %bitcast.3, bf16[8,1168,128]{2,1,0:T(8,128)(2,1)} %shard_map.46.hz, bf16[128,14336]{1,0:T(8,128)(2,1)} %cot.5, bf16[2064,128]{1,0:T(8,128)(2,1)S(1)} %collective-permute-done.q2), custom_call_target="tpu_custom_call" | custom-call | flops 234881024 | bytes 2000000 | tf_op jit(solution)/shard_map/pallas_call | solution.py:199
  50.6 8.5 %collective-permute-done.1.q1 = bf16[2064,128]{1,0:T(8,128)(2,1)S(1)} collective-permute-done((bf16[2064,128]{1,0:T(8,128)(2,1)S(1)}, bf16[2064,128]{1,0:T(8,128)(2,1)S(1)}, u32[]{:S(2)}, u32[]{:S(2)}) %collective-permute-start.1) | collective-permute-done | bytes 528416 | tf_op jit(solution)/shard_map/ppermute | solution.py:367
  59.1 12.0 %collective-permute-done.2.q3 = bf16[2064,128]{1,0:T(8,128)(2,1)S(1)} collective-permute-done((bf16[2064,128]{1,0:T(8,128)(2,1)S(1)}, bf16[2064,128]{1,0:T(8,128)(2,1)S(1)}, u32[]{:S(2)}, u32[]{:S(2)}) %collective-permute-start.2) | collective-permute-done | bytes 528416 | tf_op jit(solution)/shard_map/ppermute | solution.py:367
  71.2 1.9 %shard_map.49 = (s16[8,32,1792]{2,1,0:T(8,128)(2,1)}, f32[32,128]{1,0:T(8,128)S(1)}) custom-call(bf16[256,128]{1,0:T(8,128)(2,1)S(1)} %get-tuple-element.20.inverse, f32[256,128]{1,0:T(8,128)S(1)} %get-tuple-element.21.first, f32[8,128]{1,0:T(8,128)S(1)} %get-tuple-element.22.second, bf16[256,1792]{1,0:T(8,128)(2,1)S(1)} %get-tuple-element.23.early, ...), custom_call_target="tpu_custom_call" | custom-call | flops 234881024 | bytes 2000000 | tf_op jit(solution)/shard_map/pallas_call | solution.py:248
  73.1 0.0 all-to-all-done.1.parts
  73.1 7.2 %all-to-all-start = ((s16[8,32,1792]{2,1,0:T(8,128)(2,1)}), s16[8,32,1792]{2,1,0:T(8,128)(2,1)S(1)}, u32[]{:S(2)}, u32[]{:S(2)}) async-start(s16[8,32,1792]{2,1,0:T(8,128)(2,1)} %get-tuple-element.27), calls=%async_computation | async-start | bytes 1835008 | tf_op jit(solution)/shard_map/all_to_all | solution.py:370
  80.3 0.0 copy-start.1
  80.3 2.3 %shard_map.50 = (s16[64,896]{1,0:T(8,128)(2,1)}, s16[64,896]{1,0:T(8,128)(2,1)S(1)}, s16[64,896]{1,0:T(8,128)(2,1)S(1)}, s16[64,896]{1,0:T(8,128)(2,1)S(1)}, f32[64,128]{1,0:T(8,128)S(1)}) custom-call(bf16[256,128]{1,0:T(8,128)(2,1)S(1)} %get-tuple-element.20.inverse, f32[256,128]{1,0:T(8,128)S(1)} %get-tuple-element.21.first, ...), custom_call_target="tpu_custom_call" | custom-call | flops 469762048 | bytes 3000000 | tf_op jit(solution)/shard_map/pallas_call | solution.py:289
  82.6 4.5 %collective-permute-start.3 = (s16[64,896]{1,0:T(8,128)(2,1)S(1)}, s16[64,896]{1,0:T(8,128)(2,1)S(1)}, u32[]{:S(2)}, u32[]{:S(2)}) collective-permute-start(s16[64,896]{1,0:T(8,128)(2,1)S(1)} %get-tuple-element.30), channel_id=1, source_target_pairs={{0,16},{1,17},{2,18},{3,19},{4,20},{5,21},{6,22},{7,23},{8,24},{9,... | collective-permute-start | bytes 344072 | tf_op jit(solution)/shard_map/ppermute | solution.py:372
  87.2 4.9 %collective-permute-start.4 = (s16[64,896]{1,0:T(8,128)(2,1)S(1)}, s16[64,896]{1,0:T(8,128)(2,1)S(1)}, u32[]{:S(2)}, u32[]{:S(2)}) collective-permute-start(s16[64,896]{1,0:T(8,128)(2,1)S(1)} %get-tuple-element.31), channel_id=1, source_target_pairs={{0,8},{1,9},{2,10},{3,11},{4,12},{5,13},{6,14},{7,15},{8,16},{9,17... | collective-permute-start | bytes 344072 | tf_op jit(solution)/shard_map/ppermute | solution.py:372
  92.1 3.1 %collective-permute-start.5 = (s16[64,896]{1,0:T(8,128)(2,1)S(1)}, s16[64,896]{1,0:T(8,128)(2,1)S(1)}, u32[]{:S(2)}, u32[]{:S(2)}) collective-permute-start(s16[64,896]{1,0:T(8,128)(2,1)S(1)} %get-tuple-element.32), channel_id=1, source_target_pairs={{0,24},{1,25},{2,26},{3,27},{4,28},{5,29},{6,30},{7,31},{8,0},{9,1... | collective-permute-start | bytes 344072 | tf_op jit(solution)/shard_map/ppermute | solution.py:372
  95.1 0.1 collective-permute-done.3.s2
  95.3 1.9 %collective-permute-done.4.s1 = s16[64,896]{1,0:T(8,128)(2,1)S(1)} collective-permute-done((s16[64,896]{1,0:T(8,128)(2,1)S(1)}, s16[64,896]{1,0:T(8,128)(2,1)S(1)}, u32[]{:S(2)}, u32[]{:S(2)}) %collective-permute-start.4) | collective-permute-done | bytes 114720 | tf_op jit(solution)/shard_map/ppermute | solution.py:372
  97.2 3.4 %collective-permute-done.5.s3 = s16[64,896]{1,0:T(8,128)(2,1)S(1)} collective-permute-done((s16[64,896]{1,0:T(8,128)(2,1)S(1)}, s16[64,896]{1,0:T(8,128)(2,1)S(1)}, u32[]{:S(2)}, u32[]{:S(2)}) %collective-permute-start.5) | collective-permute-done | bytes 114720 | tf_op jit(solution)/shard_map/ppermute | solution.py:372
  100.6 1.0 shard_map.51.rest
  101.6 0.0 all-to-all-done.sy
  101.6 1.0 shard_map.52
  102.5 4.8 %all-to-all-start.2 = ((bf16[16,8,896]{2,1,0:T(8,128)(2,1)}), bf16[16,8,896]{2,1,0:T(8,128)(2,1)S(1)}, u32[]{:S(2)}, u32[]{:S(2)}) async-start(bf16[16,8,896]{2,1,0:T(8,128)(2,1)} %shard_map.52), calls=%async_computation.2 | async-start | bytes 458752 | tf_op jit(solution)/shard_map/all_to_all | solution.py:375
  107.4 5.4 %all-to-all-done.2 = bf16[16,8,896]{2,1,0:T(8,128)(2,1)S(1)} async-done(((bf16[16,8,896]{2,1,0:T(8,128)(2,1)}), bf16[16,8,896]{2,1,0:T(8,128)(2,1)S(1)}, u32[]{:S(2)}, u32[]{:S(2)}) %all-to-all-start.2) | async-done | bytes 229408 | tf_op jit(solution)/shard_map/all_to_all | solution.py:375
  112.8 2.5 %collective-permute-start.6 = (s16[8,896]{1,0:T(8,128)(2,1)S(1)}, s16[8,896]{1,0:T(8,128)(2,1)S(1)}, u32[]{:S(2)}, u32[]{:S(2)}) collective-permute-start(s16[8,896]{1,0:T(8,128)(2,1)S(1)} %convert_element_type.10), channel_id=1, source_target_pairs={{0,0},{1,32},{2,64},{3,96},{4,128},{5,160},{6,192},{7,224},{8,8},{... | collective-permute-start | bytes 43016 | tf_op jit(solution)/shard_map/ppermute | solution.py:377
  115.3 0.0 copy-done.1
  115.3 0.1 add_multiply_fusion
  115.4 0.1 copy.5
  115.5 6.8 %collective-permute-done.6 = s16[8,896]{1,0:T(8,128)(2,1)S(1)} collective-permute-done((s16[8,896]{1,0:T(8,128)(2,1)S(1)}, s16[8,896]{1,0:T(8,128)(2,1)S(1)}, u32[]{:S(2)}, u32[]{:S(2)}) %collective-permute-start.6) | collective-permute-done | bytes 14368 | tf_op jit(solution)/shard_map/ppermute | solution.py:377
  122.4 0.7 bitcast_multiply_fusion
  (2 shorter events, 0.0 us)
Async XLA Ops:
  2.7 70.4 %all-to-all-start.1 = ((bf16[8,1168,128]{2,1,0:T(8,128)(2,1)}), bf16[8,1168,128]{2,1,0:T(8,128)(2,1)S(1)}, u32[]{:S(2)}, u32[]{:S(2)}) async-start(bf16[8,1168,128]{2,1,0:T(8,128)(2,1)} %shard_map.46.hz), calls=%async_computation.1 | async-start | bytes 4784128 | tf_op jit(solution)/shard_map/all_to_all | solution.py:365
  15.4 33.2 %copy-start = (s32[256,112]{0,1:T(8,128)S(1)}, s32[256,112]{0,1:T(8,128)}, u32[]{:S(2)}) copy-start(s32[256,112]{0,1:T(8,128)} %param.6) | copy-start | bytes 344068
  17.0 31.6 %collective-permute-start = (bf16[2064,128]{1,0:T(8,128)(2,1)S(1)}, bf16[2064,128]{1,0:T(8,128)(2,1)S(1)}, u32[]{:S(2)}, u32[]{:S(2)}) collective-permute-start(bf16[2064,128]{1,0:T(8,128)(2,1)S(1)} %get-tuple-element.19), channel_id=1, source_target_pairs={{0,16},{1,17},{2,18},{3,19},{4,20},{5,21},{6,22},{7,23},{8,24},{9,... | collective-permute-start | bytes 1585160 | tf_op jit(solution)/shard_map/ppermute | solution.py:367
  24.7 34.4 %collective-permute-start.1 = (bf16[2064,128]{1,0:T(8,128)(2,1)S(1)}, bf16[2064,128]{1,0:T(8,128)(2,1)S(1)}, u32[]{:S(2)}, u32[]{:S(2)}) collective-permute-start(bf16[2064,128]{1,0:T(8,128)(2,1)S(1)} %get-tuple-element.24), channel_id=1, source_target_pairs={{0,8},{1,9},{2,10},{3,11},{4,12},{5,13},{6,14},{7,15},{8,16},{9,17... | collective-permute-start | bytes 1585160 | tf_op jit(solution)/shard_map/ppermute | solution.py:367
  27.5 43.7 %collective-permute-start.2 = (bf16[2064,128]{1,0:T(8,128)(2,1)S(1)}, bf16[2064,128]{1,0:T(8,128)(2,1)S(1)}, u32[]{:S(2)}, u32[]{:S(2)}) collective-permute-start(bf16[2064,128]{1,0:T(8,128)(2,1)S(1)} %get-tuple-element.25), channel_id=1, source_target_pairs={{0,24},{1,25},{2,26},{3,27},{4,28},{5,29},{6,30},{7,31},{8,0},{9,1... | collective-permute-start | bytes 1585160 | tf_op jit(solution)/shard_map/ppermute | solution.py:367
  73.1 28.5 %all-to-all-start = ((s16[8,32,1792]{2,1,0:T(8,128)(2,1)}), s16[8,32,1792]{2,1,0:T(8,128)(2,1)S(1)}, u32[]{:S(2)}, u32[]{:S(2)}) async-start(s16[8,32,1792]{2,1,0:T(8,128)(2,1)} %get-tuple-element.27), calls=%async_computation | async-start | bytes 1835008 | tf_op jit(solution)/shard_map/all_to_all | solution.py:370
  80.3 35.0 %copy-start.1 = (s32[8,112]{1,0:T(8,128)S(1)}, s32[8,112]{1,0:T(8,128)}, u32[]{:S(2)}) copy-start(s32[8,112]{1,0:T(8,128)} %exps.1) | copy-start | bytes 10756
  82.6 12.6 %collective-permute-start.3 = (s16[64,896]{1,0:T(8,128)(2,1)S(1)}, s16[64,896]{1,0:T(8,128)(2,1)S(1)}, u32[]{:S(2)}, u32[]{:S(2)}) collective-permute-start(s16[64,896]{1,0:T(8,128)(2,1)S(1)} %get-tuple-element.30), channel_id=1, source_target_pairs={{0,16},{1,17},{2,18},{3,19},{4,20},{5,21},{6,22},{7,23},{8,24},{9,... | collective-permute-start | bytes 344072 | tf_op jit(solution)/shard_map/ppermute | solution.py:372
  87.2 10.0 %collective-permute-start.4 = (s16[64,896]{1,0:T(8,128)(2,1)S(1)}, s16[64,896]{1,0:T(8,128)(2,1)S(1)}, u32[]{:S(2)}, u32[]{:S(2)}) collective-permute-start(s16[64,896]{1,0:T(8,128)(2,1)S(1)} %get-tuple-element.31), channel_id=1, source_target_pairs={{0,8},{1,9},{2,10},{3,11},{4,12},{5,13},{6,14},{7,15},{8,16},{9,17... | collective-permute-start | bytes 344072 | tf_op jit(solution)/shard_map/ppermute | solution.py:372
  92.1 8.5 %collective-permute-start.5 = (s16[64,896]{1,0:T(8,128)(2,1)S(1)}, s16[64,896]{1,0:T(8,128)(2,1)S(1)}, u32[]{:S(2)}, u32[]{:S(2)}) collective-permute-start(s16[64,896]{1,0:T(8,128)(2,1)S(1)} %get-tuple-element.32), channel_id=1, source_target_pairs={{0,24},{1,25},{2,26},{3,27},{4,28},{5,29},{6,30},{7,31},{8,0},{9,1... | collective-permute-start | bytes 344072 | tf_op jit(solution)/shard_map/ppermute | solution.py:372
  102.5 10.2 %all-to-all-start.2 = ((bf16[16,8,896]{2,1,0:T(8,128)(2,1)}), bf16[16,8,896]{2,1,0:T(8,128)(2,1)S(1)}, u32[]{:S(2)}, u32[]{:S(2)}) async-start(bf16[16,8,896]{2,1,0:T(8,128)(2,1)} %shard_map.52), calls=%async_computation.2 | async-start | bytes 458752 | tf_op jit(solution)/shard_map/all_to_all | solution.py:375
  112.8 9.5 %collective-permute-start.6 = (s16[8,896]{1,0:T(8,128)(2,1)S(1)}, s16[8,896]{1,0:T(8,128)(2,1)S(1)}, u32[]{:S(2)}, u32[]{:S(2)}) collective-permute-start(s16[8,896]{1,0:T(8,128)(2,1)S(1)} %convert_element_type.10), channel_id=1, source_target_pairs={{0,0},{1,32},{2,64},{3,96},{4,128},{5,160},{6,192},{7,224},{8,8},{... | collective-permute-start | bytes 43016 | tf_op jit(solution)/shard_map/ppermute | solution.py:377

commit v9 on v8

--- a/solution.py
+++ b/solution.py
@@ -18,6 +18,7 @@
 SMALL = pltpu.CompilerParams(vmem_limit_bytes=8 * 1024 * 1024)
 FIRST_Z = 5
 Z_ORDER = [(FIRST_Z + i) % NZ for i in range(NZ)]
+Z_OWNER = [0, 1, 2, 7, 4, 5, 6, 3]
 Z_GROUPS = [[y * NZ + z for z in Z_ORDER] for y in range(NY)]
 
 
@@ -31,7 +32,7 @@
         for y in range(NY):
             for z in range(NZ):
                 if group < 8:
-                    target = z * NM + y * NZ + group
+                    target = Z_OWNER[z] * NM + y * NZ + (group + 4) % 8
                 else:
                     target = (8 + 2 * y + group % 2) * NM + (((group - 8) // 2 + 2) % NY) * NZ + z
                 moves.append((group * NM + y * NZ + z, target))
@@ -58,13 +59,18 @@
     return member // NZ, lax.rem(member, NZ)
 
 
+def owner_of(z):
+    return jnp.where((z == 3) | (z == 7), 10 - z, z)
+
+
 def round_clip(values):
     return (jnp.clip(values, -127.0, 127.0) + MAGIC) - MAGIC
 
 
 def pack_z_kernel(acts, exps, cot, out, wide, held, acts_here, exps_here, padded, into, outof):
     loads = [
-        pltpu.make_async_copy(cot.at[:, z * CZ : (z + 1) * CZ], wide.at[j], into.at[j]) for j, z in enumerate(Z_ORDER)
+        pltpu.make_async_copy(cot.at[:, c * CZ : (c + 1) * CZ], wide.at[j], into.at[j])
+        for j, c in enumerate(Z_OWNER[z] for z in Z_ORDER)
     ]
     stores = [pltpu.make_async_copy(held.at[j], out.at[j], outof.at[j]) for j in range(NZ)]
     small = [
@@ -263,7 +269,7 @@
 def sum_z_kernel(inverse, first, parts, own, s2, s1, s3, factor, total_ref, diff):
     y, z = place()
     for b in range(CZ // BLK):
-        scale = spread(inverse[...], z * (CZ // BLK) + b, BLK)
+        scale = spread(inverse[...], owner_of(z) * (CZ // BLK) + b, BLK)
         for h in range(2):
             total = jnp.zeros((BLK, BLK), jnp.float32)
             for r in range(NZ):
@@ -303,13 +309,13 @@
     _, z = place()
     load = pltpu.make_async_copy(own, own_here, sem)
     load.start()
-    scale = spread(factor[...].astype(jnp.bfloat16), z * (CZ // BLK), CZ)
+    scale = spread(factor[...].astype(jnp.bfloat16), owner_of(z) * (CZ // BLK), CZ)
     total = s2[...].astype(jnp.int32) + s1[...].astype(jnp.int32) + s3[...].astype(jnp.int32)
     load.wait()
     total = total + own_here[...].astype(jnp.int32)
     codes = round_clip(total.astype(jnp.float32) * scale)
     for k in range(8):
-        out[k] = codes[8 * k : 8 * k + 8].astype(jnp.bfloat16)
+        out[(k + 4) % 8] = codes[8 * k : 8 * k + 8].astype(jnp.bfloat16)
 
 
 def second_z(factor, own, *arrays):

time: 125 us -> 125 us (level)
  no operation moved by 1% of the time
where the time goes in v9:
time: 125 us; the launch traced here: 123 us
  starting transfers between devices  55.4 us (44%)
  waiting for transfers between devices  54.2 us (43%)
  Pallas kernels  12.4 us (10%)
    ppermute x3, waiting for transfers between devices, body(): lax.ppermute(p, 'intra', y_shift(step))  36.5 us
    ppermute x3, starting transfers between devices, body(): lax.ppermute(p, 'intra', y_shift(step))  15.7 us
    all_to_all x1, starting transfers between devices, body(): lax.all_to_all(hz, 'intra', 0, 0, axis_index_groups=Z_GROUPS, tiled=True)  12.7 us
    ppermute x3, starting transfers between devices, body(): lax.ppermute(s, 'intra', y_shift(step))  12.5 us
    all_to_all x1, starting transfers between devices, body(): lax.all_to_all(sy, 'intra', 0, 0, axis_index_groups=Z_GROUPS, tiled=True)  7.23 us
    ppermute x1, waiting for transfers between devices, body(): lax.ppermute(total, ('inter', 'intra'), last_moves()).astype(jnp.float32)  6.85 us
    ppermute x3, waiting for transfers between devices, body(): lax.ppermute(s, 'intra', y_shift(step))  5.43 us
    all_to_all x1, waiting for transfers between devices, body(): received = lax.all_to_all(codes, 'inter', 0, 0, tiled=True)  5.41 us
  transfers between devices with their start and end apart: 10, of which 8 were waited for; matrix products, arithmetic and copies ran while one was open for 0% of the time, Pallas kernels for 7%

profile of v9, /device:TPU:6, one launch (start us, length us, event | category | flops | bytes accessed | tf_op | source)
XLA Modules:
  0.0 123.1 jit_solution(9118645042913387030)
XLA Ops:
  0.0 2.7 %shard_map.46.hz = bf16[8,1168,128]{2,1,0:T(8,128)(2,1)} custom-call(bf16[128,256]{1,0:T(8,128)(2,1)} %acts.1, s32[8,112]{1,0:T(8,128)} %exps.1, bf16[128,14336]{1,0:T(8,128)(2,1)} %cot.5), custom_call_target="tpu_custom_call" | custom-call | bytes 4000000 | tf_op jit(solution)/shard_map/pallas_call | solution.py:102
  2.7 12.7 %all-to-all-start.1 = ((bf16[8,1168,128]{2,1,0:T(8,128)(2,1)}), bf16[8,1168,128]{2,1,0:T(8,128)(2,1)S(1)}, u32[]{:S(2)}, u32[]{:S(2)}) async-start(bf16[8,1168,128]{2,1,0:T(8,128)(2,1)} %shard_map.46.hz), calls=%async_computation.1 | async-start | bytes 4784128 | tf_op jit(solution)/shard_map/all_to_all | solution.py:371
  15.4 0.0 copy-start
  15.4 1.6 %shard_map.47 = (bf16[2064,128]{1,0:T(8,128)(2,1)S(1)}, bf16[2064,128]{1,0:T(8,128)(2,1)S(1)}, bf16[2064,128]{1,0:T(8,128)(2,1)S(1)}) custom-call(bf16[8,1168,128]{2,1,0:T(8,128)(2,1)} %shard_map.46.hz, bf16[128,14336]{1,0:T(8,128)(2,1)} %cot.5), custom_call_target="tpu_custom_call" | custom-call | bytes 3000000 | tf_op jit(solution)/shard_map/pallas_call | solution.py:148
  17.0 7.7 %collective-permute-start = (bf16[2064,128]{1,0:T(8,128)(2,1)S(1)}, bf16[2064,128]{1,0:T(8,128)(2,1)S(1)}, u32[]{:S(2)}, u32[]{:S(2)}) collective-permute-start(bf16[2064,128]{1,0:T(8,128)(2,1)S(1)} %get-tuple-element.19), channel_id=1, source_target_pairs={{0,16},{1,17},{2,18},{3,19},{4,20},{5,21},{6,22},{7,23},{8,24},{9,... | collective-permute-start | bytes 1585160 | tf_op jit(solution)/shard_map/ppermute | solution.py:373
  24.7 2.7 %collective-permute-start.1 = (bf16[2064,128]{1,0:T(8,128)(2,1)S(1)}, bf16[2064,128]{1,0:T(8,128)(2,1)S(1)}, u32[]{:S(2)}, u32[]{:S(2)}) collective-permute-start(bf16[2064,128]{1,0:T(8,128)(2,1)S(1)} %get-tuple-element.24), channel_id=1, source_target_pairs={{0,8},{1,9},{2,10},{3,11},{4,12},{5,13},{6,14},{7,15},{8,16},{9,17... | collective-permute-start | bytes 1585160 | tf_op jit(solution)/shard_map/ppermute | solution.py:373
  27.5 5.3 %collective-permute-start.2 = (bf16[2064,128]{1,0:T(8,128)(2,1)S(1)}, bf16[2064,128]{1,0:T(8,128)(2,1)S(1)}, u32[]{:S(2)}, u32[]{:S(2)}) collective-permute-start(bf16[2064,128]{1,0:T(8,128)(2,1)S(1)} %get-tuple-element.25), channel_id=1, source_target_pairs={{0,24},{1,25},{2,26},{3,27},{4,28},{5,29},{6,30},{7,31},{8,0},{9,1... | collective-permute-start | bytes 1585160 | tf_op jit(solution)/shard_map/ppermute | solution.py:373
  32.7 15.9 %collective-permute-done.q2 = bf16[2064,128]{1,0:T(8,128)(2,1)S(1)} collective-permute-done((bf16[2064,128]{1,0:T(8,128)(2,1)S(1)}, bf16[2064,128]{1,0:T(8,128)(2,1)S(1)}, u32[]{:S(2)}, u32[]{:S(2)}) %collective-permute-start) | collective-permute-done | bytes 528416 | tf_op jit(solution)/shard_map/ppermute | solution.py:373
  48.6 0.0 copy-done
  48.6 2.0 %shard_map.48 = (bf16[256,1792]{1,0:T(8,128)(2,1)S(1)}, bf16[256,128]{1,0:T(8,128)(2,1)S(1)}, f32[256,128]{1,0:T(8,128)S(1)}, f32[8,128]{1,0:T(8,128)S(1)}) custom-call(s32[112,256]{1,0:T(8,128)S(1)} %bitcast.3, bf16[8,1168,128]{2,1,0:T(8,128)(2,1)} %shard_map.46.hz, bf16[128,14336]{1,0:T(8,128)(2,1)} %cot.5, bf16[2064,128]{1,0:T(8,128)(2,1)S(1)} %collective-permute-done.q2), custom_call_target="tpu_custom_call" | custom-call | flops 234881024 | bytes 2000000 | tf_op jit(solution)/shard_map/pallas_call | solution.py:205
  50.6 8.5 %collective-permute-done.1.q1 = bf16[2064,128]{1,0:T(8,128)(2,1)S(1)} collective-permute-done((bf16[2064,128]{1,0:T(8,128)(2,1)S(1)}, bf16[2064,128]{1,0:T(8,128)(2,1)S(1)}, u32[]{:S(2)}, u32[]{:S(2)}) %collective-permute-start.1) | collective-permute-done | bytes 528416 | tf_op jit(solution)/shard_map/ppermute | solution.py:373
  59.1 12.0 %collective-permute-done.2.q3 = bf16[2064,128]{1,0:T(8,128)(2,1)S(1)} collective-permute-done((bf16[2064,128]{1,0:T(8,128)(2,1)S(1)}, bf16[2064,128]{1,0:T(8,128)(2,1)S(1)}, u32[]{:S(2)}, u32[]{:S(2)}) %collective-permute-start.2) | collective-permute-done | bytes 528416 | tf_op jit(solution)/shard_map/ppermute | solution.py:373
  71.2 1.9 %shard_map.49 = (s16[8,32,1792]{2,1,0:T(8,128)(2,1)}, f32[32,128]{1,0:T(8,128)S(1)}) custom-call(bf16[256,128]{1,0:T(8,128)(2,1)S(1)} %get-tuple-element.20.inverse, f32[256,128]{1,0:T(8,128)S(1)} %get-tuple-element.21.first, f32[8,128]{1,0:T(8,128)S(1)} %get-tuple-element.22.second, bf16[256,1792]{1,0:T(8,128)(2,1)S(1)} %get-tuple-element.23.early, ...), custom_call_target="tpu_custom_call" | custom-call | flops 234881024 | bytes 2000000 | tf_op jit(solution)/shard_map/pallas_call | solution.py:254
  73.1 0.0 all-to-all-done.1.parts
  73.1 7.2 %all-to-all-start = ((s16[8,32,1792]{2,1,0:T(8,128)(2,1)}), s16[8,32,1792]{2,1,0:T(8,128)(2,1)S(1)}, u32[]{:S(2)}, u32[]{:S(2)}) async-start(s16[8,32,1792]{2,1,0:T(8,128)(2,1)} %get-tuple-element.27), calls=%async_computation | async-start | bytes 1835008 | tf_op jit(solution)/shard_map/all_to_all | solution.py:376
  80.3 0.0 copy-start.1
  80.3 2.3 %shard_map.50 = (s16[64,896]{1,0:T(8,128)(2,1)}, s16[64,896]{1,0:T(8,128)(2,1)S(1)}, s16[64,896]{1,0:T(8,128)(2,1)S(1)}, s16[64,896]{1,0:T(8,128)(2,1)S(1)}, f32[64,128]{1,0:T(8,128)S(1)}) custom-call(bf16[256,128]{1,0:T(8,128)(2,1)S(1)} %get-tuple-element.20.inverse, f32[256,128]{1,0:T(8,128)S(1)} %get-tuple-element.21.first, ...), custom_call_target="tpu_custom_call" | custom-call | flops 469762048 | bytes 3000000 | tf_op jit(solution)/shard_map/pallas_call | solution.py:295
  82.7 4.5 %collective-permute-start.3 = (s16[64,896]{1,0:T(8,128)(2,1)S(1)}, s16[64,896]{1,0:T(8,128)(2,1)S(1)}, u32[]{:S(2)}, u32[]{:S(2)}) collective-permute-start(s16[64,896]{1,0:T(8,128)(2,1)S(1)} %get-tuple-element.30), channel_id=1, source_target_pairs={{0,16},{1,17},{2,18},{3,19},{4,20},{5,21},{6,22},{7,23},{8,24},{9,... | collective-permute-start | bytes 344072 | tf_op jit(solution)/shard_map/ppermute | solution.py:378
  87.2 4.9 %collective-permute-start.4 = (s16[64,896]{1,0:T(8,128)(2,1)S(1)}, s16[64,896]{1,0:T(8,128)(2,1)S(1)}, u32[]{:S(2)}, u32[]{:S(2)}) collective-permute-start(s16[64,896]{1,0:T(8,128)(2,1)S(1)} %get-tuple-element.31), channel_id=1, source_target_pairs={{0,8},{1,9},{2,10},{3,11},{4,12},{5,13},{6,14},{7,15},{8,16},{9,17... | collective-permute-start | bytes 344072 | tf_op jit(solution)/shard_map/ppermute | solution.py:378
  92.1 3.1 %collective-permute-start.5 = (s16[64,896]{1,0:T(8,128)(2,1)S(1)}, s16[64,896]{1,0:T(8,128)(2,1)S(1)}, u32[]{:S(2)}, u32[]{:S(2)}) collective-permute-start(s16[64,896]{1,0:T(8,128)(2,1)S(1)} %get-tuple-element.32), channel_id=1, source_target_pairs={{0,24},{1,25},{2,26},{3,27},{4,28},{5,29},{6,30},{7,31},{8,0},{9,1... | collective-permute-start | bytes 344072 | tf_op jit(solution)/shard_map/ppermute | solution.py:378
  95.2 0.1 collective-permute-done.3.s2
  95.3 1.9 %collective-permute-done.4.s1 = s16[64,896]{1,0:T(8,128)(2,1)S(1)} collective-permute-done((s16[64,896]{1,0:T(8,128)(2,1)S(1)}, s16[64,896]{1,0:T(8,128)(2,1)S(1)}, u32[]{:S(2)}, u32[]{:S(2)}) %collective-permute-start.4) | collective-permute-done | bytes 114720 | tf_op jit(solution)/shard_map/ppermute | solution.py:378
  97.2 3.4 %collective-permute-done.5.s3 = s16[64,896]{1,0:T(8,128)(2,1)S(1)} collective-permute-done((s16[64,896]{1,0:T(8,128)(2,1)S(1)}, s16[64,896]{1,0:T(8,128)(2,1)S(1)}, u32[]{:S(2)}, u32[]{:S(2)}) %collective-permute-start.5) | collective-permute-done | bytes 114720 | tf_op jit(solution)/shard_map/ppermute | solution.py:378
  100.6 1.0 shard_map.51.rest
  101.6 0.0 all-to-all-done.sy
  101.6 1.0 shard_map.52
  102.6 4.8 %all-to-all-start.2 = ((bf16[16,8,896]{2,1,0:T(8,128)(2,1)}), bf16[16,8,896]{2,1,0:T(8,128)(2,1)S(1)}, u32[]{:S(2)}, u32[]{:S(2)}) async-start(bf16[16,8,896]{2,1,0:T(8,128)(2,1)} %shard_map.52), calls=%async_computation.2 | async-start | bytes 458752 | tf_op jit(solution)/shard_map/all_to_all | solution.py:381
  107.4 5.4 %all-to-all-done.2 = bf16[16,8,896]{2,1,0:T(8,128)(2,1)S(1)} async-done(((bf16[16,8,896]{2,1,0:T(8,128)(2,1)}), bf16[16,8,896]{2,1,0:T(8,128)(2,1)S(1)}, u32[]{:S(2)}, u32[]{:S(2)}) %all-to-all-start.2) | async-done | bytes 229408 | tf_op jit(solution)/shard_map/all_to_all | solution.py:381
  112.9 2.5 %collective-permute-start.6 = (s16[8,896]{1,0:T(8,128)(2,1)S(1)}, s16[8,896]{1,0:T(8,128)(2,1)S(1)}, u32[]{:S(2)}, u32[]{:S(2)}) collective-permute-start(s16[8,896]{1,0:T(8,128)(2,1)S(1)} %convert_element_type.10), channel_id=1, source_target_pairs={{0,4},{1,36},{2,68},{3,228},{4,132},{5,164},{6,196},{7,100},{8,12}... | collective-permute-start | bytes 43016 | tf_op jit(solution)/shard_map/ppermute | solution.py:383
  115.4 0.0 copy-done.1
  115.4 0.1 add_multiply_fusion
  115.5 0.1 copy.5
  115.5 6.8 %collective-permute-done.6 = s16[8,896]{1,0:T(8,128)(2,1)S(1)} collective-permute-done((s16[8,896]{1,0:T(8,128)(2,1)S(1)}, s16[8,896]{1,0:T(8,128)(2,1)S(1)}, u32[]{:S(2)}, u32[]{:S(2)}) %collective-permute-start.6) | collective-permute-done | bytes 14368 | tf_op jit(solution)/shard_map/ppermute | solution.py:383
  122.4 0.7 bitcast_multiply_fusion
  (2 shorter events, 0.0 us)
Async XLA Ops:
  2.7 70.4 %all-to-all-start.1 = ((bf16[8,1168,128]{2,1,0:T(8,128)(2,1)}), bf16[8,1168,128]{2,1,0:T(8,128)(2,1)S(1)}, u32[]{:S(2)}, u32[]{:S(2)}) async-start(bf16[8,1168,128]{2,1,0:T(8,128)(2,1)} %shard_map.46.hz), calls=%async_computation.1 | async-start | bytes 4784128 | tf_op jit(solution)/shard_map/all_to_all | solution.py:371
  15.4 33.2 %copy-start = (s32[256,112]{0,1:T(8,128)S(1)}, s32[256,112]{0,1:T(8,128)}, u32[]{:S(2)}) copy-start(s32[256,112]{0,1:T(8,128)} %param.6) | copy-start | bytes 344068
  17.0 31.6 %collective-permute-start = (bf16[2064,128]{1,0:T(8,128)(2,1)S(1)}, bf16[2064,128]{1,0:T(8,128)(2,1)S(1)}, u32[]{:S(2)}, u32[]{:S(2)}) collective-permute-start(bf16[2064,128]{1,0:T(8,128)(2,1)S(1)} %get-tuple-element.19), channel_id=1, source_target_pairs={{0,16},{1,17},{2,18},{3,19},{4,20},{5,21},{6,22},{7,23},{8,24},{9,... | collective-permute-start | bytes 1585160 | tf_op jit(solution)/shard_map/ppermute | solution.py:373
  24.7 34.4 %collective-permute-start.1 = (bf16[2064,128]{1,0:T(8,128)(2,1)S(1)}, bf16[2064,128]{1,0:T(8,128)(2,1)S(1)}, u32[]{:S(2)}, u32[]{:S(2)}) collective-permute-start(bf16[2064,128]{1,0:T(8,128)(2,1)S(1)} %get-tuple-element.24), channel_id=1, source_target_pairs={{0,8},{1,9},{2,10},{3,11},{4,12},{5,13},{6,14},{7,15},{8,16},{9,17... | collective-permute-start | bytes 1585160 | tf_op jit(solution)/shard_map/ppermute | solution.py:373
  27.5 43.7 %collective-permute-start.2 = (bf16[2064,128]{1,0:T(8,128)(2,1)S(1)}, bf16[2064,128]{1,0:T(8,128)(2,1)S(1)}, u32[]{:S(2)}, u32[]{:S(2)}) collective-permute-start(bf16[2064,128]{1,0:T(8,128)(2,1)S(1)} %get-tuple-element.25), channel_id=1, source_target_pairs={{0,24},{1,25},{2,26},{3,27},{4,28},{5,29},{6,30},{7,31},{8,0},{9,1... | collective-permute-start | bytes 1585160 | tf_op jit(solution)/shard_map/ppermute | solution.py:373
  73.1 28.5 %all-to-all-start = ((s16[8,32,1792]{2,1,0:T(8,128)(2,1)}), s16[8,32,1792]{2,1,0:T(8,128)(2,1)S(1)}, u32[]{:S(2)}, u32[]{:S(2)}) async-start(s16[8,32,1792]{2,1,0:T(8,128)(2,1)} %get-tuple-element.27), calls=%async_computation | async-start | bytes 1835008 | tf_op jit(solution)/shard_map/all_to_all | solution.py:376
  80.3 35.0 %copy-start.1 = (s32[8,112]{1,0:T(8,128)S(1)}, s32[8,112]{1,0:T(8,128)}, u32[]{:S(2)}) copy-start(s32[8,112]{1,0:T(8,128)} %exps.1) | copy-start | bytes 10756
  82.7 12.6 %collective-permute-start.3 = (s16[64,896]{1,0:T(8,128)(2,1)S(1)}, s16[64,896]{1,0:T(8,128)(2,1)S(1)}, u32[]{:S(2)}, u32[]{:S(2)}) collective-permute-start(s16[64,896]{1,0:T(8,128)(2,1)S(1)} %get-tuple-element.30), channel_id=1, source_target_pairs={{0,16},{1,17},{2,18},{3,19},{4,20},{5,21},{6,22},{7,23},{8,24},{9,... | collective-permute-start | bytes 344072 | tf_op jit(solution)/shard_map/ppermute | solution.py:378
  87.2 10.0 %collective-permute-start.4 = (s16[64,896]{1,0:T(8,128)(2,1)S(1)}, s16[64,896]{1,0:T(8,128)(2,1)S(1)}, u32[]{:S(2)}, u32[]{:S(2)}) collective-permute-start(s16[64,896]{1,0:T(8,128)(2,1)S(1)} %get-tuple-element.31), channel_id=1, source_target_pairs={{0,8},{1,9},{2,10},{3,11},{4,12},{5,13},{6,14},{7,15},{8,16},{9,17... | collective-permute-start | bytes 344072 | tf_op jit(solution)/shard_map/ppermute | solution.py:378
  92.1 8.5 %collective-permute-start.5 = (s16[64,896]{1,0:T(8,128)(2,1)S(1)}, s16[64,896]{1,0:T(8,128)(2,1)S(1)}, u32[]{:S(2)}, u32[]{:S(2)}) collective-permute-start(s16[64,896]{1,0:T(8,128)(2,1)S(1)} %get-tuple-element.32), channel_id=1, source_target_pairs={{0,24},{1,25},{2,26},{3,27},{4,28},{5,29},{6,30},{7,31},{8,0},{9,1... | collective-permute-start | bytes 344072 | tf_op jit(solution)/shard_map/ppermute | solution.py:378
  102.6 10.3 %all-to-all-start.2 = ((bf16[16,8,896]{2,1,0:T(8,128)(2,1)}), bf16[16,8,896]{2,1,0:T(8,128)(2,1)S(1)}, u32[]{:S(2)}, u32[]{:S(2)}) async-start(bf16[16,8,896]{2,1,0:T(8,128)(2,1)} %shard_map.52), calls=%async_computation.2 | async-start | bytes 458752 | tf_op jit(solution)/shard_map/all_to_all | solution.py:381
  112.9 9.5 %collective-permute-start.6 = (s16[8,896]{1,0:T(8,128)(2,1)S(1)}, s16[8,896]{1,0:T(8,128)(2,1)S(1)}, u32[]{:S(2)}, u32[]{:S(2)}) collective-permute-start(s16[8,896]{1,0:T(8,128)(2,1)S(1)} %convert_element_type.10), channel_id=1, source_target_pairs={{0,4},{1,36},{2,68},{3,228},{4,132},{5,164},{6,196},{7,100},{8,12}... | collective-permute-start | bytes 43016 | tf_op jit(solution)/shard_map/ppermute | solution.py:383
